TPU v7x, 32 devices: a whole 2x2x4 slice. The times are simulated.
32 devices in a mesh: ax: 4 (over y, x), circ: 8 (over z, core).
Axes of the slice: x: 2, y: 2, z: 4, core: 2. Of those that a mesh axis runs over, the one named last changes fastest.
Arguments:
- displace: float32 [3, 512, 16384], P(None, 'ax', 'circ'), may hold values from -6 to 6
- load: float32 [3, 512, 16384], P(None, 'ax', 'circ'), may hold values from -6 to 6
- history: float32 [9, 512, 16384], P(None, 'ax', 'circ'), may hold values from -4 to 4
- stiffen: float32 [512, 16384], P('ax', 'circ'), may hold values from 0.2 to 4
- modulus: float32 [9, 9], replicated, may hold values from -2 to 2
- radial_slope: float32 [32, 32], replicated, may hold values from -1 to 1
- radial_basis: float32 [32, 32], replicated, may hold values from -1 to 1
- axial_eig: float32 [512], replicated, may hold values from 0.05 to 4
- cycle_eig: float32 [512], replicated, may hold values from 0.05 to 4
- radial_eig: float32 [32], replicated, may hold values from 0.05 to 4
Outputs:
- precond: float32 [3, 512, 16384], P(None, ('ax', 'circ'))
All inputs are finite; a program needn't handle non-finite values.
Results may differ from a plain program's by a relative error of at most 0.000092.
Values sent between devices are 32-bit elements; how exact they have to be, the bound alone decides.
No kernel may reach another device: no remote copies, remote signals or barrier semaphores. Data moves between devices by JAX's collectives and lax.ppermute only.
A program may use at most 128 MiB of HBM per device.

v0:
```python
import math

import jax
import jax.numpy as jnp
from jax import lax
from jax.sharding import PartitionSpec as P

NA = 512
NC = 512
R = 32


def with_halo(block, sides, width, periodic):
    for axis, dim in sides:
        count = lax.axis_size(axis)
        forward = [(i, i + 1) for i in range(count - 1)]
        if periodic:
            forward.append((count - 1, 0))
        backward = [(target, source) for source, target in forward]
        low = lax.ppermute(
            lax.slice_in_dim(block, block.shape[dim] - width, None, axis=dim), axis, forward
        )
        high = lax.ppermute(lax.slice_in_dim(block, 0, width, axis=dim), axis, backward)
        block = jnp.concatenate([low, block, high], axis=dim)
    return block


def cycle_table(count):
    col = jnp.arange(count, dtype=jnp.int32)[:, None]
    mode = jnp.arange(count, dtype=jnp.int32)[None, :]
    half = count // 2
    folded = jnp.where(mode <= half, mode, mode - half)
    shift = jnp.where(mode <= half, 0.0, 0.5 * math.pi).astype(jnp.float32)
    scale_ends = jnp.where(
        (mode == 0) | (mode == half), math.sqrt(1.0 / count), math.sqrt(2.0 / count)
    ).astype(jnp.float32)
    phase = (col * folded % count).astype(jnp.float32) * (2.0 * math.pi / count)
    return jnp.cos(phase - shift) * scale_ends


def axial_table(rows, count):
    first = (rows + 1)[:, None]
    mode = jnp.arange(count, dtype=jnp.int32)[None, :] + 1
    phase = (first * mode % (2 * (count + 1))).astype(jnp.float32) * (math.pi / (count + 1))
    return jnp.sin(phase) * math.sqrt(2.0 / (count + 1))


def extend(field):
    rows = with_halo(field, (("ax", 1),), 1, False)
    return with_halo(rows, (("circ", 2),), R, True)


def cycle_parts(ext):
    span = ext.shape[2] - 2 * R
    left = ext[:, :, :span]
    middle = ext[:, :, R : R + span]
    right = ext[:, :, 2 * R :]
    return ((left + 4.0 * middle + right) / 6.0, (right - left) * 0.5)


def row_smooth(field):
    return (field[:, :-2] + 4.0 * field[:, 1:-1] + field[:, 2:]) / 6.0


def row_slope(field):
    return (field[:, 2:] - field[:, :-2]) * 0.5


def radial_mix(field, matrix, form):
    count, rows, flat = field.shape
    cube = field.reshape(count, rows, flat // R, R)
    mixed = jnp.einsum(form, cube, matrix, precision=lax.Precision.HIGHEST)
    return mixed.reshape(count, rows, flat)


def into_cycles(field):
    return lax.all_to_all(field, "circ", split_axis=1, concat_axis=2, tiled=True)


def cycle_forward(field, table, basis):
    count, rows, flat = field.shape
    cube = field.reshape(count * rows, NC, R)
    cube = jnp.einsum("bcr,ck->bkr", cube, table, precision=lax.Precision.HIGHEST)
    cube = jnp.einsum("bkr,rm->bkm", cube, basis, precision=lax.Precision.HIGHEST)
    return cube.reshape(count, rows, flat)


def cycle_inverse(field, table, basis):
    count, rows, flat = field.shape
    cube = field.reshape(count * rows, NC, R)
    cube = jnp.einsum("bkm,rm->bkr", cube, basis, precision=lax.Precision.HIGHEST)
    cube = jnp.einsum("bkr,ck->bcr", cube, table, precision=lax.Precision.HIGHEST)
    return cube.reshape(count, rows, flat)


def axial_solve(lines, forward_table, inverse_table, weights):
    modes = jnp.einsum("pk,cps->cks", forward_table, lines, precision=lax.Precision.HIGHEST)
    return jnp.einsum(
        "ak,cks->cas", inverse_table, modes * weights[None], precision=lax.Precision.HIGHEST
    )


def body(
    displace,
    load,
    history,
    stiffen,
    modulus,
    radial_slope,
    radial_basis,
    axial_eig,
    cycle_eig,
    radial_eig,
):
    ext = extend(displace)
    cycle_v, cycle_d = cycle_parts(ext)
    smooth_v = row_smooth(cycle_v)
    radial_part = radial_mix(smooth_v, radial_slope, "iacq,rq->iacr")
    grads = jnp.concatenate([row_slope(cycle_v), row_smooth(cycle_d), radial_part], axis=0)
    mixed = jnp.einsum("mn,nac->mac", modulus, grads, precision=lax.Precision.HIGHEST)
    stress = (1.0 + stiffen)[None] * mixed + history
    ext_stress = extend(stress)
    first_v, unused_d = cycle_parts(ext_stress[0:3])
    unused_v, second_d = cycle_parts(ext_stress[3:6])
    third_v, unused_e = cycle_parts(ext_stress[6:9])
    third = radial_mix(row_smooth(third_v), radial_slope, "iacr,rq->iacq")
    pull = -row_slope(first_v) - row_smooth(second_d) + third
    resid = load - pull
    a_dev = displace.shape[1]
    flat_dev = displace.shape[2]
    n_ax = lax.axis_size("ax")
    n_circ = lax.axis_size("circ")
    piece = flat_dev // n_ax
    rows_cycle = a_dev // n_circ
    table_cycle = cycle_table(NC)
    spec = cycle_forward(into_cycles(resid), table_cycle, radial_basis)
    start = lax.axis_index("circ") * flat_dev + lax.axis_index("ax") * piece
    index_flat = start + jnp.arange(piece, dtype=jnp.int32)
    denom = (
        axial_eig[:, None]
        + jnp.take(cycle_eig, index_flat // R)[None, :]
        + jnp.take(radial_eig, index_flat % R)[None, :]
    )
    weights = 1.0 / denom
    natural_rows = jnp.arange(NA, dtype=jnp.int32)
    inverse_table = axial_table(natural_rows, NA)
    cube = spec.reshape(3, rows_cycle, n_circ, flat_dev)
    lines = lax.all_to_all(
        lax.all_to_all(cube, "ax", split_axis=3, concat_axis=1, tiled=True),
        "circ",
        split_axis=2,
        concat_axis=1,
        tiled=True,
    ).reshape(3, NA, piece)
    group = n_ax * rows_cycle
    outer = natural_rows // group
    inner = natural_rows % group
    source_rows = inner // rows_cycle * a_dev + outer * rows_cycle + inner % rows_cycle
    forward_table = axial_table(source_rows, NA)
    solved = axial_solve(lines, forward_table, inverse_table, weights)
    cycles_back = lax.all_to_all(
        lax.all_to_all(solved, "ax", split_axis=1, concat_axis=2, tiled=True),
        "circ",
        split_axis=1,
        concat_axis=2,
        tiled=True,
    )
    return cycle_inverse(cycles_back, table_cycle, radial_basis)


def solution(mesh):
    return jax.shard_map(
        body,
        mesh=mesh,
        in_specs=(
            P(None, "ax", "circ"),
            P(None, "ax", "circ"),
            P(None, "ax", "circ"),
            P("ax", "circ"),
            P(),
            P(),
            P(),
            P(),
            P(),
            P(),
        ),
        out_specs=P(None, ("ax", "circ"), None),
        check_vma=False,
    )
```

profile of v0, /device:TPU:0, one launch (start us, length us, event | category | flops | bytes accessed | tf_op | source)
XLA Modules:
  0.0 806.0 jit_solution(6997942050114468107)
XLA Ops:
  45.7 8.1 %fusion.27 = f32[3,128,2048]{2,0,1:T(4,128)} fusion(f32[3,130,2048]{2,0,1:T(4,128)} %get-tuple-element.11), kind=kLoop, calls=%fused_computation.49 | loop fusion | flops 3145728 | bytes 12582912 | tf_op jit(solution)/shard_map/div | solution.py:62
  53.8 41.2 %bitcast_add_fusion = f32[9,128,2048]{2,0,1:T(8,128)} fusion(f32[9,128,2048]{2,1,0:T(8,128)} %param.12, f32[128,2048]{1,0:T(8,128)S(1)} %copy-done.8, f32[3,128,2048]{2,0,1:T(4,128)} %copy.129, f32[3,128,2048]{2,0,1:T(4,128)} %fusion.27, f32[3,128,2048]{2,0,1:T(4,128)} %get-tuple-element.13, f32[9,9]{1,0:T(8,128)S(1)} %copy-done.13), kind=kOutput, calls=%fused_computation.7 | convolution fusion | flops 264241152 | bytes 29360452 | tf_op jit(solution)/shard_map/mn,nac->mac/dot_general | solution.py:120
  121.1 28.8 %fusion.9 = f32[3,130,2048]{2,0,1:T(4,128)S(1)} fusion(f32[9,130,32]{2,0,1:T(8,128)S(1)} %copy.134, f32[9,1,2048]{2,0,1:T(8,128)S(1)} %collective-permute-done.5, f32[9,128,2048]{2,0,1:T(8,128)} %bitcast_add_fusion, f32[9,1,2048]{2,0,1:T(8,128)S(1)} %collective-permute-done.4, f32[9,130,32]{2,0,1:T(8,128)S(1)} %copy.132), kind=kLoop, calls=%fused_computation.10 | loop fusion | flops 9584640 | bytes 13079040 | tf_op jit(solution)/shard_map/div | solution.py:58
  168.3 35.2 %fusion.13 = (f32[3,130,2048]{2,0,1:T(4,128)S(1)}, f32[3,130,2048]{2,0,1:T(4,128)S(1)}) fusion(f32[9,130,32]{2,0,1:T(8,128)S(1)} %copy-done.5, f32[9,1,2048]{2,0,1:T(8,128)S(1)} %collective-permute-done.5, f32[9,128,2048]{2,0,1:T(8,128)} %bitcast_add_fusion, f32[9,1,2048]{2,0,1:T(8,128)S(1)} %collective-permute-done.4, f32[9,130,32]{2,0,1:T(8,128)S(1)} %copy-done.7), kind=kLoop, calls=%fused_computation.23 | loop fusion | flops 15974400 | bytes 16273920 | tf_op jit(solution)/shard_map/div | solution.py:58
  203.6 9.6 %fusion.20 = f32[3,128,2048]{2,0,1:T(4,128)} fusion(f32[3,128,2048]{2,0,1:T(4,128)S(1)} %copy-done.3, f32[3,130,2048]{2,0,1:T(4,128)S(1)} %get-tuple-element.6, f32[3,130,2048]{2,0,1:T(4,128)S(1)} %get-tuple-element.5, f32[3,128,2048]{2,1,0:T(8,128)} %param.11), kind=kLoop, calls=%fused_computation.38 | loop fusion | flops 7864320 | bytes 25165824 | tf_op jit(solution)/shard_map/sub | solution.py:128
  217.9 94.0 %all-to-all-done = f32[3,128,2048]{2,0,1:T(4,128)} async-done(((f32[3,128,2048]{2,0,1:T(4,128)}), f32[3,128,2048]{2,0,1:T(4,128)}, u32[]{:S(2)}, u32[]{:S(2)}) %all-to-all-start) | async-done | bytes 3145760 | tf_op jit(solution)/shard_map/all_to_all | solution.py:77
  330.2 11.2 %fusion.81 = f32[512,1536]{0,1:S(1)} fusion(f32[512,1536]{0,1:T(8,128)S(1)} %bitcast.127, f32[512]{0:T(512)S(1)} %get-tuple-element.52, f32[512]{0:T(512)S(1)} %get-tuple-element.51, s32[512]{0:T(512)S(1)} %iota_select_fusion), kind=kOutput, calls=%fused_computation.111 | convolution fusion | flops 4836032512 | bytes 6297600
  341.4 22.4 %fusion.89 = f32[48,512,32]{2,1,0:T(8,128)} fusion(f32[48,512,32]{1,2,0:T(8,128)S(1)} %bitcast.126, f32[32,32]{1,0:T(8,128)S(1)} %copy-done.12), kind=kOutput, calls=%fused_computation.119 | convolution fusion | flops 301989888 | bytes 6295552 | tf_op jit(solution)/shard_map/bkr,rm->bkm/dot_general | solution.py:84
  363.8 9.3 %reshape_reshape.3 = f32[3,16,8,2048]{3,2,1,0:T(8,128)S(1)} reshape(f32[48,512,32]{2,1,0:T(8,128)} %fusion.89) | data formatting | bytes 6291456 | tf_op jit(solution)/shard_map/reshape;reshape | solution.py:147
  373.0 13.7 %copy.143 = f32[3,16,8,2048]{1,2,0,3:T(8,128)} copy(f32[3,16,8,2048]{3,2,1,0:T(8,128)S(1)} %reshape_reshape.3) | data formatting | bytes 6291456 | tf_op jit(solution)/shard_map/reshape;reshape | solution.py:147
  386.7 20.1 %reshape.476 = f32[4,1,196608]{2,1,0:T(1,128)S(1)} reshape(f32[2048,3,8,16]{3,2,1,0:T(8,128)} %bitcast.113) | data formatting | bytes 6291456
  406.8 42.6 %all_to_all.81 = f32[4,1,196608]{2,1,0:T(1,128)} all-to-all(f32[4,1,196608]{2,1,0:T(1,128)S(1)} %reshape.476), channel_id=1, replica_groups=mesh['ax'=4,'circ'=8] {'ax'}, dimensions={0} | all-to-all | bytes 6291456 | tf_op jit(solution)/shard_map/all_to_all | solution.py:149
  449.9 10.0 %reduce.50 = f32[4,196608]{1,0:T(4,128)S(1)} reduce(f32[4,1,196608]{2,1,0:T(1,128)} %all_to_all.81, f32[]{:T(128)} %broadcast.808), dimensions={1}, to_apply=%all_to_all.62.reduce_sub_computation | reduce | bytes 6291460 | tf_op jit(solution)/shard_map/all_to_all | solution.py:149
  459.9 17.0 %reshape.477 = f32[2048,3,8,16]{3,2,1,0:T(8,128)} reshape(f32[4,196608]{1,0:T(4,128)S(1)} %reduce.50) | data formatting | bytes 6291456
  476.9 15.5 %copy.166 = f32[3,16,8,4,512]{4,3,2,1,0:T(4,128)S(1)} copy(f32[3,16,8,4,512]{1,2,0,4,3:T(8,128)} %bitcast.114) | data formatting | bytes 6291456 | tf_op jit(solution)/shard_map/all_to_all | solution.py:149
  509.8 15.6 %select_select_fusion = f32[512]{0:T(512)S(1)} fusion(pred[512]{0:T(512)(128)(4,1)S(1)} %get-tuple-element.55, pred[512]{0:T(512)(128)(4,1)S(1)} %get-tuple-element.56, pred[512]{0:T(512)(128)(4,1)S(1)} %get-tuple-element.57, pred[512]{0:T(512)(128)(4,1)S(1)} %get-tuple-element.58, pred[512]{0:T(512)(128)(4,1)S(1)} %get-tuple-element.59, ...), kind=kLoop, calls=%fused_computation.195 | loop fusion | flops 22528 | bytes 17000 | tf_op jit(solution)/shard_map/jit(_take)/select_n | solution.py:142
  526.6 44.6 %all-to-all-done.2 = f32[3,64,8,512]{3,1,0,2:T(8,128)S(1)} async-done(((f32[3,64,8,512]{3,1,0,2:T(8,128)}), f32[3,64,8,512]{3,1,0,2:T(8,128)S(1)}, u32[]{:S(2)}, u32[]{:S(2)}) %all-to-all-start.2) | async-done | bytes 3145760 | tf_op jit(solution)/shard_map/all_to_all | solution.py:148
  571.5 9.3 %fusion.48 = f32[3,512,512]{2,1,0:T(8,128)S(1)} fusion(f32[3,512,512]{2,1,0:T(8,128)S(1)} %bitcast.124, s32[512]{0:T(512)S(1)} %get-tuple-element.54, s32[512]{0:T(512)S(1)} %get-tuple-element.53), kind=kOutput, calls=%fused_computation.79 | convolution fusion | flops 4834459648 | bytes 6295552 | tf_op jit(solution)/shard_map/pk,cps->cks/dot_general | solution.py:97
  580.8 9.4 %fusion.35 = f32[3,512,512]{1,2,0:T(8,128)S(1)} fusion(f32[3,512,512]{2,1,0:T(8,128)S(1)} %fusion.48, f32[512,512]{0,1:T(8,128)S(1)} %copy-done.9, s32[512]{0:T(512)S(1)} %get-tuple-element.54), kind=kOutput, calls=%fused_computation.59 | convolution fusion | flops 4835246080 | bytes 7342080 | tf_op jit(solution)/shard_map/ak,cks->cas/dot_general | solution.py:98
  593.8 51.7 %all_to_all.82 = f32[3,512,512]{2,0,1:T(4,128)S(1)} all-to-all(f32[3,512,512]{2,0,1:T(4,128)} %copy.149), channel_id=1, replica_groups=mesh['ax'=4,'circ'=8] {'ax'}, dimensions={1} | all-to-all | bytes 6291456 | tf_op jit(solution)/shard_map/all_to_all | solution.py:162
  654.1 98.0 %all_to_all.83 = f32[3,128,2048]{2,0,1:T(4,128)S(1)} all-to-all(f32[3,128,2048]{2,0,1:T(4,128)} %copy.152), channel_id=1, replica_groups=mesh['ax'=4,'circ'=8] {'circ'}, dimensions={1} | all-to-all | bytes 6291456 | tf_op jit(solution)/shard_map/all_to_all | solution.py:161
  762.6 16.4 %fusion.87 = f32[48,512,32]{1,2,0:T(8,128)S(1)} fusion(f32[48,512,32]{2,1,0:T(8,128)} %reshape.315, f32[32,32]{1,0:T(8,128)S(1)} %copy-done.12), kind=kOutput, calls=%fused_computation.117 | convolution fusion | flops 301989888 | bytes 6295552 | tf_op jit(solution)/shard_map/bkm,rm->bkr/dot_general | solution.py:91
  779.0 10.0 %fusion.32 = f32[48,512,32]{1,0,2:T(8,128)S(1)} fusion(f32[48,512,32]{1,2,0:T(8,128)S(1)} %fusion.87, f32[512]{0:T(512)S(1)} %get-tuple-element.52, f32[512]{0:T(512)S(1)} %get-tuple-element.51, s32[512]{0:T(512)S(1)} %iota_select_fusion), kind=kOutput, calls=%fused_computation.58 | convolution fusion | flops 4836032512 | bytes 6297600 | tf_op jit(solution)/shard_map/bkr,ck->bcr/dot_general | solution.py:92
  795.7 10.1 %reshape.316 = f32[3,16,16384]{2,1,0:T(8,128)} reshape(f32[48,512,32]{2,1,0:T(8,128)} %copy.157) | data formatting | bytes 6291456 | tf_op jit(solution)/shard_map/reshape | solution.py:93
  (109 shorter events, 161.7 us)
Async XLA Ops:
  0.0 36.0 %copy-start = (f32[32,32]{1,0:T(8,128)S(1)}, f32[32,32]{1,0:T(8,128)}, u32[]{:S(2)}) copy-start(f32[32,32]{1,0:T(8,128)} %param.15) | copy-start | bytes 12292
  1.1 6.4 collective-permute-start
  6.0 6.0 collective-permute-start.1
  7.5 8.7 %copy-start.10 = (f32[128,2048]{1,0:T(8,128)S(1)}, f32[128,2048]{1,0:T(8,128)}, u32[]{:S(2)}) copy-start(f32[128,2048]{1,0:T(8,128)} %param.13) | copy-start | bytes 3145732
  12.2 7.9 collective-permute-start.2
  12.2 7.9 collective-permute-start.3
  45.7 8.1 %copy-start.8 = (f32[128,2048]{1,0:T(8,128)S(1)}, f32[128,2048]{1,0:T(8,128)}, u32[]{:S(2)}) copy-start(f32[128,2048]{1,0:T(8,128)} %broadcast_add_fusion) | copy-start | bytes 3145732
  45.7 8.1 %copy-start.13 = (f32[9,9]{1,0:T(8,128)S(1)}, f32[9,9]{1,0:T(8,128)}, u32[]{:S(2)}) copy-start(f32[9,9]{1,0:T(8,128)} %param.14) | copy-start | bytes 976
  96.0 7.3 collective-permute-start.5
  97.3 7.5 collective-permute-start.4
  107.0 10.6 %collective-permute-start.7 = (f32[9,130,32]{1,2,0:T(8,128)S(1)}, f32[9,130,32]{1,2,0:T(8,128)S(1)}, u32[]{:S(2)}, u32[]{:S(2)}) collective-permute-start(f32[9,130,32]{1,2,0:T(8,128)S(1)} %copy.133), channel_id=1, source_target_pairs={{1,0},{2,1},{3,2},{4,3},{5,4},{6,5},{7,6},{0,7},{9,8},{10,9},{11,1... | collective-permute-start | bytes 449288 | tf_op jit(solution)/shard_map/ppermute | solution.py:23
  110.6 8.8 %collective-permute-start.6 = (f32[9,130,32]{1,2,0:T(8,128)S(1)}, f32[9,130,32]{1,2,0:T(8,128)}, u32[]{:S(2)}, u32[]{:S(2)}) collective-permute-start(f32[9,130,32]{1,2,0:T(8,128)S(1)} %copy.131), channel_id=1, source_target_pairs={{0,1},{1,2},{2,3},{3,4},{4,5},{5,6},{6,7},{7,0},{8,9},{9,10},{10,1... | collective-permute-start | bytes 449288 | tf_op jit(solution)/shard_map/ppermute | solution.py:20
  118.4 31.5 %copy-start.4 = (f32[9,130,32]{2,0,1:T(8,128)}, f32[9,130,32]{2,0,1:T(8,128)S(1)}, u32[]{:S(2)}) copy-start(f32[9,130,32]{2,0,1:T(8,128)S(1)} %copy.134) | copy-start | bytes 449284
  121.1 28.8 %copy-start.6 = (f32[9,130,32]{2,0,1:T(8,128)}, f32[9,130,32]{2,0,1:T(8,128)S(1)}, u32[]{:S(2)}) copy-start(f32[9,130,32]{2,0,1:T(8,128)S(1)} %copy.132) | copy-start | bytes 449284
  163.0 5.3 copy-start.5
  163.0 5.3 copy-start.7
  168.3 35.2 %copy-start.3 = (f32[3,128,2048]{2,0,1:T(4,128)S(1)}, f32[3,128,2048]{2,0,1:T(4,128)}, u32[]{:S(2)}) copy-start(f32[3,128,2048]{2,0,1:T(4,128)} %copy.137) | copy-start | bytes 9437188
  213.2 98.7 %all-to-all-start = ((f32[3,128,2048]{2,0,1:T(4,128)}), f32[3,128,2048]{2,0,1:T(4,128)}, u32[]{:S(2)}, u32[]{:S(2)}) async-start(f32[3,128,2048]{2,0,1:T(4,128)} %fusion.20), calls=%async_computation | async-start | bytes 8388608 | tf_op jit(solution)/shard_map/all_to_all | solution.py:77
  330.2 11.2 %copy-start.12 = (f32[32,32]{1,0:T(8,128)S(1)}, f32[32,32]{1,0:T(8,128)}, u32[]{:S(2)}) copy-start(f32[32,32]{1,0:T(8,128)} %param.16) | copy-start | bytes 12292
  495.9 8.0 copy-start.11
  495.9 29.4 %copy-start.14 = (f32[512]{0:T(512)S(1)}, f32[512]{0:T(512)}, u32[]{:S(2)}) copy-start(f32[512]{0:T(512)} %param.17) | copy-start | bytes 6148
  495.9 75.2 %all-to-all-start.2 = ((f32[3,64,8,512]{3,1,0,2:T(8,128)}), f32[3,64,8,512]{3,1,0,2:T(8,128)S(1)}, u32[]{:S(2)}, u32[]{:S(2)}) async-start(f32[3,64,8,512]{3,1,0,2:T(8,128)} %bitcast.123), calls=%async_computation.2 | async-start | bytes 6291456 | tf_op jit(solution)/shard_map/all_to_all | solution.py:148
  571.5 9.3 %copy-start.9 = (f32[512,512]{0,1:T(8,128)S(1)}, f32[512,512]{0,1:T(8,128)}, u32[]{:S(2)}) copy-start(f32[512,512]{0,1:T(8,128)} %add_divide_fusion) | copy-start | bytes 3145732
  789.0 16.8 %copy-start.1 = (f32[32,32]{1,0:T(8,128)S(1)}, f32[32,32]{1,0:T(8,128)}, u32[]{:S(2)}) copy-start(f32[32,32]{1,0:T(8,128)} %param.15) | copy-start | bytes 12292
  (1 other events, 3.8 us)
where the time goes:
time: 811 us; the launch traced here: 806 us
  blocking collectives  192 us (24%)
  local copies, waits for them, and re-layouts  170 us (21%)
  waiting for transfers between devices  152 us (19%)
  other arithmetic  134 us (17%)
  matrix products  129 us (16%)
  starting transfers between devices  28.2 us (3%)
    all_to_all x1, blocking collectives, body(): lax.all_to_all(lax.all_to_all(solved, 'ax', split_axis=1, concat_axis=2,...  98 us
    all_to_all x1, waiting for transfers between devices, into_cycles(): lax.all_to_all(field, 'circ', split_axis=1, concat_axis=2, tiled=True)  94 us
    div x2, other arithmetic, cycle_parts(): return ((left + 4.0 * middle + right) / 6.0, (right - left) * 0.5)  64 us
    all_to_all x1, blocking collectives, body(): lax.all_to_all(solved, 'ax', split_axis=1, concat_axis=2, tiled=True)  51.7 us
    all_to_all x1, waiting for transfers between devices, body(): lax.all_to_all(lax.all_to_all(cube, 'ax', split_axis=3, concat_axis=1, ti...  44.6 us
    all_to_all x1, blocking collectives, body(): lax.all_to_all(cube, 'ax', split_axis=3, concat_axis=1, tiled=True)  42.6 us
    unnamed x36, local copies, waits for them, and re-layouts  41.6 us
    dot_general x1, matrix products, body(): jnp.einsum('mn,nac->mac', modulus, grads, precision=lax.Precision.HIGHEST)  41.2 us
  transfers between devices with their start and end apart: 10, of which 8 were waited for; matrix products, arithmetic and copies ran while one was open for 4% of the time, Pallas kernels for 0%

commit v1 on v0

--- a/solution.py
+++ b/solution.py
@@ -1,8 +1,14 @@
 import math
+
+import functools
 
 import jax
 import jax.numpy as jnp
+import ml_dtypes
+import numpy as np
 from jax import lax
+from jax.experimental import pallas as pl
+from jax.experimental.pallas import tpu as pltpu
 from jax.sharding import PartitionSpec as P
 
 NA = 512
@@ -100,7 +106,7 @@
     )
 
 
-def body(
+def plain_body(
     displace,
     load,
     history,
@@ -168,9 +174,692 @@
     return cycle_inverse(cycles_back, table_cycle, radial_basis)
 
 
+BF = jnp.bfloat16
+F32 = jnp.float32
+VMEM = pl.BlockSpec(memory_space=pltpu.VMEM)
+SMEM = pl.BlockSpec(memory_space=pltpu.SMEM)
+ANY = pl.BlockSpec(memory_space=pl.ANY)
+HALO = 8
+LANES = 128
+
+
+def params():
+    return pltpu.CompilerParams(vmem_limit_bytes=48 * 1024 * 1024)
+
+
+def cost(flops, read):
+    return pl.CostEstimate(flops=int(flops), bytes_accessed=int(read), transcendentals=0)
+
+
+def split(x):
+    hi = x.astype(BF)
+    return hi, (x - hi.astype(F32)).astype(BF)
+
+
+def dot(a, b, transposed=False):
+    dims = (((1,), (1 if transposed else 0,)), ((), ()))
+    return lax.dot_general(a, b, dims, preferred_element_type=F32)
+
+
+def dot3(ah, al, bh, bl, transposed=False):
+    return dot(ah, bh, transposed) + (dot(ah, bl, transposed) + dot(al, bh, transposed))
+
+
+def exact(a, b, transposed=False):
+    dims = (((1,), (1 if transposed else 0,)), ((), ()))
+    return lax.dot_general(
+        a, b, dims, precision=lax.Precision.HIGHEST, preferred_element_type=F32
+    )
+
+
+def host_split(table):
+    hi = table.astype(np.float32).astype(ml_dtypes.bfloat16)
+    lo = (table - hi.astype(np.float64)).astype(np.float32).astype(ml_dtypes.bfloat16)
+    return jnp.asarray(hi), jnp.asarray(lo)
+
+
+def host_cycle(count):
+    col = np.arange(count)[None, :]
+    mode = np.arange(count)[:, None]
+    half = count // 2
+    folded = np.where(mode <= half, mode, mode - half)
+    phase = 2.0 * np.pi * ((col * folded) % count) / count
+    scale = np.where((mode == 0) | (mode == half), math.sqrt(1.0 / count), math.sqrt(2.0 / count))
+    return np.where(mode <= half, np.cos(phase), np.sin(phase)) * scale
+
+
+def host_axial(count):
+    first = np.arange(1, count + 1)
+    phase = np.pi * (np.outer(first, first) % (2 * (count + 1))) / (count + 1)
+    return np.sin(phase) * math.sqrt(2.0 / (count + 1))
+
+
+def host_weave(mp):
+    table = np.zeros((mp * LANES, mp * LANES), np.float32)
+    for m in range(mp):
+        for c in range(LANES):
+            table[m * LANES + c, c * mp + m] = 1.0
+    return jnp.asarray(table.astype(ml_dtypes.bfloat16))
+
+
+def iota(shape, dim):
+    return lax.broadcasted_iota(jnp.int32, shape, dim)
+
+
+def onehot(condition):
+    return jnp.where(condition, 1.0, 0.0).astype(F32)
+
+
+def write_split(hi_ref, lo_ref, value):
+    hi, lo = split(value)
+    hi_ref[...] = hi
+    lo_ref[...] = lo
+
+
+def front_tables_kernel(mp, me_ref, slope_ref, basis_ref, krh, krl, kbh, kbl, kwh, kwl):
+    me = me_ref[0]
+    slope = slope_ref[...]
+    basis = basis_ref[...]
+    side = LANES
+    row = iota((side, R), 0)
+    col = iota((side, R), 1)
+    pick = onehot(row % R == col)
+    mask = iota((side, side), 0) // R == iota((side, side), 1) // R
+    value = exact(exact(pick, slope, True), pick, True)
+    write_split(krh, krl, jnp.where(mask, value, 0.0))
+    side = 8 * R
+    row = iota((side, R), 0)
+    col = iota((side, R), 1)
+    pick = onehot(row % R == col)
+    block = mp * 8
+    peer = jnp.bitwise_xor(row // block, me)
+    mode = onehot(peer * mp + (row % block) // 8 == col)
+    mask = iota((side, side), 0) % 8 == iota((side, side), 1) // R
+    value = exact(exact(mode, basis, True), pick, True)
+    write_split(kbh, kbl, jnp.where(mask, value, 0.0))
+    both = exact(slope, basis)
+    value = exact(exact(mode, both, True), pick, True)
+    write_split(kwh, kwl, jnp.where(mask, -value, 0.0))
+
+
+def front_tables(me, slope, basis, mp):
+    one = jax.ShapeDtypeStruct((LANES, LANES), BF)
+    two = jax.ShapeDtypeStruct((8 * R, 8 * R), BF)
+    return pl.pallas_call(
+        functools.partial(front_tables_kernel, mp),
+        out_shape=(one, one, two, two, two, two),
+        in_specs=[SMEM, VMEM, VMEM],
+        out_specs=(VMEM,) * 6,
+        compiler_params=params(),
+        name="front_tables",
+    )(me, slope, basis)
+
+
+def back_tables_kernel(mp, me_ref, basis_ref, hi_ref, lo_ref):
+    me = me_ref[0]
+    rows, cols = hi_ref.shape
+    span = LANES // mp
+    row = iota((rows, R), 0)
+    col = iota((rows, R), 1)
+    peer = jnp.bitwise_xor(row // LANES, me)
+    mode = onehot(peer * mp + row % mp == col)
+    pick = onehot(iota((cols, R), 0) % R == iota((cols, R), 1))
+    value = exact(exact(mode, basis_ref[...], True), pick, True)
+    mask = (iota((rows, cols), 0) % LANES) // mp == iota((rows, cols), 1) // R
+    write_split(hi_ref, lo_ref, jnp.where(mask, value, 0.0))
+
+
+def back_tables(me, basis, mp, peers):
+    shape = jax.ShapeDtypeStruct((peers * LANES, LANES // mp * R), BF)
+    return pl.pallas_call(
+        functools.partial(back_tables_kernel, mp),
+        out_shape=(shape, shape),
+        in_specs=[SMEM, VMEM],
+        out_specs=(VMEM, VMEM),
+        compiler_params=params(),
+        name="back_tables",
+    )(me, basis)
+
+
+def pack_rows_kernel(d_top, d_bot, h_top, h_bot, s_top, s_bot, up_ref, down_ref):
+    for i in range(3):
+        up_ref[2 * i : 2 * i + 2, :] = d_top[i, 0:2, :]
+        down_ref[2 * i : 2 * i + 2, :] = d_bot[i, 6:8, :]
+    for n in range(9):
+        up_ref[6 + n : 7 + n, :] = h_top[n, 0:1, :]
+        down_ref[6 + n : 7 + n, :] = h_bot[n, 7:8, :]
+    up_ref[15:16, :] = 1.0 + s_top[0:1, :]
+    down_ref[15:16, :] = 1.0 + s_bot[7:8, :]
+
+
+def pack_rows(displace, history, stiffen):
+    rows, flat = stiffen.shape
+    last = rows // 8 - 1
+    shape = jax.ShapeDtypeStruct((16, flat), F32)
+    return pl.pallas_call(
+        pack_rows_kernel,
+        out_shape=(shape, shape),
+        grid=(1,),
+        in_specs=[
+            pl.BlockSpec((3, 8, flat), lambda g: (0, 0, 0)),
+            pl.BlockSpec((3, 8, flat), lambda g: (0, last, 0)),
+            pl.BlockSpec((9, 8, flat), lambda g: (0, 0, 0)),
+            pl.BlockSpec((9, 8, flat), lambda g: (0, last, 0)),
+            pl.BlockSpec((8, flat), lambda g: (0, 0)),
+            pl.BlockSpec((8, flat), lambda g: (last, 0)),
+        ],
+        out_specs=(pl.BlockSpec((16, flat), lambda g: (0, 0)),) * 2,
+        compiler_params=params(),
+        name="pack_rows",
+    )(displace, displace, history, history, stiffen, stiffen)
+
+
+def pack_cols_kernel(dl, dr, hl, hr, sl, sr, tl, tr, bl, br, left_ref, right_ref, tall):
+    rows = sl.shape[0]
+    lane = iota((rows + HALO, LANES), 1)
+
+    def column(field, top, bottom, first, count):
+        tall[0:rows, :] = field
+        tall[rows : rows + HALO, :] = jnp.zeros((HALO, LANES), F32)
+        tall[rows : rows + count, :] = bottom[first : first + count, :]
+        tall[rows + HALO - count : rows + HALO, :] = top[first : first + count, :]
+        return tall[...]
+
+    def place(value, source, target):
+        shift = (target - source) % LANES
+        return pltpu.roll(value, shift, 1) if shift else value
+
+    for out, d, h, s, top, bottom, wide, slim in (
+        (left_ref, dl, hl, sl, tl, bl, 0, 0),
+        (right_ref, dr, hr, sr, tr, br, LANES - 2 * R, LANES - R),
+    ):
+        pieces = [(64 * i, 64, wide, column(d[i], top, bottom, 2 * i, 2)) for i in range(3)]
+        pieces += [(192 + 32 * n, 32, slim, column(h[n], top, bottom, 6 + n, 1)) for n in range(9)]
+        pieces += [(480, 32, slim, column(1.0 + s[...], top, bottom, 15, 1))]
+        for tile in range(4):
+            value = None
+            for at, width, source, piece in pieces:
+                if at // LANES == tile:
+                    moved = place(piece, source, at % LANES)
+                    if value is None:
+                        value = moved
+                    else:
+                        value = jnp.where(lane >= at % LANES, moved, value)
+            out[:, tile * LANES : (tile + 1) * LANES] = value
+
+
+def pack_cols(displace, history, stiffen, top, bottom):
+    rows, flat = stiffen.shape
+    last = flat // LANES - 1
+    shape = jax.ShapeDtypeStruct((rows + HALO, 4 * LANES), F32)
+
+    def three(count, at):
+        return pl.BlockSpec((count, rows, LANES), lambda g: (0, 0, at))
+
+    def two(height, at):
+        return pl.BlockSpec((height, LANES), lambda g: (0, at))
+
+    return pl.pallas_call(
+        pack_cols_kernel,
+        out_shape=(shape, shape),
+        grid=(1,),
+        in_specs=[
+            three(3, 0),
+            three(3, last),
+            three(9, 0),
+            three(9, last),
+            two(rows, 0),
+            two(rows, last),
+            two(16, 0),
+            two(16, last),
+            two(16, 0),
+            two(16, last),
+        ],
+        out_specs=(pl.BlockSpec((rows + HALO, 4 * LANES), lambda g: (0, 0)),) * 2,
+        scratch_shapes=[pltpu.VMEM((rows + HALO, LANES), F32)],
+        compiler_params=params(),
+        name="pack_cols",
+    )(displace, displace, history, history, stiffen, stiffen, top, top, bottom, bottom)
+
+
+def stencil_kernel(
+    comp,
+    mp,
+    peers,
+    modulus,
+    displace,
+    load,
+    history,
+    stiffen,
+    top,
+    bottom,
+    left,
+    right,
+    krh,
+    krl,
+    kbh,
+    kbl,
+    kwh,
+    kwl,
+    *rest,
+):
+    outs = rest[:peers]
+    xd, hx, sx, ld, st, uh, ul, wh, wl, sems = rest[peers:]
+    rows, flat = stiffen.shape
+    tall = rows + HALO
+    tiles = flat // LANES
+    center = (slice(0, rows), slice(0, flat))
+    copies = [
+        pltpu.make_async_copy(displace.at[i], xd.at[(i,) + center], sems.at[i]) for i in range(3)
+    ]
+    copies += [
+        pltpu.make_async_copy(history.at[comp + 3 * k], hx.at[(k,) + center], sems.at[3 + k])
+        for k in range(3)
+    ]
+    copies += [pltpu.make_async_copy(stiffen, sx.at[center], sems.at[6])]
+    copies += [pltpu.make_async_copy(load.at[comp], ld, sems.at[7])]
+    for copy in copies:
+        copy.start()
+    lane = iota((tall, LANES), 1)
+
+    def tile_of(ref, at, target):
+        value = ref[:, at // LANES * LANES : (at // LANES + 1) * LANES]
+        shift = (target - at) % LANES
+        return pltpu.roll(value, shift, 1) if shift else value
+
+    halo_rows = slice(rows, tall)
+    zeros = jnp.zeros((HALO, flat), F32)
+    for i in range(3):
+        xd[i, halo_rows, 0:flat] = zeros
+        xd[i, rows : rows + 2, 0:flat] = bottom[2 * i : 2 * i + 2, :]
+        xd[i, tall - 2 : tall, 0:flat] = top[2 * i : 2 * i + 2, :]
+        xd[i, :, flat:] = jnp.where(
+            lane < 64, tile_of(right, 64 * i, 0), tile_of(left, 64 * i, 64)
+        )
+    for k in range(3):
+        n = comp + 3 * k
+        at = 192 + 32 * n
+        hx[k, halo_rows, 0:flat] = zeros
+        hx[k, rows : rows + 1, 0:flat] = bottom[6 + n : 7 + n, :]
+        hx[k, tall - 1 : tall, 0:flat] = top[6 + n : 7 + n, :]
+        hx[k, :, flat:] = jnp.where(lane < 64, tile_of(right, at, 0), tile_of(left, at, 96))
+    sx[halo_rows, 0:flat] = zeros
+    sx[rows : rows + 1, 0:flat] = bottom[15:16, :] - 1.0
+    sx[tall - 1 : tall, 0:flat] = top[15:16, :] - 1.0
+    sx[:, flat:] = jnp.where(lane < 64, tile_of(right, 480, 0), tile_of(left, 480, 96)) - 1.0
+    for copy in copies:
+        copy.wait()
+
+    def lanes(t):
+        return pl.ds(pl.multiple_of(t * LANES, LANES), LANES)
+
+    def beside(ref, k, t):
+        now = ref[k, :, lanes(t)]
+        before = ref[k, :, lanes(lax.rem(t + tiles, tiles + 1))]
+        after = ref[k, :, lanes(lax.rem(t + 1, tiles + 1))]
+        low = jnp.where(lane < R, pltpu.roll(before, R, 1), pltpu.roll(now, R, 1))
+        high = jnp.where(
+            lane >= LANES - R, pltpu.roll(after, LANES - R, 1), pltpu.roll(now, LANES - R, 1)
+        )
+        return low, now, high
+
+    def up(x):
+        return pltpu.roll(x, 1, 0)
+
+    def down(x):
+        return pltpu.roll(x, tall - 1, 0)
+
+    def stress_step(t, carry):
+        total = [None] * 3
+        for i in range(3):
+            low, now, high = beside(xd, i, t)
+            smooth = (low + 4.0 * now + high) * (1.0 / 6.0)
+            slope = (high - low) * 0.5
+            above, below = up(smooth), down(smooth)
+            first = (below - above) * 0.5
+            second = (up(slope) + 4.0 * slope + down(slope)) * (1.0 / 6.0)
+            both = (above + 4.0 * smooth + below) * (1.0 / 6.0)
+            bh, bl = split(both)
+            third = dot3(bh, bl, krh[...], krl[...])
+            for k in range(3):
+                m = comp + 3 * k
+                part = (
+                    modulus[m, i] * first + modulus[m, 3 + i] * second + modulus[m, 6 + i] * third
+                )
+                total[k] = part if total[k] is None else total[k] + part
+        factor = 1.0 + sx[:, lanes(t)]
+        for k in range(3):
+            st[k, :, lanes(t)] = factor * total[k] + hx[k, :, lanes(t)]
+        return carry
+
+    lax.fori_loop(0, tiles + 1, stress_step, 0)
+
+    def pull_step(t, carry):
+        low, now, high = beside(st, 0, t)
+        first = (low + 4.0 * now + high) * (1.0 / 12.0)
+        low, now, high = beside(st, 1, t)
+        second = (high - low) * (1.0 / 12.0)
+        mixed = up(second - first) + down(second + first) + 4.0 * second
+        u = ld[:, lanes(t)] + mixed[0:rows]
+        hi, lo = split(u)
+        uh[:, lanes(t)] = hi
+        ul[:, lanes(t)] = lo
+        low, now, high = beside(st, 2, t)
+        third = (low + 4.0 * now + high) * (1.0 / 36.0)
+        w = (up(third) + 4.0 * third + down(third))[0:rows]
+        hi, lo = split(w)
+        wh[:, lanes(t)] = hi
+        wl[:, lanes(t)] = lo
+        return carry
+
+    lax.fori_loop(0, tiles, pull_step, 0)
+
+    def message_step(t, carry):
+        at = pl.ds(pl.multiple_of(t * 2 * LANES, 2 * LANES), 2 * LANES)
+        value = dot3(kbh[...], kbl[...], uh[:, at], ul[:, at], True)
+        value = value + dot3(kwh[...], kwl[...], wh[:, at], wl[:, at], True)
+        here = pl.ds(pl.multiple_of(t * 8, 8), 8)
+        for peer in range(peers):
+            for m in range(mp):
+                row = (peer * mp + m) * 8
+                outs[peer][here, m * rows : (m + 1) * rows] = value[row : row + 8, :]
+        return carry
+
+    lax.fori_loop(0, tiles // 2, message_step, 0)
+
+
+def stencil(comp, mp, peers, modulus, displace, load, history, stiffen, halos, tables):
+    rows, flat = stiffen.shape
+    tall = rows + HALO
+    wide = flat + LANES
+    shape = jax.ShapeDtypeStruct((flat // R, mp * rows), F32)
+    return pl.pallas_call(
+        functools.partial(stencil_kernel, comp, mp, peers),
+        out_shape=(shape,) * peers,
+        in_specs=[SMEM] + [ANY] * 4 + [VMEM] * 10,
+        out_specs=(VMEM,) * peers,
+        scratch_shapes=[
+            pltpu.VMEM((3, tall, wide), F32),
+            pltpu.VMEM((3, tall, wide), F32),
+            pltpu.VMEM((tall, wide), F32),
+            pltpu.VMEM((rows, flat), F32),
+            pltpu.VMEM((3, tall, wide), F32),
+            pltpu.VMEM((rows, flat), BF),
+            pltpu.VMEM((rows, flat), BF),
+            pltpu.VMEM((rows, flat), BF),
+            pltpu.VMEM((rows, flat), BF),
+            pltpu.SemaphoreType.DMA((8,)),
+        ],
+        compiler_params=params(),
+        cost_estimate=cost(2e9, 10 << 20),
+        name="stencil",
+    )(modulus, displace, load, history, stiffen, *halos, *tables)
+
+
+def cycle_kernel(peers, parts, ids, *refs):
+    ins = refs[:peers]
+    th, tl = refs[peers : peers + 2]
+    outs = refs[peers + 2 : peers + 2 + parts]
+    xh, xl = refs[peers + 2 + parts :]
+    height = ins[0].shape[0]
+    for j in range(peers):
+        source = jnp.bitwise_xor(ids[0], j)
+        at = pl.ds(pl.multiple_of(source * height, height), height)
+        hi, lo = split(ins[j][...])
+        xh[at, :] = hi
+        xl[at, :] = lo
+    block = outs[0].shape[0]
+    for d in range(parts):
+        target = jnp.bitwise_xor(ids[1], d)
+        at = pl.ds(pl.multiple_of(target * block, block), block)
+        outs[d][...] = dot3(th[at, :], tl[at, :], xh[...], xl[...])
+
+
+def cycle_stage(ids, pieces, table, parts):
+    peers = len(pieces)
+    height, width = pieces[0].shape
+    count = peers * height
+    shape = jax.ShapeDtypeStruct((count // parts, width), F32)
+    return pl.pallas_call(
+        functools.partial(cycle_kernel, peers, parts),
+        out_shape=(shape,) * parts,
+        in_specs=[SMEM] + [VMEM] * (peers + 2),
+        out_specs=(VMEM,) * parts,
+        scratch_shapes=[pltpu.VMEM((count, width), BF)] * 2,
+        compiler_params=params(),
+        cost_estimate=cost(6 * count * count * width, 5 << 20),
+        name="cycle_stage",
+    )(ids, *pieces, *table)
+
+
+def axial_kernel(mp, parts, ids, radial, cyc, axial, *refs):
+    ins = refs[:parts]
+    th, tl = refs[parts : parts + 2]
+    outs = refs[parts + 2 : 2 * parts + 2]
+    xh, xl = refs[2 * parts + 2 :]
+    kc, width = ins[0].shape
+    rows = width // mp
+    for j in range(parts):
+        source = jnp.bitwise_xor(ids[1], j)
+        at = pl.ds(pl.multiple_of(source * rows, rows), rows)
+        for m in range(mp):
+            hi, lo = split(ins[j][:, m * rows : (m + 1) * rows])
+            xh[m * kc : (m + 1) * kc, at] = hi
+            xl[m * kc : (m + 1) * kc, at] = lo
+    mine = cyc[pl.ds(pl.multiple_of(ids[1] * kc, kc), kc), :]
+    base = axial[...] + mine
+    for m in range(mp):
+        part = slice(m * kc, (m + 1) * kc)
+        value = dot3(xh[part, :], xl[part, :], th[...], tl[...])
+        value = value / (base + radial[ids[0] * mp + m])
+        hi, lo = split(value)
+        xh[part, :] = hi
+        xl[part, :] = lo
+    for d in range(parts):
+        target = jnp.bitwise_xor(ids[1], d)
+        at = pl.ds(pl.multiple_of(target * rows, rows), rows)
+        outs[d][...] = dot3(th[at, :], tl[at, :], xh[...], xl[...], True)
+
+
+def axial_stage(ids, radial, cyc, axial, pieces, table, mp):
+    parts = len(pieces)
+    kc, width = pieces[0].shape
+    rows = width // mp
+    shape = jax.ShapeDtypeStruct((rows, mp * kc), F32)
+    return pl.pallas_call(
+        functools.partial(axial_kernel, mp, parts),
+        out_shape=(shape,) * parts,
+        in_specs=[SMEM, SMEM] + [VMEM] * (parts + 4),
+        out_specs=(VMEM,) * parts,
+        scratch_shapes=[pltpu.VMEM((mp * kc, parts * rows), BF)] * 2,
+        compiler_params=params(),
+        cost_estimate=cost(12 * parts * rows * parts * rows * mp * kc, 5 << 20),
+        name="axial_stage",
+    )(ids, radial, cyc, axial, *pieces, *table)
+
+
+def uncycle_kernel(mp, parts, peers, ids, *refs):
+    ins = refs[:parts]
+    th, tl, weave = refs[parts : parts + 3]
+    outs = refs[parts + 3 : parts + 3 + peers]
+    xh, xl, full = refs[parts + 3 + peers :]
+    rows, width = ins[0].shape
+    kc = width // mp
+    count = th.shape[1]
+    for j in range(parts):
+        source = jnp.bitwise_xor(ids[1], j)
+        at = pl.ds(pl.multiple_of(source * kc, kc), kc)
+        for m in range(mp):
+            hi, lo = split(ins[j][:, m * kc : (m + 1) * kc])
+            xh[m * rows : (m + 1) * rows, at] = hi
+            xl[m * rows : (m + 1) * rows, at] = lo
+    value = dot3(xh[...], xl[...], th[...], tl[...])
+    hi, lo = split(value)
+    span = mp * LANES
+    for t in range(count // LANES):
+        columns = slice(t * LANES, (t + 1) * LANES)
+
+        def gather(x):
+            return jnp.concatenate(
+                [x[m * rows : (m + 1) * rows, columns] for m in range(mp)], axis=1
+            )
+
+        full[:, t * span : (t + 1) * span] = dot(gather(hi), weave[...]) + dot(
+            gather(lo), weave[...]
+        )
+    few = outs[0].shape[0]
+    for d in range(peers):
+        target = jnp.bitwise_xor(ids[0], d)
+        outs[d][...] = full[pl.ds(pl.multiple_of(target * few, few), few), :]
+
+
+def uncycle_stage(ids, pieces, table, weave, mp, peers):
+    parts = len(pieces)
+    rows, width = pieces[0].shape
+    count = table[0].shape[0]
+    shape = jax.ShapeDtypeStruct((rows // peers, mp * count), F32)
+    return pl.pallas_call(
+        functools.partial(uncycle_kernel, mp, parts, peers),
+        out_shape=(shape,) * peers,
+        in_specs=[SMEM] + [VMEM] * (parts + 3),
+        out_specs=(VMEM,) * peers,
+        scratch_shapes=[
+            pltpu.VMEM((mp * rows, count), BF),
+            pltpu.VMEM((mp * rows, count), BF),
+            pltpu.VMEM((rows, mp * count), F32),
+        ],
+        compiler_params=params(),
+        cost_estimate=cost(8 * mp * rows * count * count, 5 << 20),
+        name="uncycle_stage",
+    )(ids, *pieces, *table, weave)
+
+
+def radial_kernel(comp, peers, *refs):
+    ins = refs[:peers]
+    th, tl = refs[peers : peers + 2]
+    out, xh, xl = refs[-3:]
+    few, width = ins[0].shape
+    groups = width // LANES
+    span = th.shape[1]
+    for j in range(peers):
+        for g in range(groups):
+            hi, lo = split(ins[j][:, g * LANES : (g + 1) * LANES])
+            xh[g * few : (g + 1) * few, j * LANES : (j + 1) * LANES] = hi
+            xl[g * few : (g + 1) * few, j * LANES : (j + 1) * LANES] = lo
+    value = dot3(xh[...], xl[...], th[...], tl[...])
+    for g in range(groups):
+        out[0, :, g * span : (g + 1) * span] = value[g * few : (g + 1) * few, :]
+
+
+def radial_stage(comp, pieces, table, carried):
+    peers = len(pieces)
+    few, width = pieces[0].shape
+    groups = width // LANES
+    depth, span = table[0].shape
+    shape = jax.ShapeDtypeStruct((3, few, groups * span), F32)
+    extra = [] if carried is None else [carried]
+    return pl.pallas_call(
+        functools.partial(radial_kernel, comp, peers),
+        out_shape=shape,
+        grid=(1,),
+        in_specs=[VMEM] * (peers + 2) + [ANY] * len(extra),
+        out_specs=pl.BlockSpec((1, few, groups * span), lambda g: (comp, 0, 0)),
+        scratch_shapes=[pltpu.VMEM((groups * few, depth), BF)] * 2,
+        input_output_aliases={peers + 2: 0} if extra else {},
+        compiler_params=params(),
+        cost_estimate=cost(6 * groups * few * depth * span, 6 << 20),
+        name="radial_stage",
+    )(*pieces, *table, *extra)
+
+
+def swap(pieces, axis):
+    count = len(pieces)
+    return [pieces[0]] + [
+        lax.ppermute(pieces[d], axis, [(i, i ^ d) for i in range(count)]) for d in range(1, count)
+    ]
+
+
+def body(
+    displace,
+    load,
+    history,
+    stiffen,
+    modulus,
+    radial_slope,
+    radial_basis,
+    axial_eig,
+    cycle_eig,
+    radial_eig,
+):
+    parts = lax.axis_size("ax")
+    peers = lax.axis_size("circ")
+    mp = R // peers
+    rows, flat = stiffen.shape
+    count_a = parts * rows
+    count_c = peers * flat // R
+    me = lax.axis_index("circ").astype(jnp.int32)
+    pe = lax.axis_index("ax").astype(jnp.int32)
+    ids = jnp.stack([me, pe])
+
+    upward, downward = pack_rows(displace, history, stiffen)
+    ahead = [(i, i + 1) for i in range(parts - 1)]
+    bottom = lax.ppermute(upward, "ax", [(j, i) for i, j in ahead])
+    top = lax.ppermute(downward, "ax", ahead)
+    front = front_tables(ids, radial_slope, radial_basis, mp)
+    to_left, to_right = pack_cols(displace, history, stiffen, top, bottom)
+    around = [(i, (i + 1) % peers) for i in range(peers)]
+    right = lax.ppermute(to_left, "circ", [(j, i) for i, j in around])
+    left = lax.ppermute(to_right, "circ", around)
+    back = back_tables(ids, radial_basis, mp, peers)
+    halos = (top, bottom, left, right)
+
+    cycle_table_parts = host_split(host_cycle(count_c))
+    axial_table_parts = host_split(host_axial(count_a))
+    weave = host_weave(mp)
+    cyc = cycle_eig[:, None]
+    axial = axial_eig[None, :]
+
+    out = None
+    lines = []
+    for i in range(3):
+        sent = stencil(
+            i, mp, peers, modulus, displace, load, history, stiffen, halos, front
+        )
+        lines.append(swap(list(sent), "circ"))
+    lines = [swap(list(cycle_stage(ids, x, cycle_table_parts, parts)), "ax") for x in lines]
+    lines = [
+        swap(list(axial_stage(ids, radial_eig, cyc, axial, x, axial_table_parts, mp)), "ax")
+        for x in lines
+    ]
+    lines = [
+        swap(list(uncycle_stage(ids, x, cycle_table_parts, weave, mp, peers)), "circ")
+        for x in lines
+    ]
+    for i in range(3):
+        out = radial_stage(i, lines[i], back, out)
+    return out
+
+
+def tiled(mesh):
+    parts, peers = mesh.shape["ax"], mesh.shape["circ"]
+    rows, flat = NA // parts, NC // peers * R
+    return (
+        parts & (parts - 1) == 0
+        and peers & (peers - 1) == 0
+        and R == 32
+        and R % peers == 0
+        and peers * (R // peers) * 8 == 8 * R
+        and rows % LANES == 0
+        and (NC // parts) % LANES == 0
+        and flat % (2 * LANES) == 0
+        and (NC // peers) % 16 == 0
+        and (rows // peers) % 16 == 0
+    )
+
+
 def solution(mesh):
     return jax.shard_map(
-        body,
+        body if tiled(mesh) else plain_body,
         mesh=mesh,
         in_specs=(
             P(None, "ax", "circ"),

time: 811 us -> 291 us (0.36)
  blocking collectives: 192 us -> 0 us
  local copies, waits for them, and re-layouts: 170 us -> 16.6 us
  other arithmetic: 134 us -> 0.07 us
  matrix products: 129 us -> 0 us
  Pallas kernels: 0 us -> 107 us
  waiting for transfers between devices: 152 us -> 71.8 us
  starting transfers between devices: 28.2 us -> 90.2 us
    all_to_all x3 -> x0, blocking collectives: 192 us -> none  [the longest x1 98 us: body(): lax.all_to_all(lax.all_to_all(solved, 'ax', split_axis=1, concat_axis=2,...]
    all_to_all x2 -> x0, waiting for transfers between devices: 139 us -> none  [the longest x1 94 us: into_cycles(): lax.all_to_all(field, 'circ', split_axis=1, concat_axis=2, tiled=True)]
    dot_general x8 -> x0, matrix products: 118 us -> none  [the longest x1 41.2 us: body(): jnp.einsum('mn,nac->mac', modulus, grads, precision=lax.Precision.HIGHEST)]
    pallas_call x0 -> x19, Pallas kernels: none -> 107 us  [the longest x3 65.3 us: stencil(): pl.pallas_call(functools.partial(stencil_kernel, comp, mp, peers), out_sh...]
    div x5 -> x0, other arithmetic: 78.5 us -> none  [the longest x2 64 us: cycle_parts(): return ((left + 4.0 * middle + right) / 6.0, (right - left) * 0.5)]
    ppermute x8 -> x64, starting transfers between devices: 19.7 us -> 90.2 us  [the longest x60 80.4 us: swap(): lax.ppermute(pieces[d], axis, [(i, i ^ d) for i in range(count)])]
    ppermute x8 -> x64, waiting for transfers between devices: 13.5 us -> 71.8 us  [the longest x60 62.8 us: swap(): lax.ppermute(pieces[d], axis, [(i, i ^ d) for i in range(count)])]
    reshape x6 -> x0, local copies, waits for them, and re-layouts: 41.6 us -> none  [the longest x2 14.2 us: cycle_forward(): cube = field.reshape(count * rows, NC, R)]
  transfers between devices with their start and end apart: 10 -> 64, of which waited for: 8 -> 17; matrix products, arithmetic and copies ran while one was open for 4% -> 0% of each run, Pallas kernels for 0% -> 28%
where the time goes in v1:
time: 291 us; the launch traced here: 286 us
  Pallas kernels  107 us (37%)
  starting transfers between devices  90.2 us (31%)
  waiting for transfers between devices  71.8 us (25%)
  local copies, waits for them, and re-layouts  16.6 us (6%)
    ppermute x60, starting transfers between devices, swap(): lax.ppermute(pieces[d], axis, [(i, i ^ d) for i in range(count)])  80.4 us
    pallas_call x3, Pallas kernels, stencil(): pl.pallas_call(functools.partial(stencil_kernel, comp, mp, peers), out_sh...  65.3 us
    ppermute x60, waiting for transfers between devices, swap(): lax.ppermute(pieces[d], axis, [(i, i ^ d) for i in range(count)])  62.8 us
    unnamed x68, local copies, waits for them, and re-layouts  16.4 us
    pallas_call x3, Pallas kernels, axial_stage(): pl.pallas_call(functools.partial(axial_kernel, mp, parts), out_shape=(sha...  10.8 us
    pallas_call x3, Pallas kernels, radial_stage(): pl.pallas_call(functools.partial(radial_kernel, comp, peers), out_shape=s...  8.45 us
    pallas_call x3, Pallas kernels, uncycle_stage(): pl.pallas_call(functools.partial(uncycle_kernel, mp, parts, peers), out_s...  7.24 us
  transfers between devices with their start and end apart: 64, of which 17 were waited for; matrix products, arithmetic and copies ran while one was open for 0% of the time, Pallas kernels for 28%

profile of v1, /device:TPU:0, one launch (start us, length us, event | category | flops | bytes accessed | tf_op | source)
XLA Modules:
  0.0 285.9 jit_solution(11644413640575913471)
XLA Ops:
  4.5 4.8 %collective-permute-start = (f32[16,2048]{1,0:T(8,128)S(1)}, f32[16,2048]{1,0:T(8,128)S(1)}, u32[]{:S(2)}, u32[]{:S(2)}) collective-permute-start(f32[16,2048]{1,0:T(8,128)S(1)} %get-tuple-element.89), channel_id=1, source_target_pairs={{0,8},{8,16},{16,24},{1,9},{9,17},{17,25},{2,10},{10,18},{18,26},{... | collective-permute-start | bytes 393224 | tf_op jit(solution)/shard_map/ppermute | solution.py:807
  12.1 4.8 %collective-permute-done.1.bl.br.bottom = f32[16,2048]{1,0:T(8,128)S(1)} collective-permute-done((f32[16,2048]{1,0:T(8,128)S(1)}, f32[16,2048]{1,0:T(8,128)S(1)}, u32[]{:S(2)}, u32[]{:S(2)}) %collective-permute-start.1) | collective-permute-done | bytes 131104 | tf_op jit(solution)/shard_map/ppermute | solution.py:806
  18.6 3.5 %collective-permute-start.3 = (f32[136,512]{1,0:T(8,128)S(1)}, f32[136,512]{1,0:T(8,128)S(1)}, u32[]{:S(2)}, u32[]{:S(2)}) collective-permute-start(f32[136,512]{1,0:T(8,128)S(1)} %get-tuple-element.92), channel_id=1, source_target_pairs={{1,0},{2,1},{3,2},{4,3},{5,4},{6,5},{7,6},{0,7},{9,8},{10,9},{11,1... | collective-permute-start | bytes 835592 | tf_op jit(solution)/shard_map/ppermute | solution.py:811
  24.1 3.0 %collective-permute-done.2.left = f32[136,512]{1,0:T(8,128)S(1)} collective-permute-done((f32[136,512]{1,0:T(8,128)S(1)}, f32[136,512]{1,0:T(8,128)S(1)}, u32[]{:S(2)}, u32[]{:S(2)}) %collective-permute-start.2) | collective-permute-done | bytes 278560 | tf_op jit(solution)/shard_map/ppermute | solution.py:812
  27.2 21.8 %stencil.5 = (f32[64,512]{1,0:T(8,128)S(1)}, f32[64,512]{1,0:T(8,128)S(1)}, f32[64,512]{1,0:T(8,128)S(1)}, f32[64,512]{1,0:T(8,128)S(1)}, f32[64,512]{1,0:T(8,12...) custom-call(f32[9,9]{1,0:T(8,128)S(1)} %copy-done.3, f32[3,128,2048]{2,1,0:T(8,128)} %displace.5, ...), custom_call_target="tpu_custom_call" | custom-call | flops 2000000000 | bytes 10485760 | tf_op jit(solution)/shard_map/stencil/pallas_call | solution.py:576
  55.4 21.6 %stencil.4 = (f32[64,512]{1,0:T(8,128)S(1)}, f32[64,512]{1,0:T(8,128)S(1)}, f32[64,512]{1,0:T(8,128)S(1)}, f32[64,512]{1,0:T(8,128)S(1)}, f32[64,512]{1,0:T(8,12...) custom-call(f32[9,9]{1,0:T(8,128)S(1)} %copy-done.3, f32[3,128,2048]{2,1,0:T(8,128)} %displace.5, ...), custom_call_target="tpu_custom_call" | custom-call | flops 2000000000 | bytes 10485760 | tf_op jit(solution)/shard_map/stencil/pallas_call | solution.py:576
  82.5 21.9 %stencil.3 = (f32[64,512]{1,0:T(8,128)S(1)}, f32[64,512]{1,0:T(8,128)S(1)}, f32[64,512]{1,0:T(8,128)S(1)}, f32[64,512]{1,0:T(8,128)S(1)}, f32[64,512]{1,0:T(8,12...) custom-call(f32[9,9]{1,0:T(8,128)S(1)} %copy-done.3, f32[3,128,2048]{2,1,0:T(8,128)} %displace.5, ...), custom_call_target="tpu_custom_call" | custom-call | flops 2000000000 | bytes 10485760 | tf_op jit(solution)/shard_map/stencil/pallas_call | solution.py:576
  109.4 7.4 %collective-permute-done.27.refs_4_ = f32[64,512]{1,0:T(8,128)S(1)} collective-permute-done((f32[64,512]{1,0:T(8,128)S(1)}, f32[64,512]{1,0:T(8,128)S(1)}, u32[]{:S(2)}, u32[]{:S(2)}) %collective-permute-start.27) | collective-permute-done | bytes 131104 | tf_op jit(solution)/shard_map/ppermute | solution.py:778
  127.4 6.5 %collective-permute-done.7.refs_4_ = f32[64,512]{1,0:T(8,128)S(1)} collective-permute-done((f32[64,512]{1,0:T(8,128)S(1)}, f32[64,512]{1,0:T(8,128)S(1)}, u32[]{:S(2)}, u32[]{:S(2)}) %collective-permute-start.7) | collective-permute-done | bytes 131104 | tf_op jit(solution)/shard_map/ppermute | solution.py:778
  166.1 3.5 %axial_stage.5 = (f32[128,512]{1,0:T(8,128)S(1)}, f32[128,512]{1,0:T(8,128)S(1)}, f32[128,512]{1,0:T(8,128)S(1)}, f32[128,512]{1,0:T(8,128)S(1)}) custom-call(s32[2]{0:T(128)S(1)} %pad_add_fusion.me_ref.ids, f32[32]{0:T(128)S(1)} %copy-done.19, f32[512,1]{1,0:T(8,128)S(1)} %copy.18.cyc, f32[1,512]{1,0:T(1,128)S(1)} %bitcast.4, f32[128,512]{1,0:T(8,128)S(1)} %copy-done.30, ...), custom_call_target="tpu_custom_call" | custom-call | flops 1610612736 | bytes 5242880 | tf_op jit(solution)/shard_map/axial_stage/pallas_call | solution.py:669
  173.3 3.6 %axial_stage.3 = (f32[128,512]{1,0:T(8,128)S(1)}, f32[128,512]{1,0:T(8,128)S(1)}, f32[128,512]{1,0:T(8,128)S(1)}, f32[128,512]{1,0:T(8,128)S(1)}) custom-call(s32[2]{0:T(128)S(1)} %pad_add_fusion.me_ref.ids, f32[32]{0:T(128)S(1)} %copy-done.19, f32[512,1]{1,0:T(8,128)S(1)} %copy.18.cyc, f32[1,512]{1,0:T(1,128)S(1)} %bitcast.5, f32[128,512]{1,0:T(8,128)S(1)} %copy-done.32, ...), custom_call_target="tpu_custom_call" | custom-call | flops 1610612736 | bytes 5242880 | tf_op jit(solution)/shard_map/axial_stage/pallas_call | solution.py:669
  180.4 3.7 %axial_stage.4 = (f32[128,512]{1,0:T(8,128)S(1)}, f32[128,512]{1,0:T(8,128)S(1)}, f32[128,512]{1,0:T(8,128)S(1)}, f32[128,512]{1,0:T(8,128)S(1)}) custom-call(s32[2]{0:T(128)S(1)} %pad_add_fusion.me_ref.ids, f32[32]{0:T(128)S(1)} %copy-done.19, f32[512,1]{1,0:T(8,128)S(1)} %copy.18.cyc, f32[1,512]{1,0:T(1,128)S(1)} %bitcast.6, ...), custom_call_target="tpu_custom_call" | custom-call | flops 1610612736 | bytes 5242880 | tf_op jit(solution)/shard_map/axial_stage/pallas_call | solution.py:669
  187.6 3.6 %collective-permute-done.56.refs_3_ = f32[128,512]{1,0:T(8,128)S(1)} collective-permute-done((f32[128,512]{1,0:T(8,128)S(1)}, f32[128,512]{1,0:T(8,128)S(1)}, u32[]{:S(2)}, u32[]{:S(2)}) %collective-permute-start.56) | collective-permute-done | bytes 262176 | tf_op jit(solution)/shard_map/ppermute | solution.py:778
  191.2 4.2 %collective-permute-done.14.refs_1_ = f32[128,512]{1,0:T(8,128)S(1)} collective-permute-done((f32[128,512]{1,0:T(8,128)S(1)}, f32[128,512]{1,0:T(8,128)S(1)}, u32[]{:S(2)}, u32[]{:S(2)}) %collective-permute-start.14) | collective-permute-done | bytes 262176 | tf_op jit(solution)/shard_map/ppermute | solution.py:778
  202.5 4.8 %collective-permute-start.58 = (f32[16,2048]{1,0:T(8,128)S(1)}, f32[16,2048]{1,0:T(8,128)S(1)}, u32[]{:S(2)}, u32[]{:S(2)}) collective-permute-start(f32[16,2048]{1,0:T(8,128)S(1)} %get-tuple-element.167), channel_id=1, source_target_pairs={{0,2},{1,3},{2,0},{3,1},{4,6},{5,7},{6,4},{7,5},{8,10},{9,11},{10,... | collective-permute-start | bytes 393224 | tf_op jit(solution)/shard_map/ppermute | solution.py:778
  209.0 4.7 %collective-permute-start.60 = (f32[16,2048]{1,0:T(8,128)S(1)}, f32[16,2048]{1,0:T(8,128)S(1)}, u32[]{:S(2)}, u32[]{:S(2)}) collective-permute-start(f32[16,2048]{1,0:T(8,128)S(1)} %get-tuple-element.169), channel_id=1, source_target_pairs={{0,4},{1,5},{2,6},{3,7},{4,0},{5,1},{6,2},{7,3},{8,12},{9,13},{10,... | collective-permute-start | bytes 393224 | tf_op jit(solution)/shard_map/ppermute | solution.py:778
  222.4 3.2 %collective-permute-start.63 = (f32[16,2048]{1,0:T(8,128)S(1)}, f32[16,2048]{1,0:T(8,128)S(1)}, u32[]{:S(2)}, u32[]{:S(2)}) collective-permute-start(f32[16,2048]{1,0:T(8,128)S(1)} %get-tuple-element.172), channel_id=1, source_target_pairs={{0,7},{1,6},{2,5},{3,4},{4,3},{5,2},{6,1},{7,0},{8,15},{9,14},{10,... | collective-permute-start | bytes 393224 | tf_op jit(solution)/shard_map/ppermute | solution.py:778
  225.7 7.2 %collective-permute-done.61.refs_5_ = f32[16,2048]{1,0:T(8,128)S(1)} collective-permute-done((f32[16,2048]{1,0:T(8,128)S(1)}, f32[16,2048]{1,0:T(8,128)S(1)}, u32[]{:S(2)}, u32[]{:S(2)}) %collective-permute-start.61) | collective-permute-done | bytes 131104 | tf_op jit(solution)/shard_map/ppermute | solution.py:778
  235.0 4.9 %back_tables.1 = (bf16[1024,1024]{1,0:T(8,128)(2,1)S(1)}, bf16[1024,1024]{1,0:T(8,128)(2,1)S(1)}) custom-call(s32[2]{0:T(128)S(1)} %pad_add_fusion.me_ref.ids, f32[32,32]{1,0:T(8,128)S(1)} %copy-done.4), custom_call_target="tpu_custom_call" | custom-call | tf_op jit(solution)/shard_map/back_tables/pallas_call | solution.py:314
  249.7 9.6 %collective-permute-done.40.refs_4_ = f32[16,2048]{1,0:T(8,128)S(1)} collective-permute-done((f32[16,2048]{1,0:T(8,128)S(1)}, f32[16,2048]{1,0:T(8,128)S(1)}, u32[]{:S(2)}, u32[]{:S(2)}) %collective-permute-start.40) | collective-permute-done | bytes 131104 | tf_op jit(solution)/shard_map/ppermute | solution.py:778
  260.8 3.3 %collective-permute-start.22 = (f32[16,2048]{1,0:T(8,128)S(1)}, f32[16,2048]{1,0:T(8,128)S(1)}, u32[]{:S(2)}, u32[]{:S(2)}) collective-permute-start(f32[16,2048]{1,0:T(8,128)S(1)} %get-tuple-element.121), channel_id=1, source_target_pairs={{0,6},{1,7},{2,4},{3,5},{4,2},{5,3},{6,0},{7,1},{8,14},{9,15},{10,... | collective-permute-start | bytes 393224 | tf_op jit(solution)/shard_map/ppermute | solution.py:778
  264.1 3.8 %collective-permute-start.23 = (f32[16,2048]{1,0:T(8,128)S(1)}, f32[16,2048]{1,0:T(8,128)S(1)}, u32[]{:S(2)}, u32[]{:S(2)}) collective-permute-start(f32[16,2048]{1,0:T(8,128)S(1)} %get-tuple-element.122), channel_id=1, source_target_pairs={{0,7},{1,6},{2,5},{3,4},{4,3},{5,2},{6,1},{7,0},{8,15},{9,14},{10,... | collective-permute-start | bytes 393224 | tf_op jit(solution)/shard_map/ppermute | solution.py:778
  270.7 11.1 %collective-permute-done.20.refs_4_ = f32[16,2048]{1,0:T(8,128)S(1)} collective-permute-done((f32[16,2048]{1,0:T(8,128)S(1)}, f32[16,2048]{1,0:T(8,128)S(1)}, u32[]{:S(2)}, u32[]{:S(2)}) %collective-permute-start.20) | collective-permute-done | bytes 131104 | tf_op jit(solution)/shard_map/ppermute | solution.py:778
  283.1 2.8 radial_stage.5
  (193 shorter events, 116.1 us)
Async XLA Ops:
  48.9 28.1 %collective-permute-start.44 = (f32[64,512]{1,0:T(8,128)S(1)}, f32[64,512]{1,0:T(8,128)S(1)}, u32[]{:S(2)}, u32[]{:S(2)}) collective-permute-start(f32[64,512]{1,0:T(8,128)S(1)} %get-tuple-element.150), channel_id=1, source_target_pairs={{0,1},{1,0},{2,3},{3,2},{4,5},{5,4},{6,7},{7,6},{8,9},{9,8},{10,11... | collective-permute-start | bytes 393224 | tf_op jit(solution)/shard_map/ppermute | solution.py:778
  51.0 28.2 %collective-permute-start.45 = (f32[64,512]{1,0:T(8,128)S(1)}, f32[64,512]{1,0:T(8,128)S(1)}, u32[]{:S(2)}, u32[]{:S(2)}) collective-permute-start(f32[64,512]{1,0:T(8,128)S(1)} %get-tuple-element.151), channel_id=1, source_target_pairs={{0,2},{1,3},{2,0},{3,1},{4,6},{5,7},{6,4},{7,5},{8,10},{9,11},{10,... | collective-permute-start | bytes 393224 | tf_op jit(solution)/shard_map/ppermute | solution.py:778
  51.5 28.8 %collective-permute-start.46 = (f32[64,512]{1,0:T(8,128)S(1)}, f32[64,512]{1,0:T(8,128)S(1)}, u32[]{:S(2)}, u32[]{:S(2)}) collective-permute-start(f32[64,512]{1,0:T(8,128)S(1)} %get-tuple-element.152), channel_id=1, source_target_pairs={{0,3},{1,2},{2,1},{3,0},{4,7},{5,6},{6,5},{7,4},{8,11},{9,10},{10,... | collective-permute-start | bytes 393224 | tf_op jit(solution)/shard_map/ppermute | solution.py:778
  52.4 28.7 %collective-permute-start.47 = (f32[64,512]{1,0:T(8,128)S(1)}, f32[64,512]{1,0:T(8,128)S(1)}, u32[]{:S(2)}, u32[]{:S(2)}) collective-permute-start(f32[64,512]{1,0:T(8,128)S(1)} %get-tuple-element.153), channel_id=1, source_target_pairs={{0,4},{1,5},{2,6},{3,7},{4,0},{5,1},{6,2},{7,3},{8,12},{9,13},{10,... | collective-permute-start | bytes 393224 | tf_op jit(solution)/shard_map/ppermute | solution.py:778
  53.8 27.2 %collective-permute-start.48 = (f32[64,512]{1,0:T(8,128)S(1)}, f32[64,512]{1,0:T(8,128)S(1)}, u32[]{:S(2)}, u32[]{:S(2)}) collective-permute-start(f32[64,512]{1,0:T(8,128)S(1)} %get-tuple-element.154), channel_id=1, source_target_pairs={{0,5},{1,4},{2,7},{3,6},{4,1},{5,0},{6,3},{7,2},{8,13},{9,12},{10,... | collective-permute-start | bytes 393224 | tf_op jit(solution)/shard_map/ppermute | solution.py:778
  77.0 27.4 %collective-permute-start.49 = (f32[64,512]{1,0:T(8,128)S(1)}, f32[64,512]{1,0:T(8,128)S(1)}, u32[]{:S(2)}, u32[]{:S(2)}) collective-permute-start(f32[64,512]{1,0:T(8,128)S(1)} %get-tuple-element.155), channel_id=1, source_target_pairs={{0,6},{1,7},{2,4},{3,5},{4,2},{5,3},{6,0},{7,1},{8,14},{9,15},{10,... | collective-permute-start | bytes 393224 | tf_op jit(solution)/shard_map/ppermute | solution.py:778
  79.2 26.6 %collective-permute-start.50 = (f32[64,512]{1,0:T(8,128)S(1)}, f32[64,512]{1,0:T(8,128)S(1)}, u32[]{:S(2)}, u32[]{:S(2)}) collective-permute-start(f32[64,512]{1,0:T(8,128)S(1)} %get-tuple-element.156), channel_id=1, source_target_pairs={{0,7},{1,6},{2,5},{3,4},{4,3},{5,2},{6,1},{7,0},{8,15},{9,14},{10,... | collective-permute-start | bytes 393224 | tf_op jit(solution)/shard_map/ppermute | solution.py:778
  80.3 27.2 %collective-permute-start.24 = (f32[64,512]{1,0:T(8,128)S(1)}, f32[64,512]{1,0:T(8,128)S(1)}, u32[]{:S(2)}, u32[]{:S(2)}) collective-permute-start(f32[64,512]{1,0:T(8,128)S(1)} %get-tuple-element.126), channel_id=1, source_target_pairs={{0,1},{1,0},{2,3},{3,2},{4,5},{5,4},{6,7},{7,6},{8,9},{9,8},{10,11... | collective-permute-start | bytes 393224 | tf_op jit(solution)/shard_map/ppermute | solution.py:778
  81.0 26.5 %collective-permute-start.25 = (f32[64,512]{1,0:T(8,128)S(1)}, f32[64,512]{1,0:T(8,128)S(1)}, u32[]{:S(2)}, u32[]{:S(2)}) collective-permute-start(f32[64,512]{1,0:T(8,128)S(1)} %get-tuple-element.127), channel_id=1, source_target_pairs={{0,2},{1,3},{2,0},{3,1},{4,6},{5,7},{6,4},{7,5},{8,10},{9,11},{10,... | collective-permute-start | bytes 393224 | tf_op jit(solution)/shard_map/ppermute | solution.py:778
  81.1 27.1 %collective-permute-start.26 = (f32[64,512]{1,0:T(8,128)S(1)}, f32[64,512]{1,0:T(8,128)S(1)}, u32[]{:S(2)}, u32[]{:S(2)}) collective-permute-start(f32[64,512]{1,0:T(8,128)S(1)} %get-tuple-element.128), channel_id=1, source_target_pairs={{0,3},{1,2},{2,1},{3,0},{4,7},{5,6},{6,5},{7,4},{8,11},{9,10},{10,... | collective-permute-start | bytes 393224 | tf_op jit(solution)/shard_map/ppermute | solution.py:778
  125.4 24.7 %collective-permute-start.51 = (f32[128,512]{1,0:T(8,128)S(1)}, f32[128,512]{1,0:T(8,128)S(1)}, u32[]{:S(2)}, u32[]{:S(2)}) collective-permute-start(f32[128,512]{1,0:T(8,128)S(1)} %get-tuple-element.158), channel_id=1, source_target_pairs={{0,8},{8,0},{16,24},{24,16},{1,9},{9,1},{17,25},{25,17},{2,10},{10... | collective-permute-start | bytes 786440 | tf_op jit(solution)/shard_map/ppermute | solution.py:778
  133.9 26.2 %collective-permute-start.52 = (f32[128,512]{1,0:T(8,128)S(1)}, f32[128,512]{1,0:T(8,128)S(1)}, u32[]{:S(2)}, u32[]{:S(2)}) collective-permute-start(f32[128,512]{1,0:T(8,128)S(1)} %get-tuple-element.159), channel_id=1, source_target_pairs={{0,16},{8,24},{16,0},{24,8},{1,17},{9,25},{17,1},{25,9},{2,18},{10... | collective-permute-start | bytes 786440 | tf_op jit(solution)/shard_map/ppermute | solution.py:778
  136.5 24.6 %collective-permute-start.53 = (f32[128,512]{1,0:T(8,128)S(1)}, f32[128,512]{1,0:T(8,128)S(1)}, u32[]{:S(2)}, u32[]{:S(2)}) collective-permute-start(f32[128,512]{1,0:T(8,128)S(1)} %get-tuple-element.160), channel_id=1, source_target_pairs={{0,24},{8,16},{16,8},{24,0},{1,25},{9,17},{17,9},{25,1},{2,26},{10... | collective-permute-start | bytes 786440 | tf_op jit(solution)/shard_map/ppermute | solution.py:778
  144.8 24.9 %collective-permute-start.11 = (f32[128,512]{1,0:T(8,128)S(1)}, f32[128,512]{1,0:T(8,128)S(1)}, u32[]{:S(2)}, u32[]{:S(2)}) collective-permute-start(f32[128,512]{1,0:T(8,128)S(1)} %get-tuple-element.108), channel_id=1, source_target_pairs={{0,8},{8,0},{16,24},{24,16},{1,9},{9,1},{17,25},{25,17},{2,10},{10... | collective-permute-start | bytes 786440 | tf_op jit(solution)/shard_map/ppermute | solution.py:778
  147.9 22.5 %collective-permute-start.12 = (f32[128,512]{1,0:T(8,128)S(1)}, f32[128,512]{1,0:T(8,128)S(1)}, u32[]{:S(2)}, u32[]{:S(2)}) collective-permute-start(f32[128,512]{1,0:T(8,128)S(1)} %get-tuple-element.109), channel_id=1, source_target_pairs={{0,16},{8,24},{16,0},{24,8},{1,17},{9,25},{17,1},{25,9},{2,18},{10... | collective-permute-start | bytes 786440 | tf_op jit(solution)/shard_map/ppermute | solution.py:778
  150.1 21.1 %collective-permute-start.13 = (f32[128,512]{1,0:T(8,128)S(1)}, f32[128,512]{1,0:T(8,128)S(1)}, u32[]{:S(2)}, u32[]{:S(2)}) collective-permute-start(f32[128,512]{1,0:T(8,128)S(1)} %get-tuple-element.110), channel_id=1, source_target_pairs={{0,24},{8,16},{16,8},{24,0},{1,25},{9,17},{17,9},{25,1},{2,26},{10... | collective-permute-start | bytes 786440 | tf_op jit(solution)/shard_map/ppermute | solution.py:778
  179.9 20.0 %collective-permute-start.15 = (f32[128,512]{1,0:T(8,128)S(1)}, f32[128,512]{1,0:T(8,128)S(1)}, u32[]{:S(2)}, u32[]{:S(2)}) collective-permute-start(f32[128,512]{1,0:T(8,128)S(1)} %get-tuple-element.113), channel_id=1, source_target_pairs={{0,16},{8,24},{16,0},{24,8},{1,17},{9,25},{17,1},{25,9},{2,18},{10... | collective-permute-start | bytes 786440 | tf_op jit(solution)/shard_map/ppermute | solution.py:778
  186.2 21.1 %collective-permute-start.34 = (f32[128,512]{1,0:T(8,128)S(1)}, f32[128,512]{1,0:T(8,128)S(1)}, u32[]{:S(2)}, u32[]{:S(2)}) collective-permute-start(f32[128,512]{1,0:T(8,128)S(1)} %get-tuple-element.138), channel_id=1, source_target_pairs={{0,8},{8,0},{16,24},{24,16},{1,9},{9,1},{17,25},{25,17},{2,10},{10... | collective-permute-start | bytes 786440 | tf_op jit(solution)/shard_map/ppermute | solution.py:778
  202.5 19.9 %collective-permute-start.58 = (f32[16,2048]{1,0:T(8,128)S(1)}, f32[16,2048]{1,0:T(8,128)S(1)}, u32[]{:S(2)}, u32[]{:S(2)}) collective-permute-start(f32[16,2048]{1,0:T(8,128)S(1)} %get-tuple-element.167), channel_id=1, source_target_pairs={{0,2},{1,3},{2,0},{3,1},{4,6},{5,7},{6,4},{7,5},{8,10},{9,11},{10,... | collective-permute-start | bytes 393224 | tf_op jit(solution)/shard_map/ppermute | solution.py:778
  213.7 19.2 %collective-permute-start.61 = (f32[16,2048]{1,0:T(8,128)S(1)}, f32[16,2048]{1,0:T(8,128)S(1)}, u32[]{:S(2)}, u32[]{:S(2)}) collective-permute-start(f32[16,2048]{1,0:T(8,128)S(1)} %get-tuple-element.170), channel_id=1, source_target_pairs={{0,5},{1,4},{2,7},{3,6},{4,1},{5,0},{6,3},{7,2},{8,13},{9,12},{10,... | collective-permute-start | bytes 393224 | tf_op jit(solution)/shard_map/ppermute | solution.py:778
  249.7 21.0 %collective-permute-start.19 = (f32[16,2048]{1,0:T(8,128)S(1)}, f32[16,2048]{1,0:T(8,128)S(1)}, u32[]{:S(2)}, u32[]{:S(2)}) collective-permute-start(f32[16,2048]{1,0:T(8,128)S(1)} %get-tuple-element.118), channel_id=1, source_target_pairs={{0,3},{1,2},{2,1},{3,0},{4,7},{5,6},{6,5},{7,4},{8,11},{9,10},{10,... | collective-permute-start | bytes 393224 | tf_op jit(solution)/shard_map/ppermute | solution.py:778
  259.3 22.4 %collective-permute-start.20 = (f32[16,2048]{1,0:T(8,128)S(1)}, f32[16,2048]{1,0:T(8,128)S(1)}, u32[]{:S(2)}, u32[]{:S(2)}) collective-permute-start(f32[16,2048]{1,0:T(8,128)S(1)} %get-tuple-element.119), channel_id=1, source_target_pairs={{0,4},{1,5},{2,6},{3,7},{4,0},{5,1},{6,2},{7,3},{8,12},{9,13},{10,... | collective-permute-start | bytes 393224 | tf_op jit(solution)/shard_map/ppermute | solution.py:778
  260.8 22.3 %collective-permute-start.21 = (f32[16,2048]{1,0:T(8,128)S(1)}, f32[16,2048]{1,0:T(8,128)S(1)}, u32[]{:S(2)}, u32[]{:S(2)}) collective-permute-start(f32[16,2048]{1,0:T(8,128)S(1)} %get-tuple-element.120), channel_id=1, source_target_pairs={{0,5},{1,4},{2,7},{3,6},{4,1},{5,0},{6,3},{7,2},{8,13},{9,12},{10,... | collective-permute-start | bytes 393224 | tf_op jit(solution)/shard_map/ppermute | solution.py:778
  260.8 22.3 %collective-permute-start.22 = (f32[16,2048]{1,0:T(8,128)S(1)}, f32[16,2048]{1,0:T(8,128)S(1)}, u32[]{:S(2)}, u32[]{:S(2)}) collective-permute-start(f32[16,2048]{1,0:T(8,128)S(1)} %get-tuple-element.121), channel_id=1, source_target_pairs={{0,6},{1,7},{2,4},{3,5},{4,2},{5,3},{6,0},{7,1},{8,14},{9,15},{10,... | collective-permute-start | bytes 393224 | tf_op jit(solution)/shard_map/ppermute | solution.py:778
  (74 other events, 1058.4 us)

commit v2 on v0

--- a/solution.py
+++ b/solution.py
@@ -1,8 +1,14 @@
 import math
+
+import functools
 
 import jax
 import jax.numpy as jnp
+import ml_dtypes
+import numpy as np
 from jax import lax
+from jax.experimental import pallas as pl
+from jax.experimental.pallas import tpu as pltpu
 from jax.sharding import PartitionSpec as P
 
 NA = 512
@@ -100,7 +106,7 @@
     )
 
 
-def body(
+def plain_body(
     displace,
     load,
     history,
@@ -168,9 +174,863 @@
     return cycle_inverse(cycles_back, table_cycle, radial_basis)
 
 
+BF = jnp.bfloat16
+F32 = jnp.float32
+VMEM = pl.BlockSpec(memory_space=pltpu.VMEM)
+SMEM = pl.BlockSpec(memory_space=pltpu.SMEM)
+HBM = pl.BlockSpec(memory_space=pltpu.HBM)
+HALO = 8
+PAD = 8
+LANES = 128
+
+
+def params(mebibytes=24):
+    return pltpu.CompilerParams(vmem_limit_bytes=mebibytes << 20)
+
+
+def cost(microseconds):
+    return pl.CostEstimate(flops=1, bytes_accessed=int(microseconds * 3.6e6) + 1, transcendentals=0)
+
+
+def split(x):
+    hi = x.astype(BF)
+    return hi, (x - hi.astype(F32)).astype(BF)
+
+
+def dot(a, b, transposed=False):
+    dims = (((1,), (1 if transposed else 0,)), ((), ()))
+    return lax.dot_general(a, b, dims, preferred_element_type=F32)
+
+
+def dot3(ah, al, bh, bl, transposed=False):
+    return dot(ah, bh, transposed) + (dot(ah, bl, transposed) + dot(al, bh, transposed))
+
+
+def exact(a, b, transposed=False):
+    dims = (((1,), (1 if transposed else 0,)), ((), ()))
+    return lax.dot_general(
+        a, b, dims, precision=lax.Precision.HIGHEST, preferred_element_type=F32
+    )
+
+
+def host_split(table):
+    hi = table.astype(np.float32).astype(ml_dtypes.bfloat16)
+    lo = (table - hi.astype(np.float64)).astype(np.float32).astype(ml_dtypes.bfloat16)
+    return jnp.asarray(hi), jnp.asarray(lo)
+
+
+def host_cycle(count):
+    col = np.arange(count)[None, :]
+    mode = np.arange(count)[:, None]
+    half = count // 2
+    folded = np.where(mode <= half, mode, mode - half)
+    phase = 2.0 * np.pi * ((col * folded) % count) / count
+    scale = np.where((mode == 0) | (mode == half), math.sqrt(1.0 / count), math.sqrt(2.0 / count))
+    return np.where(mode <= half, np.cos(phase), np.sin(phase)) * scale
+
+
+def host_axial(count):
+    first = np.arange(1, count + 1)
+    phase = np.pi * (np.outer(first, first) % (2 * (count + 1))) / (count + 1)
+    return np.sin(phase) * math.sqrt(2.0 / (count + 1))
+
+
+def host_weave(mp):
+    table = np.zeros((mp * LANES, mp * LANES), np.float32)
+    for m in range(mp):
+        for c in range(LANES):
+            table[m * LANES + c, c * mp + m] = 1.0
+    return jnp.asarray(table.astype(ml_dtypes.bfloat16))
+
+
+def iota(shape, dim):
+    return lax.broadcasted_iota(jnp.int32, shape, dim)
+
+
+def onehot(condition):
+    return jnp.where(condition, 1.0, 0.0).astype(F32)
+
+
+def write_split(hi_ref, lo_ref, value):
+    hi, lo = split(value)
+    hi_ref[...] = hi
+    lo_ref[...] = lo
+
+
+TOKEN = jax.ShapeDtypeStruct((8, LANES), F32)
+
+
+def fetch(sources, targets, sems):
+    copies = [
+        pltpu.make_async_copy(source, target, sems.at[k])
+        for k, (source, target) in enumerate(zip(sources, targets, strict=True))
+    ]
+    for copy in copies:
+        copy.start()
+    return copies
+
+
+def front_tables_kernel(mp, slope_ref, basis_ref, krh, krl, kbh, kbl, kwh, kwl):
+    slope = slope_ref[...]
+    basis = basis_ref[...]
+    side = LANES
+    row = iota((side, R), 0)
+    col = iota((side, R), 1)
+    pick = onehot(row % R == col)
+    mask = iota((side, side), 0) // R == iota((side, side), 1) // R
+    value = exact(exact(pick, slope, True), pick, True)
+    write_split(krh, krl, jnp.where(mask, value * (1.0 / 36.0), 0.0))
+    side = 8 * R
+    row = iota((side, R), 0)
+    col = iota((side, R), 1)
+    pick = onehot(row % R == col)
+    block = mp * 8
+    mode = onehot(row // block * mp + (row % block) // 8 == col)
+    mask = iota((side, side), 0) % 8 == iota((side, side), 1) // R
+    value = exact(exact(mode, basis, True), pick, True)
+    write_split(kbh, kbl, jnp.where(mask, value, 0.0))
+    both = exact(slope, basis)
+    value = exact(exact(mode, both, True), pick, True)
+    write_split(kwh, kwl, jnp.where(mask, value * (-1.0 / 36.0), 0.0))
+
+
+def front_tables(slope, basis, mp):
+    one = jax.ShapeDtypeStruct((LANES, LANES), BF)
+    two = jax.ShapeDtypeStruct((8 * R, 8 * R), BF)
+    return pl.pallas_call(
+        functools.partial(front_tables_kernel, mp),
+        out_shape=(one, one, two, two, two, two),
+        in_specs=[VMEM, VMEM],
+        out_specs=(VMEM,) * 6,
+        compiler_params=params(),
+        name="front_tables",
+    )(slope, basis)
+
+
+def back_tables_kernel(mp, basis_ref, hi_ref, lo_ref):
+    rows, cols = hi_ref.shape
+    row = iota((rows, R), 0)
+    col = iota((rows, R), 1)
+    mode = onehot(row // LANES * mp + row % mp == col)
+    pick = onehot(iota((cols, R), 0) % R == iota((cols, R), 1))
+    value = exact(exact(mode, basis_ref[...], True), pick, True)
+    mask = (iota((rows, cols), 0) % LANES) // mp == iota((rows, cols), 1) // R
+    write_split(hi_ref, lo_ref, jnp.where(mask, value, 0.0))
+
+
+def back_tables(basis, mp, peers):
+    shape = jax.ShapeDtypeStruct((peers * LANES, LANES // mp * R), BF)
+    return pl.pallas_call(
+        functools.partial(back_tables_kernel, mp),
+        out_shape=(shape, shape),
+        in_specs=[VMEM],
+        out_specs=(VMEM, VMEM),
+        compiler_params=params(),
+        name="back_tables",
+    )(basis)
+
+
+def pack_columns(out, lane, wide, slim, pieces):
+    for tile in range(4):
+        value = None
+        for index, piece in enumerate(pieces):
+            at = 64 * index if index < 3 else 96 + 32 * index
+            if at // LANES == tile:
+                shift = (at - (wide if index < 3 else slim)) % LANES
+                moved = pltpu.roll(piece, shift, 1) if shift else piece
+                value = moved if value is None else jnp.where(lane >= at % LANES, moved, value)
+        out[:, tile * LANES : (tile + 1) * LANES] = value
+
+
+def pack_kernel(
+    displace, history, stiffen, up_ref, down_ref, left_ref, right_ref, d, h, s, dc, hc, sc, sems
+):
+    rows, flat = stiffen.shape
+    sources, targets = [], []
+    for k, at in enumerate((slice(0, 8), slice(rows - 8, rows))):
+        sources += [displace.at[:, at, :], history.at[:, at, :], stiffen.at[at, :]]
+        targets += [d.at[k], h.at[k], s.at[k]]
+    for k, at in enumerate((slice(0, LANES), slice(flat - LANES, flat))):
+        sources += [displace.at[:, :, at], history.at[:, :, at], stiffen.at[:, at]]
+        targets += [dc.at[k], hc.at[k], sc.at[k]]
+    copies = fetch(sources, targets, sems)
+    for copy in copies[:6]:
+        copy.wait()
+    for k, first, last, out in ((0, 0, 0, up_ref), (1, 6, 7, down_ref)):
+        for i in range(3):
+            out[2 * i : 2 * i + 2, :] = d[k, i, first : first + 2, :]
+        for n in range(9):
+            out[6 + n : 7 + n, :] = h[k, n, last : last + 1, :]
+        out[15:16, :] = 1.0 + s[k, last : last + 1, :]
+    for copy in copies[6:]:
+        copy.wait()
+    lane = iota((rows, LANES), 1)
+    for k, out, wide, slim in ((0, left_ref, 0, 0), (1, right_ref, LANES - 2 * R, LANES - R)):
+        pieces = [dc[k, i] for i in range(3)] + [hc[k, n] for n in range(9)] + [1.0 + sc[k]]
+        pack_columns(out, lane, wide, slim, pieces)
+
+
+def pack(displace, history, stiffen):
+    rows, flat = stiffen.shape
+    row = jax.ShapeDtypeStruct((16, flat), F32)
+    column = jax.ShapeDtypeStruct((rows, 4 * LANES), F32)
+    return pl.pallas_call(
+        pack_kernel,
+        out_shape=(row, row, column, column),
+        in_specs=[HBM] * 3,
+        out_specs=(VMEM,) * 4,
+        scratch_shapes=[
+            pltpu.VMEM((2, 3, 8, flat), F32),
+            pltpu.VMEM((2, 9, 8, flat), F32),
+            pltpu.VMEM((2, 8, flat), F32),
+            pltpu.VMEM((2, 3, rows, LANES), F32),
+            pltpu.VMEM((2, 9, rows, LANES), F32),
+            pltpu.VMEM((2, rows, LANES), F32),
+            pltpu.SemaphoreType.DMA((12,)),
+        ],
+        compiler_params=params(60),
+        cost_estimate=cost(0),
+        name="pack",
+    )(displace, history, stiffen)
+
+
+def corners_kernel(top, bottom, left_ref, right_ref, tall):
+    flat = top.shape[1]
+    lane = iota((HALO, LANES), 1)
+    tall[...] = jnp.zeros_like(tall)
+    for out, at, wide, slim in (
+        (left_ref, slice(0, LANES), 0, 0),
+        (right_ref, slice(flat - LANES, flat), LANES - 2 * R, LANES - R),
+    ):
+        pieces = []
+        for index in range(13):
+            first, count = (2 * index, 2) if index < 3 else (3 + index, 1)
+            tall[index, 0:count, :] = bottom[first : first + count, at]
+            tall[index, HALO - count : HALO, :] = top[first : first + count, at]
+            pieces.append(tall[index])
+        pack_columns(out, lane, wide, slim, pieces)
+
+
+def corners(top, bottom):
+    shape = jax.ShapeDtypeStruct((HALO, 4 * LANES), F32)
+    return pl.pallas_call(
+        corners_kernel,
+        out_shape=(shape, shape),
+        in_specs=[VMEM] * 2,
+        out_specs=(VMEM, VMEM),
+        scratch_shapes=[pltpu.VMEM((13, HALO, LANES), F32)],
+        compiler_params=params(),
+        cost_estimate=cost(0),
+        name="corners",
+    )(top, bottom)
+
+
+def stencil_kernel(
+    comps,
+    mp,
+    peers,
+    modulus,
+    displace,
+    load,
+    history,
+    stiffen,
+    top,
+    bottom,
+    left,
+    left_corner,
+    right,
+    right_corner,
+    krh,
+    krl,
+    kbh,
+    kbl,
+    kwh,
+    kwl,
+    after,
+    *rest,
+):
+    n = len(comps)
+    outs = rest[:n]
+    token, xd, hx, sx, ld, st, sums, diffs, made, sems = rest[n:]
+    token[...] = jnp.zeros_like(token)
+    rows, flat = stiffen.shape
+    tall = rows + HALO
+    tiles = flat // LANES
+    entries = [comp + 3 * k for comp in comps for k in range(3)]
+    center = (slice(0, rows), slice(0, flat))
+
+    def displace_copy(i, t):
+        return pltpu.make_async_copy(
+            displace.at[i, :, t * LANES : (t + 1) * LANES],
+            xd.at[i, t, PAD : PAD + rows, :],
+            sems.at[i * tiles + t],
+        )
+
+    moves = [displace_copy(i, t) for t in range(tiles) for i in range(3)]
+    base = 3 * tiles
+    late = [pltpu.make_async_copy(stiffen, sx.at[center], sems.at[base])]
+    late += [
+        pltpu.make_async_copy(history.at[m], hx.at[(k,) + center], sems.at[base + 1 + k])
+        for k, m in enumerate(entries)
+    ]
+    final = [
+        pltpu.make_async_copy(load.at[comp], ld.at[k], sems.at[base + 1 + 3 * n + k])
+        for k, comp in enumerate(comps)
+    ]
+    for copy in moves + late + final:
+        copy.start()
+    left = (left, left_corner)
+    right = (right, right_corner)
+    lane = iota((tall, LANES), 1)
+    short = iota((rows, LANES), 1)
+
+    def tile_of(refs, at, target):
+        part = slice(at // LANES * LANES, (at // LANES + 1) * LANES)
+        value = jnp.concatenate([ref[:, part] for ref in refs], axis=0)
+        shift = (target - at) % LANES
+        return pltpu.roll(value, shift, 1) if shift else value
+
+    for i in range(3):
+        tile = jnp.where(lane < 64, tile_of(right, 64 * i, 0), tile_of(left, 64 * i, 64))
+        xd[i, tiles, PAD : PAD + tall, :] = tile
+        xd[i, tiles, PAD - 1 : PAD, :] = tile[tall - 1 : tall]
+        xd[i, tiles, PAD + tall : PAD + tall + 1, :] = tile[0:1]
+        for t in range(tiles):
+            part = slice(t * LANES, (t + 1) * LANES)
+            above = top[2 * i : 2 * i + 2, part]
+            xd[i, t, PAD + rows : PAD + rows + 2, :] = bottom[2 * i : 2 * i + 2, part]
+            xd[i, t, PAD + tall - 2 : PAD + tall, :] = above
+            xd[i, t, PAD - 1 : PAD, :] = above[1:2]
+    zeros = jnp.zeros((HALO, flat), F32)
+    for k, m in enumerate(entries):
+        at = 192 + 32 * m
+        hx[k, rows:tall, 0:flat] = zeros
+        hx[k, rows : rows + 1, 0:flat] = bottom[6 + m : 7 + m, :]
+        hx[k, tall - 1 : tall, 0:flat] = top[6 + m : 7 + m, :]
+        hx[k, :, flat:] = jnp.where(lane < 64, tile_of(right, at, 0), tile_of(left, at, 96))
+    sx[rows:tall, 0:flat] = zeros
+    sx[rows : rows + 1, 0:flat] = bottom[15:16, :] - 1.0
+    sx[tall - 1 : tall, 0:flat] = top[15:16, :] - 1.0
+    sx[:, flat:] = jnp.where(lane < 64, tile_of(right, 480, 0), tile_of(left, 480, 96)) - 1.0
+
+    def lanes(t):
+        return pl.ds(pl.multiple_of(t * LANES, LANES), LANES)
+
+    def previous(t):
+        return lax.rem(t + tiles, tiles + 1)
+
+    def following(t):
+        return lax.rem(t + 1, tiles + 1)
+
+    def rolled(value, amount):
+        return pltpu.roll(value, amount % LANES, 1)
+
+    def lower(ref, k, t, height, mask):
+        return jnp.where(mask < R, ref[k, previous(t), 0:height, :], ref[k, t, 0:height, :])
+
+    def higher(ref, k, t, height, mask):
+        return jnp.where(
+            mask >= LANES - R, ref[k, following(t), 0:height, :], ref[k, t, 0:height, :]
+        )
+
+    for copy in moves:
+        copy.wait()
+
+    def rows_step(t, carry):
+        for i in range(3):
+            xd[i, t, PAD + tall : PAD + tall + 1, :] = xd[i, t, PAD : PAD + 1, :]
+            above = xd[i, t, PAD - 1 : PAD - 1 + tall, :]
+            below = xd[i, t, PAD + 1 : PAD + 1 + tall, :]
+            total = above + 4.0 * xd[i, t, PAD : PAD + tall, :] + below
+            change = below - above
+            sums[3 * i, t] = total
+            sums[3 * i + 1, t] = rolled(total, R)
+            sums[3 * i + 2, t] = rolled(total, -R)
+            diffs[3 * i, t] = change
+            diffs[3 * i + 1, t] = rolled(change, R)
+            diffs[3 * i + 2, t] = rolled(change, -R)
+        return carry
+
+    lax.fori_loop(0, tiles + 1, rows_step, 0)
+    for copy in late:
+        copy.wait()
+
+    def stress_step(t, carry):
+        total = [None] * len(entries)
+        for i in range(3):
+            low = lower(sums, 3 * i + 1, t, tall, lane)
+            high = higher(sums, 3 * i + 2, t, tall, lane)
+            second = high - low
+            both = low + high + 4.0 * sums[3 * i, t]
+            low = lower(diffs, 3 * i + 1, t, tall, lane)
+            high = higher(diffs, 3 * i + 2, t, tall, lane)
+            first = low + high + 4.0 * diffs[3 * i, t]
+            bh, bl = split(both)
+            third = dot3(bh, bl, krh[...], krl[...])
+            for k, m in enumerate(entries):
+                part = (
+                    (modulus[m, i] * (1.0 / 12.0)) * first
+                    + (modulus[m, 3 + i] * (1.0 / 12.0)) * second
+                    + modulus[m, 6 + i] * third
+                )
+                total[k] = part if total[k] is None else total[k] + part
+        factor = 1.0 + sx[:, lanes(t)]
+        for k in range(len(entries)):
+            value = factor * total[k] + hx[k, :, lanes(t)]
+            st[k, t, PAD : PAD + tall, :] = value
+            st[k, t, PAD - 1 : PAD, :] = value[tall - 1 : tall]
+        return carry
+
+    lax.fori_loop(0, tiles + 1, stress_step, 0)
+    for copy in final:
+        copy.wait()
+
+    sent = []
+    for index in range(n):
+        first_entry = 3 * index
+        out = made.at[index]
+
+        def pull_rows(t, carry):
+            def around(k):
+                field = first_entry + k
+                return (
+                    st[field, t, PAD - 1 : PAD - 1 + rows, :],
+                    st[field, t, PAD : PAD + rows, :],
+                    st[field, t, PAD + 1 : PAD + 1 + rows, :],
+                )
+
+            above, _, below = around(0)
+            p = below - above
+            above, now, below = around(1)
+            q = above + 4.0 * now + below
+            above, now, below = around(2)
+            w = above + 4.0 * now + below
+            sums[0, t, 0:rows, :] = 4.0 * p
+            sums[1, t, 0:rows, :] = rolled(p - q, R)
+            sums[2, t, 0:rows, :] = rolled(p + q, -R)
+            sums[3, t, 0:rows, :] = 4.0 * w
+            sums[4, t, 0:rows, :] = rolled(w, R)
+            sums[5, t, 0:rows, :] = rolled(w, -R)
+            return carry
+
+        lax.fori_loop(0, tiles + 1, pull_rows, 0)
+
+        def message_step(s, carry):
+            us, ws = [], []
+            for half in range(2):
+                t = 2 * s + half
+                pull = sums[0, t, 0:rows, :] + lower(sums, 1, t, rows, short)
+                pull = pull + higher(sums, 2, t, rows, short)
+                us.append(ld[index, :, lanes(t)] + pull * (1.0 / 12.0))
+                w = sums[3, t, 0:rows, :] + lower(sums, 4, t, rows, short)
+                ws.append(w + higher(sums, 5, t, rows, short))
+            uh, ul = split(jnp.concatenate(us, axis=1))
+            wh, wl = split(jnp.concatenate(ws, axis=1))
+            value = dot3(kbh[...], kbl[...], uh, ul, True)
+            value = value + dot3(kwh[...], kwl[...], wh, wl, True)
+            here = pl.ds(pl.multiple_of(s * 8, 8), 8)
+            for peer in range(peers):
+                for m in range(mp):
+                    row = (peer * mp + m) * 8
+                    out[peer, here, m * rows : (m + 1) * rows] = value[row : row + 8, :]
+            return carry
+
+        lax.fori_loop(0, tiles // 2, message_step, 0)
+        sent += [pltpu.make_async_copy(out, outs[index], sems.at[base + 1 + 4 * n + index])]
+        sent[-1].start()
+    for copy in sent:
+        copy.wait()
+
+
+def stencil(comps, mp, peers, modulus, displace, load, history, stiffen, halos, tables, after):
+    rows, flat = stiffen.shape
+    tall = rows + HALO
+    wide = flat + LANES
+    tiles = flat // LANES
+    n = len(comps)
+    shape = jax.ShapeDtypeStruct((peers, flat // R, mp * rows), F32)
+    return pl.pallas_call(
+        functools.partial(stencil_kernel, comps, mp, peers),
+        out_shape=(shape,) * n + (TOKEN,),
+        in_specs=[SMEM] + [HBM] * 4 + [VMEM] * 12 + [HBM],
+        out_specs=(HBM,) * n + (VMEM,),
+        scratch_shapes=[
+            pltpu.VMEM((3, tiles + 1, PAD + tall + HALO, LANES), F32),
+            pltpu.VMEM((3 * n, tall, wide), F32),
+            pltpu.VMEM((tall, wide), F32),
+            pltpu.VMEM((n, rows, flat), F32),
+            pltpu.VMEM((3 * n, tiles + 1, PAD + tall, LANES), F32),
+            pltpu.VMEM((9, tiles + 1, tall, LANES), F32),
+            pltpu.VMEM((9, tiles + 1, tall, LANES), F32),
+            pltpu.VMEM((n,) + shape.shape, F32),
+            pltpu.SemaphoreType.DMA((3 * tiles + 1 + 5 * n,)),
+        ],
+        compiler_params=params(56),
+        cost_estimate=cost(13 + 8 * n),
+        name="stencil",
+    )(modulus, displace, load, history, stiffen, *halos, *tables, after)
+
+
+def cycle_kernel(parts, ids, piece, th_ref, tl_ref, after, *refs):
+    outs = refs[:parts]
+    token, xh, xl, raw, th, tl, sems = refs[parts:]
+    token[...] = jnp.zeros_like(token)
+    copies = fetch((piece, th_ref, tl_ref), (raw, th, tl), sems)
+    copies[0].wait()
+    hi, lo = split(raw[...])
+    xh[...] = hi
+    xl[...] = lo
+    copies[1].wait()
+    copies[2].wait()
+    block = outs[0].shape[0]
+    for d in range(parts):
+        target = jnp.bitwise_xor(ids[1], d)
+        at = pl.ds(pl.multiple_of(target * block, block), block)
+        outs[d][...] = dot3(th[at, :], tl[at, :], xh[...], xl[...])
+
+
+def cycle_stage(ids, piece, table, parts, after):
+    count, width = piece.shape
+    shape = jax.ShapeDtypeStruct((count // parts, width), F32)
+    return pl.pallas_call(
+        functools.partial(cycle_kernel, parts),
+        out_shape=(shape,) * parts + (TOKEN,),
+        in_specs=[SMEM] + [HBM] * 4,
+        out_specs=(VMEM,) * (parts + 1),
+        scratch_shapes=[
+            pltpu.VMEM((count, width), BF),
+            pltpu.VMEM((count, width), BF),
+            pltpu.VMEM((count, width), F32),
+            pltpu.VMEM((count, count), BF),
+            pltpu.VMEM((count, count), BF),
+            pltpu.SemaphoreType.DMA((3,)),
+        ],
+        compiler_params=params(),
+        cost_estimate=cost(0),
+        name="cycle_stage",
+    )(ids, piece, *table, after)
+
+
+def axial_kernel(mp, parts, ids, radial, cyc, axial, *refs):
+    ins = refs[:parts]
+    th_ref, tl_ref, after = refs[parts : parts + 3]
+    outs = refs[parts + 3 : 2 * parts + 3]
+    token, xh, xl, raw, th, tl, sems = refs[2 * parts + 3 :]
+    token[...] = jnp.zeros_like(token)
+    kc, width = ins[0].shape
+    rows = width // mp
+    copies = fetch([*ins, th_ref, tl_ref], [raw.at[j] for j in range(parts)] + [th, tl], sems)
+    for j in range(parts):
+        source = jnp.bitwise_xor(ids[1], j)
+        at = pl.ds(pl.multiple_of(source * rows, rows), rows)
+        copies[j].wait()
+        for m in range(mp):
+            hi, lo = split(raw[j, :, m * rows : (m + 1) * rows])
+            xh[m * kc : (m + 1) * kc, at] = hi
+            xl[m * kc : (m + 1) * kc, at] = lo
+    copies[parts].wait()
+    copies[parts + 1].wait()
+    mine = cyc[pl.ds(pl.multiple_of(ids[1] * kc, kc), kc), :]
+    base = axial[...] + mine
+    for m in range(mp):
+        part = slice(m * kc, (m + 1) * kc)
+        value = dot3(xh[part, :], xl[part, :], th[...], tl[...])
+        value = value / (base + radial[ids[0] * mp + m])
+        hi, lo = split(value)
+        xh[part, :] = hi
+        xl[part, :] = lo
+    for d in range(parts):
+        target = jnp.bitwise_xor(ids[1], d)
+        at = pl.ds(pl.multiple_of(target * rows, rows), rows)
+        outs[d][...] = dot3(th[at, :], tl[at, :], xh[...], xl[...], True)
+
+
+def axial_stage(ids, radial, cyc, axial, pieces, table, mp, after):
+    parts = len(pieces)
+    kc, width = pieces[0].shape
+    rows = width // mp
+    shape = jax.ShapeDtypeStruct((rows, mp * kc), F32)
+    return pl.pallas_call(
+        functools.partial(axial_kernel, mp, parts),
+        out_shape=(shape,) * parts + (TOKEN,),
+        in_specs=[SMEM, SMEM, VMEM, VMEM] + [HBM] * (parts + 3),
+        out_specs=(VMEM,) * (parts + 1),
+        scratch_shapes=[
+            pltpu.VMEM((mp * kc, parts * rows), BF),
+            pltpu.VMEM((mp * kc, parts * rows), BF),
+            pltpu.VMEM((parts, kc, width), F32),
+            pltpu.VMEM((parts * rows, parts * rows), BF),
+            pltpu.VMEM((parts * rows, parts * rows), BF),
+            pltpu.SemaphoreType.DMA((parts + 2,)),
+        ],
+        compiler_params=params(),
+        cost_estimate=cost(0),
+        name="axial_stage",
+    )(ids, radial, cyc, axial, *pieces, *table, after)
+
+
+def uncycle_kernel(mp, parts, ids, *refs):
+    ins = refs[:parts]
+    th_ref, tl_ref, weave_ref, after, out = refs[parts : parts + 5]
+    token, xh, xl, raw, th, tl, weave, full, sems = refs[parts + 5 :]
+    token[...] = jnp.zeros_like(token)
+    rows, width = ins[0].shape
+    kc = width // mp
+    count = th.shape[1]
+    copies = fetch(
+        [*ins, th_ref, tl_ref, weave_ref],
+        [raw.at[j] for j in range(parts)] + [th, tl, weave],
+        sems,
+    )
+    for j in range(parts):
+        source = jnp.bitwise_xor(ids[1], j)
+        at = pl.ds(pl.multiple_of(source * kc, kc), kc)
+        copies[j].wait()
+        for m in range(mp):
+            hi, lo = split(raw[j, :, m * kc : (m + 1) * kc])
+            xh[m * rows : (m + 1) * rows, at] = hi
+            xl[m * rows : (m + 1) * rows, at] = lo
+    for copy in copies[parts:]:
+        copy.wait()
+    value = dot3(xh[...], xl[...], th[...], tl[...])
+    hi, lo = split(value)
+    span = mp * LANES
+    sent = []
+    for t in range(count // LANES):
+        columns = slice(t * LANES, (t + 1) * LANES)
+
+        def gather(x):
+            return jnp.concatenate(
+                [x[m * rows : (m + 1) * rows, columns] for m in range(mp)], axis=1
+            )
+
+        wide = slice(t * span, (t + 1) * span)
+        full[:, wide] = dot(gather(hi), weave[...]) + dot(gather(lo), weave[...])
+        sent += [pltpu.make_async_copy(full.at[:, wide], out.at[:, wide], sems.at[parts + 3 + t])]
+        sent[-1].start()
+    for copy in sent:
+        copy.wait()
+
+
+def uncycle_stage(ids, pieces, table, weave, mp, after):
+    parts = len(pieces)
+    rows, width = pieces[0].shape
+    count = table[0].shape[0]
+    shape = jax.ShapeDtypeStruct((rows, mp * count), F32)
+    return pl.pallas_call(
+        functools.partial(uncycle_kernel, mp, parts),
+        out_shape=(shape, TOKEN),
+        in_specs=[SMEM] + [HBM] * (parts + 4),
+        out_specs=(HBM, VMEM),
+        scratch_shapes=[
+            pltpu.VMEM((mp * rows, count), BF),
+            pltpu.VMEM((mp * rows, count), BF),
+            pltpu.VMEM((parts, rows, width), F32),
+            pltpu.VMEM((count, count), BF),
+            pltpu.VMEM((count, count), BF),
+            pltpu.VMEM(weave.shape, BF),
+            pltpu.VMEM((rows, mp * count), F32),
+            pltpu.SemaphoreType.DMA((parts + 3 + count // LANES,)),
+        ],
+        compiler_params=params(),
+        cost_estimate=cost(0),
+        name="uncycle_stage",
+    )(ids, *pieces, *table, weave, after)
+
+
+def radial_kernel(comp, piece, th_ref, tl_ref, *refs):
+    out, token, xh, xl, raw, th, tl, sems = refs[-8:]
+    token[...] = jnp.zeros_like(token)
+    peers, few, width = piece.shape
+    groups = width // LANES
+    span = th.shape[1]
+    copies = fetch(
+        [piece.at[j] for j in range(peers)] + [th_ref, tl_ref],
+        [raw.at[j] for j in range(peers)] + [th, tl],
+        sems,
+    )
+    for j in range(peers):
+        copies[j].wait()
+        for g in range(groups):
+            hi, lo = split(raw[j, :, g * LANES : (g + 1) * LANES])
+            xh[g * few : (g + 1) * few, j * LANES : (j + 1) * LANES] = hi
+            xl[g * few : (g + 1) * few, j * LANES : (j + 1) * LANES] = lo
+    copies[peers].wait()
+    copies[peers + 1].wait()
+    value = dot3(xh[...], xl[...], th[...], tl[...])
+    for g in range(groups):
+        out[0, :, g * span : (g + 1) * span] = value[g * few : (g + 1) * few, :]
+
+
+def radial_stage(comp, piece, table, carried, after):
+    peers, few, width = piece.shape
+    groups = width // LANES
+    depth, span = table[0].shape
+    shape = jax.ShapeDtypeStruct((3, few, groups * span), F32)
+    extra = [after] if carried is None else [after, carried]
+    return pl.pallas_call(
+        functools.partial(radial_kernel, comp),
+        out_shape=(shape, TOKEN),
+        grid=(1,),
+        in_specs=[HBM] * (3 + len(extra)),
+        out_specs=(pl.BlockSpec((1, few, groups * span), lambda g: (comp, 0, 0)), VMEM),
+        scratch_shapes=[
+            pltpu.VMEM((groups * few, depth), BF),
+            pltpu.VMEM((groups * few, depth), BF),
+            pltpu.VMEM((peers, few, width), F32),
+            pltpu.VMEM((depth, span), BF),
+            pltpu.VMEM((depth, span), BF),
+            pltpu.SemaphoreType.DMA((peers + 2,)),
+        ],
+        input_output_aliases={4: 0} if carried is not None else {},
+        compiler_params=params(),
+        cost_estimate=cost(0),
+        name="radial_stage",
+    )(piece, *table, *extra)
+
+
+def gate_kernel(block, after, out):
+    del block, after, out
+
+
+def gate(block, after):
+    return pl.pallas_call(
+        gate_kernel,
+        out_shape=jax.ShapeDtypeStruct(block.shape, block.dtype),
+        in_specs=[HBM, HBM],
+        out_specs=HBM,
+        input_output_aliases={0: 0},
+        compiler_params=params(),
+        cost_estimate=cost(0),
+        name="gate",
+    )(block, after)
+
+
+def across(block, axis):
+    return lax.all_to_all(block, axis, split_axis=0, concat_axis=0, tiled=True)
+
+
+def swap(pieces, axis):
+    count = len(pieces)
+    return [pieces[0]] + [
+        lax.ppermute(pieces[d], axis, [(i, i ^ d) for i in range(count)]) for d in range(1, count)
+    ]
+
+
+ORDER = (
+    ("stencil", (0,)),
+    ("send", 0),
+    ("stencil", (1, 2)),
+    ("send", 1),
+    ("cycle", 0),
+    ("axial", 0),
+    ("send", 2),
+    ("cycle", 1),
+    ("axial", 1),
+    ("uncycle", 0),
+    ("cycle", 2),
+    ("axial", 2),
+    ("uncycle", 1),
+    ("radial", 0),
+    ("uncycle", 2),
+    ("radial", 1),
+    ("radial", 2),
+)
+
+
+def body(
+    displace,
+    load,
+    history,
+    stiffen,
+    modulus,
+    radial_slope,
+    radial_basis,
+    axial_eig,
+    cycle_eig,
+    radial_eig,
+):
+    parts = lax.axis_size("ax")
+    peers = lax.axis_size("circ")
+    mp = R // peers
+    rows, flat = stiffen.shape
+    count_a = parts * rows
+    count_c = peers * flat // R
+    me = lax.axis_index("circ").astype(jnp.int32)
+    pe = lax.axis_index("ax").astype(jnp.int32)
+    ids = jnp.stack([me, pe])
+
+    upward, downward, leftward, rightward = pack(displace, history, stiffen)
+    ahead = [(i, i + 1) for i in range(parts - 1)]
+    back_ahead = [(j, i) for i, j in ahead]
+    around = [(i, (i + 1) % peers) for i in range(peers)]
+    back_around = [(j, i) for i, j in around]
+    bottom = lax.ppermute(upward, "ax", back_ahead)
+    top = lax.ppermute(downward, "ax", ahead)
+    right = lax.ppermute(leftward, "circ", back_around)
+    left = lax.ppermute(rightward, "circ", around)
+    to_left, to_right = corners(top, bottom)
+    right_corner = lax.ppermute(to_left, "circ", back_around)
+    left_corner = lax.ppermute(to_right, "circ", around)
+    front = front_tables(radial_slope, radial_basis, mp)
+    back = back_tables(radial_basis, mp, peers)
+    halos = (top, bottom, left, left_corner, right, right_corner)
+
+    cycle_table_parts = host_split(host_cycle(count_c))
+    axial_table_parts = host_split(host_axial(count_a))
+    weave = host_weave(mp)
+    cyc = cycle_eig[:, None]
+    axial = axial_eig[None, :]
+
+    lines = [None] * 3
+    out, token = None, ids
+    for step in ORDER:
+        kind, i = step
+        if kind == "stencil":
+            *sent, token = stencil(
+                i, mp, peers, modulus, displace, load, history, stiffen, halos, front, token
+            )
+            for comp, block in zip(i, sent, strict=True):
+                lines[comp] = block
+        elif kind == "send":
+            block = lines[i] if i < 2 else gate(lines[i], token)
+            lines[i] = across(block, "circ").reshape(count_c, mp * rows)
+        elif kind == "cycle":
+            *sent, token = cycle_stage(ids, lines[i], cycle_table_parts, parts, token)
+            lines[i] = swap(sent, "ax")
+        elif kind == "axial":
+            *sent, token = axial_stage(
+                ids, radial_eig, cyc, axial, lines[i], axial_table_parts, mp, token
+            )
+            lines[i] = swap(sent, "ax")
+        elif kind == "uncycle":
+            sent, token = uncycle_stage(ids, lines[i], cycle_table_parts, weave, mp, token)
+            lines[i] = across(sent.reshape(peers, rows // peers, mp * count_c), "circ")
+        else:
+            out, token = radial_stage(i, lines[i], back, out, token)
+    return out
+
+
+def tiled(mesh):
+    parts, peers = mesh.shape["ax"], mesh.shape["circ"]
+    rows, flat = NA // parts, NC // peers * R
+    return (
+        parts & (parts - 1) == 0
+        and peers & (peers - 1) == 0
+        and R == 32
+        and R % peers == 0
+        and peers * (R // peers) * 8 == 8 * R
+        and rows % LANES == 0
+        and (NC // parts) % LANES == 0
+        and flat % (2 * LANES) == 0
+        and (NC // peers) % 16 == 0
+        and (rows // peers) % 16 == 0
+    )
+
+
 def solution(mesh):
     return jax.shard_map(
-        body,
+        body if tiled(mesh) else plain_body,
         mesh=mesh,
         in_specs=(
             P(None, "ax", "circ"),

time: 811 us -> 264 us (0.33)
  blocking collectives: 192 us -> 0 us
  local copies, waits for them, and re-layouts: 170 us -> 15.1 us
  other arithmetic: 134 us -> 0.58 us
  matrix products: 129 us -> 0 us
  Pallas kernels: 0 us -> 107 us
  waiting for transfers between devices: 152 us -> 78.9 us
  starting transfers between devices: 28.2 us -> 61.4 us
    all_to_all x3 -> x0, blocking collectives: 192 us -> none  [the longest x1 98 us: body(): lax.all_to_all(lax.all_to_all(solved, 'ax', split_axis=1, concat_axis=2,...]
    dot_general x8 -> x0, matrix products: 118 us -> none  [the longest x1 41.2 us: body(): jnp.einsum('mn,nac->mac', modulus, grads, precision=lax.Precision.HIGHEST)]
    all_to_all x2 -> x6, waiting for transfers between devices: 139 us -> 28.7 us  [across(): return lax.all_to_all(block, axis, split_axis=0, concat_axis=0, tiled=True)]
    pallas_call x0 -> x19, Pallas kernels: none -> 107 us  [the longest x2 53 us: stencil(): pl.pallas_call(functools.partial(stencil_kernel, comps, mp, peers), out_s...]
    div x5 -> x0, other arithmetic: 78.5 us -> none  [the longest x2 64 us: cycle_parts(): return ((left + 4.0 * middle + right) / 6.0, (right - left) * 0.5)]
    reshape x6 -> x0, local copies, waits for them, and re-layouts: 41.6 us -> none  [the longest x2 14.2 us: cycle_forward(): cube = field.reshape(count * rows, NC, R)]
    ppermute x8 -> x24, waiting for transfers between devices: 13.5 us -> 50.2 us  [the longest x18 44.4 us: swap(): lax.ppermute(pieces[d], axis, [(i, i ^ d) for i in range(count)])]
    all_to_all x10 -> x0, local copies, waits for them, and re-layouts: 36.1 us -> none  [the longest x3 19.5 us: body(): lax.all_to_all(cube, 'ax', split_axis=3, concat_axis=1, tiled=True)]
  transfers between devices with their start and end apart: 10 -> 30, of which waited for: 8 -> 14; matrix products, arithmetic and copies ran while one was open for 4% -> 0% of each run, Pallas kernels for 0% -> 29%
where the time goes in v2:
time: 264 us
  Pallas kernels  107 us (41%)
  waiting for transfers between devices  78.9 us (30%)
  starting transfers between devices  61.4 us (23%)
  local copies, waits for them, and re-layouts  15.1 us (6%)
    pallas_call x2, Pallas kernels, stencil(): pl.pallas_call(functools.partial(stencil_kernel, comps, mp, peers), out_s...  53 us
    ppermute x18, waiting for transfers between devices, swap(): lax.ppermute(pieces[d], axis, [(i, i ^ d) for i in range(count)])  44.4 us
    all_to_all x6, waiting for transfers between devices, across(): return lax.all_to_all(block, axis, split_axis=0, concat_axis=0, tiled=True)  28.7 us
    all_to_all x6, starting transfers between devices, across(): return lax.all_to_all(block, axis, split_axis=0, concat_axis=0, tiled=True)  27.3 us
    ppermute x18, starting transfers between devices, swap(): lax.ppermute(pieces[d], axis, [(i, i ^ d) for i in range(count)])  20.7 us
    unnamed x72, local copies, waits for them, and re-layouts  15 us
    pallas_call x3, Pallas kernels, axial_stage(): pl.pallas_call(functools.partial(axial_kernel, mp, parts), out_shape=(sha...  14.2 us
    pallas_call x3, Pallas kernels, radial_stage(): pl.pallas_call(functools.partial(radial_kernel, comp), out_shape=(shape,...  12.5 us
  transfers between devices with their start and end apart: 30, of which 14 were waited for; matrix products, arithmetic and copies ran while one was open for 0% of the time, Pallas kernels for 29%

profile of v2, /device:TPU:0, one launch (start us, length us, event | category | flops | bytes accessed | tf_op | source)
XLA Modules:
  0.0 263.6 jit_solution(16124180095865105980)
XLA Ops:
  3.7 4.1 %collective-permute-start.4 = (f32[128,512]{1,0:T(8,128)}, f32[128,512]{1,0:T(8,128)S(1)}, u32[]{:S(2)}, u32[]{:S(2)}) collective-permute-start(f32[128,512]{1,0:T(8,128)} %get-tuple-element.69), channel_id=1, source_target_pairs={{1,0},{2,1},{3,2},{4,3},{5,4},{6,5},{7,6},{0,7},{9,8},{10,9},{11,1... | collective-permute-start | bytes 786440 | tf_op jit(solution)/shard_map/ppermute | solution.py:970
  14.4 4.3 %collective-permute-done.1.bottom = f32[16,2048]{1,0:T(8,128)S(1)} collective-permute-done((f32[16,2048]{1,0:T(8,128)}, f32[16,2048]{1,0:T(8,128)S(1)}, u32[]{:S(2)}, u32[]{:S(2)}) %collective-permute-start.1) | collective-permute-done | bytes 131104 | tf_op jit(solution)/shard_map/ppermute | solution.py:968
  29.0 22.6 %stencil.2 = (f32[8,64,512]{2,1,0:T(8,128)}, f32[8,128]{1,0:T(8,128)}) custom-call(f32[9,9]{1,0:T(8,128)} %modulus.3, f32[3,128,2048]{2,1,0:T(8,128)} %displace.5, f32[3,128,2048]{2,1,0:T(8,128)} %load.3, f32[9,128,2048]{2,1,0:T(8,128)} %history.5, f32[128,2048]{1,0:T(8,128)} %stiffen.5, f32[16,2048]{1,0:T(8,128)} %copy-done.11, f32[16,2048]{1,0:T(8,128)} %copy-done.12, ...), custom_call_target="tpu_custom_call" | custom-call | flops 1 | bytes 75600000 | tf_op jit(solution)/shard_map/stencil/pallas_call | solution.py:652
  55.3 30.3 %stencil.3 = (f32[8,64,512]{2,1,0:T(8,128)}, f32[8,64,512]{2,1,0:T(8,128)}, f32[8,128]{1,0:T(8,128)}) custom-call(f32[9,9]{1,0:T(8,128)} %modulus.3, f32[3,128,2048]{2,1,0:T(8,128)} %displace.5, f32[3,128,2048]{2,1,0:T(8,128)} %load.3, f32[9,128,2048]{2,1,0:T(8,128)} %history.5, f32[128,2048]{1,0:T(8,128)} %stiffen.5, f32[16,2048]{1,0:T(8,128)} %copy-done.11, ...), custom_call_target="tpu_custom_call" | custom-call | flops 1 | bytes 104400000 | tf_op jit(solution)/shard_map/stencil/pallas_call | solution.py:652
  85.7 5.2 %all-to-all-start.2 = ((f32[8,64,512]{2,1,0:T(8,128)}), f32[8,64,512]{2,1,0:T(8,128)}, u32[]{:S(2)}, u32[]{:S(2)}) async-start(f32[8,64,512]{2,1,0:T(8,128)} %get-tuple-element.91), calls=%async_computation.2 | async-start | bytes 2097152 | tf_op jit(solution)/shard_map/all_to_all | solution.py:910
  98.8 5.9 %collective-permute-done.6.refs_1_ = f32[128,512]{1,0:T(8,128)} collective-permute-done((f32[128,512]{1,0:T(8,128)}, f32[128,512]{1,0:T(8,128)}, u32[]{:S(2)}, u32[]{:S(2)}) %collective-permute-start.6) | collective-permute-done | bytes 262176 | tf_op jit(solution)/shard_map/ppermute | solution.py:916
  104.7 6.9 %collective-permute-done.7.refs_2_ = f32[128,512]{1,0:T(8,128)} collective-permute-done((f32[128,512]{1,0:T(8,128)}, f32[128,512]{1,0:T(8,128)}, u32[]{:S(2)}, u32[]{:S(2)}) %collective-permute-start.7) | collective-permute-done | bytes 262176 | tf_op jit(solution)/shard_map/ppermute | solution.py:916
  112.5 5.3 %axial_stage.3 = (f32[128,512]{1,0:T(8,128)S(1)}, f32[128,512]{1,0:T(8,128)}, f32[128,512]{1,0:T(8,128)}, f32[128,512]{1,0:T(8,128)}, f32[8,128]{1,0:T(8,128)S(1)}) custom-call(s32[2]{0:T(128)S(1)} %copy-done.26, f32[32]{0:T(128)S(1)} %copy-done.29, f32[512,1]{1,0:T(8,128)S(1)} %copy.21.cyc, f32[1,512]{1,0:T(1,128)S(1)} %bitcast.13, ...), custom_call_target="tpu_custom_call" | custom-call | flops 1 | bytes 1 | tf_op jit(solution)/shard_map/axial_stage/pallas_call | solution.py:753
  119.5 4.9 %all-to-all-start.1 = ((f32[8,64,512]{2,1,0:T(8,128)}), f32[8,64,512]{2,1,0:T(8,128)}, u32[]{:S(2)}, u32[]{:S(2)}) async-start(f32[8,64,512]{2,1,0:T(8,128)} %copy-done.10), calls=%async_computation.1 | async-start | bytes 2097152 | tf_op jit(solution)/shard_map/all_to_all | solution.py:910
  137.7 4.8 %collective-permute-done.13.refs_2_ = f32[128,512]{1,0:T(8,128)S(1)} collective-permute-done((f32[128,512]{1,0:T(8,128)S(1)}, f32[128,512]{1,0:T(8,128)S(1)}, u32[]{:S(2)}, u32[]{:S(2)}) %collective-permute-start.13) | collective-permute-done | bytes 262176 | tf_op jit(solution)/shard_map/ppermute | solution.py:916
  142.4 4.4 %axial_stage.4 = (f32[128,512]{1,0:T(8,128)S(1)}, f32[128,512]{1,0:T(8,128)}, f32[128,512]{1,0:T(8,128)}, f32[128,512]{1,0:T(8,128)}, f32[8,128]{1,0:T(8,128)S(1)}) custom-call(s32[2]{0:T(128)S(1)} %copy-done.26, f32[32]{0:T(128)S(1)} %copy-done.29, f32[512,1]{1,0:T(8,128)S(1)} %copy.21.cyc, f32[1,512]{1,0:T(1,128)S(1)} %bitcast.14, ...), custom_call_target="tpu_custom_call" | custom-call | flops 1 | bytes 1 | tf_op jit(solution)/shard_map/axial_stage/pallas_call | solution.py:753
  147.8 5.3 %collective-permute-done.10.refs_2_ = f32[128,512]{1,0:T(8,128)S(1)} collective-permute-done((f32[128,512]{1,0:T(8,128)}, f32[128,512]{1,0:T(8,128)S(1)}, u32[]{:S(2)}, u32[]{:S(2)}) %collective-permute-start.10) | collective-permute-done | bytes 262176 | tf_op jit(solution)/shard_map/ppermute | solution.py:916
  157.3 4.7 %all-to-all-start.3 = ((f32[8,16,2048]{2,1,0:T(8,128)}), f32[8,16,2048]{2,1,0:T(8,128)}, u32[]{:S(2)}, u32[]{:S(2)}) async-start(f32[8,16,2048]{2,1,0:T(8,128)} %bitcast.11), calls=%async_computation.3 | async-start | bytes 2097152 | tf_op jit(solution)/shard_map/all_to_all | solution.py:910
  175.5 5.9 %collective-permute-done.16.refs_2_ = f32[128,512]{1,0:T(8,128)S(1)} collective-permute-done((f32[128,512]{1,0:T(8,128)S(1)}, f32[128,512]{1,0:T(8,128)S(1)}, u32[]{:S(2)}, u32[]{:S(2)}) %collective-permute-start.16) | collective-permute-done | bytes 262176 | tf_op jit(solution)/shard_map/ppermute | solution.py:916
  181.5 4.5 %axial_stage.5 = (f32[128,512]{1,0:T(8,128)S(1)}, f32[128,512]{1,0:T(8,128)}, f32[128,512]{1,0:T(8,128)}, f32[128,512]{1,0:T(8,128)}, f32[8,128]{1,0:T(8,128)S(1)}) custom-call(s32[2]{0:T(128)S(1)} %copy-done.26, f32[32]{0:T(128)S(1)} %copy-done.29, f32[512,1]{1,0:T(8,128)S(1)} %copy.21.cyc, f32[1,512]{1,0:T(1,128)S(1)} %bitcast.15, ...), custom_call_target="tpu_custom_call" | custom-call | flops 1 | bytes 1 | tf_op jit(solution)/shard_map/axial_stage/pallas_call | solution.py:753
  186.0 6.1 %collective-permute-done.22.refs_2_ = f32[128,512]{1,0:T(8,128)S(1)} collective-permute-done((f32[128,512]{1,0:T(8,128)}, f32[128,512]{1,0:T(8,128)S(1)}, u32[]{:S(2)}, u32[]{:S(2)}) %collective-permute-start.22) | collective-permute-done | bytes 262176 | tf_op jit(solution)/shard_map/ppermute | solution.py:916
  195.4 4.8 %all-to-all-start.5 = ((f32[8,16,2048]{2,1,0:T(8,128)}), f32[8,16,2048]{2,1,0:T(8,128)}, u32[]{:S(2)}, u32[]{:S(2)}) async-start(f32[8,16,2048]{2,1,0:T(8,128)} %bitcast.9), calls=%async_computation.5 | async-start | bytes 2097152 | tf_op jit(solution)/shard_map/all_to_all | solution.py:910
  203.7 4.4 %back_tables.1 = (bf16[1024,1024]{1,0:T(8,128)(2,1)S(1)}, bf16[1024,1024]{1,0:T(8,128)(2,1)S(1)}) custom-call(f32[32,32]{1,0:T(8,128)S(1)} %copy-done.25), custom_call_target="tpu_custom_call" | custom-call | tf_op jit(solution)/shard_map/back_tables/pallas_call | solution.py:323
  208.1 4.2 %radial_stage.3 = (f32[3,16,16384]{2,1,0:T(8,128)}, f32[8,128]{1,0:T(8,128)S(1)}) custom-call(f32[8,16,2048]{2,1,0:T(8,128)} %all-to-all-done.3.piece, bf16[1024,1024]{1,0:T(8,128)(2,1)S(1)} %get-tuple-element.109.th_ref, bf16[1024,1024]{1,0:T(8,128)(2,1)S(1)} %get-tuple-element.110.tl_ref, f32[8,128]{1,0:T(8,128)S(1)} %get-tuple-element.116.refs_0_), custom_call_target="tpu_custom_call" | custom-call | flops 1 | bytes 1 | tf_op jit(solution)/shard_map/radial_stage/pallas_call | solution.py:871
  219.0 7.8 %all-to-all-done.5.piece = f32[8,16,2048]{2,1,0:T(8,128)} async-done(((f32[8,16,2048]{2,1,0:T(8,128)}), f32[8,16,2048]{2,1,0:T(8,128)}, u32[]{:S(2)}, u32[]{:S(2)}) %all-to-all-start.5) | async-done | bytes 1048608 | tf_op jit(solution)/shard_map/all_to_all | solution.py:910
  226.8 4.2 %all-to-all-start.4 = ((f32[8,16,2048]{2,1,0:T(8,128)}), f32[8,16,2048]{2,1,0:T(8,128)}, u32[]{:S(2)}, u32[]{:S(2)}) async-start(f32[8,16,2048]{2,1,0:T(8,128)} %bitcast.12), calls=%async_computation.4 | async-start | bytes 2097152 | tf_op jit(solution)/shard_map/all_to_all | solution.py:910
  232.7 4.2 %radial_stage.4 = (f32[3,16,16384]{2,1,0:T(8,128)}, f32[8,128]{1,0:T(8,128)S(1)}) custom-call(f32[8,16,2048]{2,1,0:T(8,128)} %all-to-all-done.5.piece, bf16[1024,1024]{1,0:T(8,128)(2,1)S(1)} %get-tuple-element.109.th_ref, bf16[1024,1024]{1,0:T(8,128)(2,1)S(1)} %copy-done.3, ...), custom_call_target="tpu_custom_call", output_to_operand_aliasing={{0}: (4, {})} | custom-call | flops 1 | bytes 1 | tf_op jit(solution)/shard_map/radial_stage/pallas_call | solution.py:871
  236.9 20.8 %all-to-all-done.4.piece = f32[8,16,2048]{2,1,0:T(8,128)} async-done(((f32[8,16,2048]{2,1,0:T(8,128)}), f32[8,16,2048]{2,1,0:T(8,128)}, u32[]{:S(2)}, u32[]{:S(2)}) %all-to-all-start.4) | async-done | bytes 1048608 | tf_op jit(solution)/shard_map/all_to_all | solution.py:910
  259.3 4.2 %radial_stage.5 = (f32[3,16,16384]{2,1,0:T(8,128)}, f32[8,128]{1,0:T(8,128)}) custom-call(f32[8,16,2048]{2,1,0:T(8,128)} %all-to-all-done.4.piece, bf16[1024,1024]{1,0:T(8,128)(2,1)S(1)} %get-tuple-element.109.th_ref, bf16[1024,1024]{1,0:T(8,128)(2,1)S(1)} %copy-done.4, f32[8,128]{1,0:T(8,128)S(1)} %get-tuple-element.122.refs_0_, ...), custom_call_target="tpu_custom_call", output_to_operand_aliasing={{0}: (4, {})} | custom-call | flops 1 | bytes 1 | tf_op jit(solution)/shard_map/radial_stage/pallas_call | solution.py:871
  (129 shorter events, 83.4 us)
Async XLA Ops:
  3.2 25.1 %collective-permute-start.2 = (f32[128,512]{1,0:T(8,128)}, f32[128,512]{1,0:T(8,128)S(1)}, u32[]{:S(2)}, u32[]{:S(2)}) collective-permute-start(f32[128,512]{1,0:T(8,128)} %get-tuple-element.67), channel_id=1, source_target_pairs={{0,1},{1,2},{2,3},{3,4},{4,5},{5,6},{6,7},{7,0},{8,9},{9,10},{10,1... | collective-permute-start | bytes 786440 | tf_op jit(solution)/shard_map/ppermute | solution.py:971
  3.7 24.6 %collective-permute-start.4 = (f32[128,512]{1,0:T(8,128)}, f32[128,512]{1,0:T(8,128)S(1)}, u32[]{:S(2)}, u32[]{:S(2)}) collective-permute-start(f32[128,512]{1,0:T(8,128)} %get-tuple-element.69), channel_id=1, source_target_pairs={{1,0},{2,1},{3,2},{4,3},{5,4},{6,5},{7,6},{0,7},{9,8},{10,9},{11,1... | collective-permute-start | bytes 786440 | tf_op jit(solution)/shard_map/ppermute | solution.py:970
  51.7 34.0 %all-to-all-start = ((f32[8,64,512]{2,1,0:T(8,128)}), f32[8,64,512]{2,1,0:T(8,128)S(1)}, u32[]{:S(2)}, u32[]{:S(2)}) async-start(f32[8,64,512]{2,1,0:T(8,128)} %get-tuple-element.79), calls=%async_computation | async-start | bytes 2097152 | tf_op jit(solution)/shard_map/all_to_all | solution.py:910
  85.7 33.8 %all-to-all-start.2 = ((f32[8,64,512]{2,1,0:T(8,128)}), f32[8,64,512]{2,1,0:T(8,128)}, u32[]{:S(2)}, u32[]{:S(2)}) async-start(f32[8,64,512]{2,1,0:T(8,128)} %get-tuple-element.91), calls=%async_computation.2 | async-start | bytes 2097152 | tf_op jit(solution)/shard_map/all_to_all | solution.py:910
  94.8 9.9 %collective-permute-start.6 = (f32[128,512]{1,0:T(8,128)}, f32[128,512]{1,0:T(8,128)}, u32[]{:S(2)}, u32[]{:S(2)}) collective-permute-start(f32[128,512]{1,0:T(8,128)} %get-tuple-element.82), channel_id=1, source_target_pairs={{0,8},{8,0},{16,24},{24,16},{1,9},{9,1},{17,25},{25,17},{2,10},{10... | collective-permute-start | bytes 786440 | tf_op jit(solution)/shard_map/ppermute | solution.py:916
  97.2 14.4 %collective-permute-start.7 = (f32[128,512]{1,0:T(8,128)}, f32[128,512]{1,0:T(8,128)}, u32[]{:S(2)}, u32[]{:S(2)}) collective-permute-start(f32[128,512]{1,0:T(8,128)} %get-tuple-element.83), channel_id=1, source_target_pairs={{0,16},{8,24},{16,0},{24,8},{1,17},{9,25},{17,1},{25,9},{2,18},{10... | collective-permute-start | bytes 786440 | tf_op jit(solution)/shard_map/ppermute | solution.py:916
  97.2 14.4 %collective-permute-start.8 = (f32[128,512]{1,0:T(8,128)}, f32[128,512]{1,0:T(8,128)}, u32[]{:S(2)}, u32[]{:S(2)}) collective-permute-start(f32[128,512]{1,0:T(8,128)} %get-tuple-element.84), channel_id=1, source_target_pairs={{0,24},{8,16},{16,8},{24,0},{1,25},{9,17},{17,9},{25,1},{2,26},{10... | collective-permute-start | bytes 786440 | tf_op jit(solution)/shard_map/ppermute | solution.py:916
  119.5 37.8 %all-to-all-start.1 = ((f32[8,64,512]{2,1,0:T(8,128)}), f32[8,64,512]{2,1,0:T(8,128)}, u32[]{:S(2)}, u32[]{:S(2)}) async-start(f32[8,64,512]{2,1,0:T(8,128)} %copy-done.10), calls=%async_computation.1 | async-start | bytes 2097152 | tf_op jit(solution)/shard_map/all_to_all | solution.py:910
  127.7 14.7 %collective-permute-start.13 = (f32[128,512]{1,0:T(8,128)S(1)}, f32[128,512]{1,0:T(8,128)S(1)}, u32[]{:S(2)}, u32[]{:S(2)}) collective-permute-start(f32[128,512]{1,0:T(8,128)S(1)} %get-tuple-element.94), channel_id=1, source_target_pairs={{0,16},{8,24},{16,0},{24,8},{1,17},{9,25},{17,1},{25,9},{2,18},{10... | collective-permute-start | bytes 786440 | tf_op jit(solution)/shard_map/ppermute | solution.py:916
  129.1 13.3 %collective-permute-start.14 = (f32[128,512]{1,0:T(8,128)S(1)}, f32[128,512]{1,0:T(8,128)S(1)}, u32[]{:S(2)}, u32[]{:S(2)}) collective-permute-start(f32[128,512]{1,0:T(8,128)S(1)} %get-tuple-element.95), channel_id=1, source_target_pairs={{0,24},{8,16},{16,8},{24,0},{1,25},{9,17},{17,9},{25,1},{2,26},{10... | collective-permute-start | bytes 786440 | tf_op jit(solution)/shard_map/ppermute | solution.py:916
  130.9 16.9 %collective-permute-start.9 = (f32[128,512]{1,0:T(8,128)}, f32[128,512]{1,0:T(8,128)S(1)}, u32[]{:S(2)}, u32[]{:S(2)}) collective-permute-start(f32[128,512]{1,0:T(8,128)} %get-tuple-element.88), channel_id=1, source_target_pairs={{0,8},{8,0},{16,24},{24,16},{1,9},{9,1},{17,25},{25,17},{2,10},{10... | collective-permute-start | bytes 786440 | tf_op jit(solution)/shard_map/ppermute | solution.py:916
  131.2 21.9 %collective-permute-start.10 = (f32[128,512]{1,0:T(8,128)}, f32[128,512]{1,0:T(8,128)S(1)}, u32[]{:S(2)}, u32[]{:S(2)}) collective-permute-start(f32[128,512]{1,0:T(8,128)} %get-tuple-element.89), channel_id=1, source_target_pairs={{0,16},{8,24},{16,0},{24,8},{1,17},{9,25},{17,1},{25,9},{2,18},{10... | collective-permute-start | bytes 786440 | tf_op jit(solution)/shard_map/ppermute | solution.py:916
  136.5 16.6 %collective-permute-start.11 = (f32[128,512]{1,0:T(8,128)}, f32[128,512]{1,0:T(8,128)S(1)}, u32[]{:S(2)}, u32[]{:S(2)}) collective-permute-start(f32[128,512]{1,0:T(8,128)} %get-tuple-element.90), channel_id=1, source_target_pairs={{0,24},{8,16},{16,8},{24,0},{1,25},{9,17},{17,9},{25,1},{2,26},{10... | collective-permute-start | bytes 786440 | tf_op jit(solution)/shard_map/ppermute | solution.py:916
  157.3 38.1 %all-to-all-start.3 = ((f32[8,16,2048]{2,1,0:T(8,128)}), f32[8,16,2048]{2,1,0:T(8,128)}, u32[]{:S(2)}, u32[]{:S(2)}) async-start(f32[8,16,2048]{2,1,0:T(8,128)} %bitcast.11), calls=%async_computation.3 | async-start | bytes 2097152 | tf_op jit(solution)/shard_map/all_to_all | solution.py:910
  166.7 14.8 %collective-permute-start.16 = (f32[128,512]{1,0:T(8,128)S(1)}, f32[128,512]{1,0:T(8,128)S(1)}, u32[]{:S(2)}, u32[]{:S(2)}) collective-permute-start(f32[128,512]{1,0:T(8,128)S(1)} %get-tuple-element.101), channel_id=1, source_target_pairs={{0,16},{8,24},{16,0},{24,8},{1,17},{9,25},{17,1},{25,9},{2,18},{10... | collective-permute-start | bytes 786440 | tf_op jit(solution)/shard_map/ppermute | solution.py:916
  167.0 14.5 %collective-permute-start.17 = (f32[128,512]{1,0:T(8,128)S(1)}, f32[128,512]{1,0:T(8,128)S(1)}, u32[]{:S(2)}, u32[]{:S(2)}) collective-permute-start(f32[128,512]{1,0:T(8,128)S(1)} %get-tuple-element.102), channel_id=1, source_target_pairs={{0,24},{8,16},{16,8},{24,0},{1,25},{9,17},{17,9},{25,1},{2,26},{10... | collective-permute-start | bytes 786440 | tf_op jit(solution)/shard_map/ppermute | solution.py:916
  168.5 17.4 %collective-permute-start.21 = (f32[128,512]{1,0:T(8,128)}, f32[128,512]{1,0:T(8,128)S(1)}, u32[]{:S(2)}, u32[]{:S(2)}) collective-permute-start(f32[128,512]{1,0:T(8,128)} %get-tuple-element.112), channel_id=1, source_target_pairs={{0,8},{8,0},{16,24},{24,16},{1,9},{9,1},{17,25},{25,17},{2,10},{10... | collective-permute-start | bytes 786440 | tf_op jit(solution)/shard_map/ppermute | solution.py:916
  170.2 21.8 %collective-permute-start.22 = (f32[128,512]{1,0:T(8,128)}, f32[128,512]{1,0:T(8,128)S(1)}, u32[]{:S(2)}, u32[]{:S(2)}) collective-permute-start(f32[128,512]{1,0:T(8,128)} %get-tuple-element.113), channel_id=1, source_target_pairs={{0,16},{8,24},{16,0},{24,8},{1,17},{9,25},{17,1},{25,9},{2,18},{10... | collective-permute-start | bytes 786440 | tf_op jit(solution)/shard_map/ppermute | solution.py:916
  174.2 17.9 %collective-permute-start.23 = (f32[128,512]{1,0:T(8,128)}, f32[128,512]{1,0:T(8,128)S(1)}, u32[]{:S(2)}, u32[]{:S(2)}) collective-permute-start(f32[128,512]{1,0:T(8,128)} %get-tuple-element.114), channel_id=1, source_target_pairs={{0,24},{8,16},{16,8},{24,0},{1,25},{9,17},{17,9},{25,1},{2,26},{10... | collective-permute-start | bytes 786440 | tf_op jit(solution)/shard_map/ppermute | solution.py:916
  195.4 31.5 %all-to-all-start.5 = ((f32[8,16,2048]{2,1,0:T(8,128)}), f32[8,16,2048]{2,1,0:T(8,128)}, u32[]{:S(2)}, u32[]{:S(2)}) async-start(f32[8,16,2048]{2,1,0:T(8,128)} %bitcast.9), calls=%async_computation.5 | async-start | bytes 2097152 | tf_op jit(solution)/shard_map/all_to_all | solution.py:910
  200.2 13.4 %collective-permute-start.18 = (f32[128,512]{1,0:T(8,128)}, f32[128,512]{1,0:T(8,128)S(1)}, u32[]{:S(2)}, u32[]{:S(2)}) collective-permute-start(f32[128,512]{1,0:T(8,128)} %get-tuple-element.105), channel_id=1, source_target_pairs={{0,8},{8,0},{16,24},{24,16},{1,9},{9,1},{17,25},{25,17},{2,10},{10... | collective-permute-start | bytes 786440 | tf_op jit(solution)/shard_map/ppermute | solution.py:916
  200.6 14.2 %collective-permute-start.19 = (f32[128,512]{1,0:T(8,128)}, f32[128,512]{1,0:T(8,128)S(1)}, u32[]{:S(2)}, u32[]{:S(2)}) collective-permute-start(f32[128,512]{1,0:T(8,128)} %get-tuple-element.106), channel_id=1, source_target_pairs={{0,16},{8,24},{16,0},{24,8},{1,17},{9,25},{17,1},{25,9},{2,18},{10... | collective-permute-start | bytes 786440 | tf_op jit(solution)/shard_map/ppermute | solution.py:916
  202.0 12.8 %collective-permute-start.20 = (f32[128,512]{1,0:T(8,128)}, f32[128,512]{1,0:T(8,128)S(1)}, u32[]{:S(2)}, u32[]{:S(2)}) collective-permute-start(f32[128,512]{1,0:T(8,128)} %get-tuple-element.107), channel_id=1, source_target_pairs={{0,24},{8,16},{16,8},{24,0},{1,25},{9,17},{17,9},{25,1},{2,26},{10... | collective-permute-start | bytes 786440 | tf_op jit(solution)/shard_map/ppermute | solution.py:916
  226.8 30.8 %all-to-all-start.4 = ((f32[8,16,2048]{2,1,0:T(8,128)}), f32[8,16,2048]{2,1,0:T(8,128)}, u32[]{:S(2)}, u32[]{:S(2)}) async-start(f32[8,16,2048]{2,1,0:T(8,128)} %bitcast.12), calls=%async_computation.4 | async-start | bytes 2097152 | tf_op jit(solution)/shard_map/all_to_all | solution.py:910
  (42 other events, 466.2 us)

commit v3 on v2

--- a/solution.py
+++ b/solution.py
@@ -184,7 +184,7 @@
 LANES = 128
 
 
-def params(mebibytes=24):
+def params(mebibytes=60):
     return pltpu.CompilerParams(vmem_limit_bytes=mebibytes << 20)
 
 
@@ -204,6 +204,12 @@
 
 def dot3(ah, al, bh, bl, transposed=False):
     return dot(ah, bh, transposed) + (dot(ah, bl, transposed) + dot(al, bh, transposed))
+
+
+def stacked3(both, bh, bl, transposed=False):
+    rows = both.shape[0] // 2
+    upper = dot(both[...], bh, transposed)
+    return upper[:rows] + (upper[rows:] + dot(both[0:rows, :], bl, transposed))
 
 
 def exact(a, b, transposed=False):
@@ -216,7 +222,7 @@
 def host_split(table):
     hi = table.astype(np.float32).astype(ml_dtypes.bfloat16)
     lo = (table - hi.astype(np.float64)).astype(np.float32).astype(ml_dtypes.bfloat16)
-    return jnp.asarray(hi), jnp.asarray(lo)
+    return jnp.asarray(np.concatenate([hi, lo], axis=0))
 
 
 def host_cycle(count):
@@ -257,9 +263,6 @@
     lo_ref[...] = lo
 
 
-TOKEN = jax.ShapeDtypeStruct((8, LANES), F32)
-
-
 def fetch(sources, targets, sems):
     copies = [
         pltpu.make_async_copy(source, target, sems.at[k])
@@ -270,7 +273,26 @@
     return copies
 
 
-def front_tables_kernel(mp, slope_ref, basis_ref, krh, krl, kbh, kbl, kwh, kwl):
+def write_stack(ref, value):
+    rows = value.shape[0]
+    hi, lo = split(value)
+    ref[0:rows, :] = hi
+    ref[rows:, :] = lo
+
+
+def fetch(sources, targets, sems):
+    copies = [
+        pltpu.make_async_copy(source, target, sems.at[k])
+        for k, (source, target) in enumerate(zip(sources, targets, strict=True))
+    ]
+    for copy in copies:
+        copy.start()
+    return copies
+
+
+def front_tables_kernel(mp, slope_ref, basis_ref, *refs):
+    outs, made, sems = refs[:6], refs[6:12], refs[12]
+    krh, krl, kbh, kbl, kwh, kwl = made
     slope = slope_ref[...]
     basis = basis_ref[...]
     side = LANES
@@ -292,6 +314,8 @@
     both = exact(slope, basis)
     value = exact(exact(mode, both, True), pick, True)
     write_split(kwh, kwl, jnp.where(mask, value * (-1.0 / 36.0), 0.0))
+    for copy in fetch(made, outs, sems):
+        copy.wait()
 
 
 def front_tables(slope, basis, mp):
@@ -301,33 +325,40 @@
         functools.partial(front_tables_kernel, mp),
         out_shape=(one, one, two, two, two, two),
         in_specs=[VMEM, VMEM],
-        out_specs=(VMEM,) * 6,
+        out_specs=(HBM,) * 6,
+        scratch_shapes=[pltpu.VMEM(x.shape, BF) for x in (one, one, two, two, two, two)]
+        + [pltpu.SemaphoreType.DMA((6,))],
         compiler_params=params(),
         name="front_tables",
     )(slope, basis)
 
 
-def back_tables_kernel(mp, basis_ref, hi_ref, lo_ref):
-    rows, cols = hi_ref.shape
+def back_tables_kernel(mp, basis_ref, after, out, made, sem):
+    del after
+    rows, cols = made.shape[0] // 2, made.shape[1]
     row = iota((rows, R), 0)
     col = iota((rows, R), 1)
     mode = onehot(row // LANES * mp + row % mp == col)
     pick = onehot(iota((cols, R), 0) % R == iota((cols, R), 1))
     value = exact(exact(mode, basis_ref[...], True), pick, True)
     mask = (iota((rows, cols), 0) % LANES) // mp == iota((rows, cols), 1) // R
-    write_split(hi_ref, lo_ref, jnp.where(mask, value, 0.0))
-
-
-def back_tables(basis, mp, peers):
-    shape = jax.ShapeDtypeStruct((peers * LANES, LANES // mp * R), BF)
+    write_stack(made, jnp.where(mask, value, 0.0))
+    copy = pltpu.make_async_copy(made, out, sem)
+    copy.start()
+    copy.wait()
+
+
+def back_tables(basis, mp, peers, after):
+    shape = jax.ShapeDtypeStruct((2 * peers * LANES, LANES // mp * R), BF)
     return pl.pallas_call(
         functools.partial(back_tables_kernel, mp),
-        out_shape=(shape, shape),
-        in_specs=[VMEM],
-        out_specs=(VMEM, VMEM),
-        compiler_params=params(),
+        out_shape=shape,
+        in_specs=[VMEM, HBM],
+        out_specs=HBM,
+        scratch_shapes=[pltpu.VMEM(shape.shape, BF), pltpu.SemaphoreType.DMA],
+        compiler_params=params(24),
         name="back_tables",
-    )(basis)
+    )(basis, after)
 
 
 def pack_columns(out, lane, wide, slim, pieces):
@@ -440,19 +471,10 @@
     left_corner,
     right,
     right_corner,
-    krh,
-    krl,
-    kbh,
-    kbl,
-    kwh,
-    kwl,
-    after,
     *rest,
 ):
     n = len(comps)
-    outs = rest[:n]
-    token, xd, hx, sx, ld, st, sums, diffs, made, sems = rest[n:]
-    token[...] = jnp.zeros_like(token)
+    out, xd, hx, sx, ld, st, sums, diffs, made, krh, krl, kbh, kbl, kwh, kwl, sems = rest[7:]
     rows, flat = stiffen.shape
     tall = rows + HALO
     tiles = flat // LANES
@@ -477,6 +499,14 @@
         pltpu.make_async_copy(load.at[comp], ld.at[k], sems.at[base + 1 + 3 * n + k])
         for k, comp in enumerate(comps)
     ]
+    tables = [
+        pltpu.make_async_copy(source, target, sems.at[base + 1 + 5 * n + k])
+        for k, (source, target) in enumerate(
+            zip(rest[:6], (krh, krl, kbh, kbl, kwh, kwl), strict=True)
+        )
+    ]
+    late += tables[:2]
+    final += tables[2:]
     for copy in moves + late + final:
         copy.start()
     left = (left, left_corner)
@@ -588,7 +618,7 @@
     sent = []
     for index in range(n):
         first_entry = 3 * index
-        out = made.at[index]
+        message = made.at[index]
 
         def pull_rows(t, carry):
             def around(k):
@@ -632,11 +662,11 @@
             for peer in range(peers):
                 for m in range(mp):
                     row = (peer * mp + m) * 8
-                    out[peer, here, m * rows : (m + 1) * rows] = value[row : row + 8, :]
+                    message[peer, here, m * rows : (m + 1) * rows] = value[row : row + 8, :]
             return carry
 
         lax.fori_loop(0, tiles // 2, message_step, 0)
-        sent += [pltpu.make_async_copy(out, outs[index], sems.at[base + 1 + 4 * n + index])]
+        sent += [pltpu.make_async_copy(message, out.at[:, index], sems.at[base + 1 + 4 * n + index])]
         sent[-1].start()
     for copy in sent:
         copy.wait()
@@ -648,12 +678,12 @@
     wide = flat + LANES
     tiles = flat // LANES
     n = len(comps)
-    shape = jax.ShapeDtypeStruct((peers, flat // R, mp * rows), F32)
+    block = (flat // R, mp * rows)
     return pl.pallas_call(
         functools.partial(stencil_kernel, comps, mp, peers),
-        out_shape=(shape,) * n + (TOKEN,),
-        in_specs=[SMEM] + [HBM] * 4 + [VMEM] * 12 + [HBM],
-        out_specs=(HBM,) * n + (VMEM,),
+        out_shape=jax.ShapeDtypeStruct((peers, n) + block, F32),
+        in_specs=[SMEM] + [HBM] * 4 + [VMEM] * 6 + [HBM] * 7,
+        out_specs=HBM,
         scratch_shapes=[
             pltpu.VMEM((3, tiles + 1, PAD + tall + HALO, LANES), F32),
             pltpu.VMEM((3 * n, tall, wide), F32),
@@ -662,248 +692,190 @@
             pltpu.VMEM((3 * n, tiles + 1, PAD + tall, LANES), F32),
             pltpu.VMEM((9, tiles + 1, tall, LANES), F32),
             pltpu.VMEM((9, tiles + 1, tall, LANES), F32),
-            pltpu.VMEM((n,) + shape.shape, F32),
-            pltpu.SemaphoreType.DMA((3 * tiles + 1 + 5 * n,)),
+            pltpu.VMEM((n, peers) + block, F32),
+            *(pltpu.VMEM(table.shape, BF) for table in tables),
+            pltpu.SemaphoreType.DMA((3 * tiles + 7 + 5 * n,)),
         ],
-        compiler_params=params(56),
+        compiler_params=params(),
         cost_estimate=cost(13 + 8 * n),
         name="stencil",
     )(modulus, displace, load, history, stiffen, *halos, *tables, after)
 
 
-def cycle_kernel(parts, ids, piece, th_ref, tl_ref, after, *refs):
+def cycle_kernel(index, parts, ids, piece, table_ref, after, *refs):
+    del after
     outs = refs[:parts]
-    token, xh, xl, raw, th, tl, sems = refs[parts:]
-    token[...] = jnp.zeros_like(token)
-    copies = fetch((piece, th_ref, tl_ref), (raw, th, tl), sems)
-    copies[0].wait()
-    hi, lo = split(raw[...])
-    xh[...] = hi
-    xl[...] = lo
-    copies[1].wait()
-    copies[2].wait()
+    xh, xl, raw, table, made, sems = refs[parts:]
+    peers, _, height, _ = piece.shape
+    copies = fetch(
+        [piece.at[j, index] for j in range(peers)] + [table_ref],
+        [raw.at[j] for j in range(peers)] + [table],
+        sems,
+    )
+    for j in range(peers):
+        copies[j].wait()
+        at = slice(j * height, (j + 1) * height)
+        hi, lo = split(raw[j])
+        xh[at, :] = hi
+        xl[at, :] = lo
+    copies[peers].wait()
+    value = stacked3(table, xh[...], xl[...])
     block = outs[0].shape[0]
-    for d in range(parts):
-        target = jnp.bitwise_xor(ids[1], d)
-        at = pl.ds(pl.multiple_of(target * block, block), block)
-        outs[d][...] = dot3(th[at, :], tl[at, :], xh[...], xl[...])
-
-
-def cycle_stage(ids, piece, table, parts, after):
-    count, width = piece.shape
+    for b in range(parts):
+        made[jnp.bitwise_xor(ids[1], b)] = value[b * block : (b + 1) * block]
+    sent = fetch([made.at[d] for d in range(parts)], outs, sems.at[pl.ds(peers + 1, parts)])
+    for copy in sent:
+        copy.wait()
+
+
+def cycle_stage(index, ids, piece, table, parts, after):
+    peers, _, height, width = piece.shape
+    count = peers * height
     shape = jax.ShapeDtypeStruct((count // parts, width), F32)
     return pl.pallas_call(
-        functools.partial(cycle_kernel, parts),
-        out_shape=(shape,) * parts + (TOKEN,),
-        in_specs=[SMEM] + [HBM] * 4,
-        out_specs=(VMEM,) * (parts + 1),
+        functools.partial(cycle_kernel, index, parts),
+        out_shape=(shape,) * parts,
+        in_specs=[SMEM] + [HBM] * 3,
+        out_specs=(HBM,) * parts,
         scratch_shapes=[
             pltpu.VMEM((count, width), BF),
             pltpu.VMEM((count, width), BF),
-            pltpu.VMEM((count, width), F32),
-            pltpu.VMEM((count, count), BF),
-            pltpu.VMEM((count, count), BF),
-            pltpu.SemaphoreType.DMA((3,)),
+            pltpu.VMEM((peers, height, width), F32),
+            pltpu.VMEM(table.shape, BF),
+            pltpu.VMEM((parts,) + shape.shape, F32),
+            pltpu.SemaphoreType.DMA((peers + 1 + parts,)),
         ],
-        compiler_params=params(),
+        compiler_params=params(24),
         cost_estimate=cost(0),
         name="cycle_stage",
-    )(ids, piece, *table, after)
+    )(ids, piece, table, after)
 
 
 def axial_kernel(mp, parts, ids, radial, cyc, axial, *refs):
     ins = refs[:parts]
-    th_ref, tl_ref, after = refs[parts : parts + 3]
-    outs = refs[parts + 3 : 2 * parts + 3]
-    token, xh, xl, raw, th, tl, sems = refs[2 * parts + 3 :]
-    token[...] = jnp.zeros_like(token)
+    table_ref, after, out, x, xh, xl, raw, table, made, sems = refs[parts:]
+    del after
     kc, width = ins[0].shape
     rows = width // mp
-    copies = fetch([*ins, th_ref, tl_ref], [raw.at[j] for j in range(parts)] + [th, tl], sems)
+    half = mp * kc
+    count = parts * rows
+    copies = fetch([*ins, table_ref], [raw.at[j] for j in range(parts)] + [table], sems)
     for j in range(parts):
         source = jnp.bitwise_xor(ids[1], j)
         at = pl.ds(pl.multiple_of(source * rows, rows), rows)
         copies[j].wait()
         for m in range(mp):
             hi, lo = split(raw[j, :, m * rows : (m + 1) * rows])
-            xh[m * kc : (m + 1) * kc, at] = hi
-            xl[m * kc : (m + 1) * kc, at] = lo
+            x[m * kc : (m + 1) * kc, at] = hi
+            x[half + m * kc : half + (m + 1) * kc, at] = lo
     copies[parts].wait()
-    copies[parts + 1].wait()
     mine = cyc[pl.ds(pl.multiple_of(ids[1] * kc, kc), kc), :]
     base = axial[...] + mine
+    value = stacked3(x, table[0:count, :], table[count:, :])
     for m in range(mp):
         part = slice(m * kc, (m + 1) * kc)
-        value = dot3(xh[part, :], xl[part, :], th[...], tl[...])
-        value = value / (base + radial[ids[0] * mp + m])
-        hi, lo = split(value)
+        hi, lo = split(value[part] / (base + radial[ids[0] * mp + m]))
         xh[part, :] = hi
         xl[part, :] = lo
-    for d in range(parts):
-        target = jnp.bitwise_xor(ids[1], d)
-        at = pl.ds(pl.multiple_of(target * rows, rows), rows)
-        outs[d][...] = dot3(th[at, :], tl[at, :], xh[...], xl[...], True)
+    made[...] = stacked3(table, xh[...], xl[...], True)
+    copy = pltpu.make_async_copy(made, out, sems.at[parts + 1])
+    copy.start()
+    copy.wait()
 
 
 def axial_stage(ids, radial, cyc, axial, pieces, table, mp, after):
     parts = len(pieces)
     kc, width = pieces[0].shape
-    rows = width // mp
-    shape = jax.ShapeDtypeStruct((rows, mp * kc), F32)
+    count = width // mp * parts
     return pl.pallas_call(
         functools.partial(axial_kernel, mp, parts),
-        out_shape=(shape,) * parts + (TOKEN,),
-        in_specs=[SMEM, SMEM, VMEM, VMEM] + [HBM] * (parts + 3),
-        out_specs=(VMEM,) * (parts + 1),
+        out_shape=jax.ShapeDtypeStruct((count, mp * kc), F32),
+        in_specs=[SMEM, SMEM, VMEM, VMEM] + [HBM] * (parts + 2),
+        out_specs=HBM,
         scratch_shapes=[
-            pltpu.VMEM((mp * kc, parts * rows), BF),
-            pltpu.VMEM((mp * kc, parts * rows), BF),
+            pltpu.VMEM((2 * mp * kc, count), BF),
+            pltpu.VMEM((mp * kc, count), BF),
+            pltpu.VMEM((mp * kc, count), BF),
             pltpu.VMEM((parts, kc, width), F32),
-            pltpu.VMEM((parts * rows, parts * rows), BF),
-            pltpu.VMEM((parts * rows, parts * rows), BF),
+            pltpu.VMEM(table.shape, BF),
+            pltpu.VMEM((count, mp * kc), F32),
             pltpu.SemaphoreType.DMA((parts + 2,)),
         ],
-        compiler_params=params(),
+        compiler_params=params(24),
         cost_estimate=cost(0),
         name="axial_stage",
-    )(ids, radial, cyc, axial, *pieces, *table, after)
-
-
-def uncycle_kernel(mp, parts, ids, *refs):
-    ins = refs[:parts]
-    th_ref, tl_ref, weave_ref, after, out = refs[parts : parts + 5]
-    token, xh, xl, raw, th, tl, weave, full, sems = refs[parts + 5 :]
-    token[...] = jnp.zeros_like(token)
-    rows, width = ins[0].shape
+    )(ids, radial, cyc, axial, *pieces, table, after)
+
+
+def return_kernel(comp, mp, parts, peers, piece, *refs):
+    out, x, y, raw, table, weave, kernel, made, sems = refs[-9:]
+    _, few, width = piece.shape
     kc = width // mp
-    count = th.shape[1]
-    copies = fetch(
-        [*ins, th_ref, tl_ref, weave_ref],
-        [raw.at[j] for j in range(parts)] + [th, tl, weave],
-        sems,
-    )
-    for j in range(parts):
-        source = jnp.bitwise_xor(ids[1], j)
-        at = pl.ds(pl.multiple_of(source * kc, kc), kc)
-        copies[j].wait()
-        for m in range(mp):
-            hi, lo = split(raw[j, :, m * kc : (m + 1) * kc])
-            xh[m * rows : (m + 1) * rows, at] = hi
-            xl[m * rows : (m + 1) * rows, at] = lo
-    for copy in copies[parts:]:
+    count = table.shape[1]
+    depth, span = kernel.shape[0] // 2, kernel.shape[1]
+    half = mp * peers * few
+    groups = count * mp // LANES
+    copies = fetch((piece, *refs[:3]), (raw, table, weave, kernel), sems)
+    copies[0].wait()
+    for p in range(parts):
+        for q in range(peers):
+            for m in range(mp):
+                row = (m * peers + q) * few
+                hi, lo = split(raw[p * peers + q, :, m * kc : (m + 1) * kc])
+                x[row : row + few, p * kc : (p + 1) * kc] = hi
+                x[half + row : half + row + few, p * kc : (p + 1) * kc] = lo
+    for copy in copies[1:]:
         copy.wait()
-    value = dot3(xh[...], xl[...], th[...], tl[...])
-    hi, lo = split(value)
-    span = mp * LANES
-    sent = []
+    value = split(stacked3(x, table[0:count, :], table[count:, :]))
+    rows = peers * few
     for t in range(count // LANES):
         columns = slice(t * LANES, (t + 1) * LANES)
-
-        def gather(x):
-            return jnp.concatenate(
-                [x[m * rows : (m + 1) * rows, columns] for m in range(mp)], axis=1
+        for part, first in zip(value, (0, groups * few), strict=True):
+            gathered = jnp.concatenate(
+                [part[m * rows : (m + 1) * rows, columns] for m in range(mp)], axis=1
             )
-
-        wide = slice(t * span, (t + 1) * span)
-        full[:, wide] = dot(gather(hi), weave[...]) + dot(gather(lo), weave[...])
-        sent += [pltpu.make_async_copy(full.at[:, wide], out.at[:, wide], sems.at[parts + 3 + t])]
-        sent[-1].start()
-    for copy in sent:
-        copy.wait()
-
-
-def uncycle_stage(ids, pieces, table, weave, mp, after):
-    parts = len(pieces)
-    rows, width = pieces[0].shape
-    count = table[0].shape[0]
-    shape = jax.ShapeDtypeStruct((rows, mp * count), F32)
+            woven = dot(gathered, weave[...]).astype(BF)
+            for g in range(mp):
+                for q in range(peers):
+                    row = first + (t * mp + g) * few
+                    y[row : row + few, q * LANES : (q + 1) * LANES] = woven[
+                        q * few : (q + 1) * few, g * LANES : (g + 1) * LANES
+                    ]
+    result = stacked3(y, kernel[0:depth, :], kernel[depth:, :])
+    for g in range(groups):
+        made[:, g * span : (g + 1) * span] = result[g * few : (g + 1) * few, :]
+    copy = pltpu.make_async_copy(made, out.at[comp], sems.at[4])
+    copy.start()
+    copy.wait()
+
+
+def return_stage(comp, piece, table, weave, back, mp, parts, carried):
+    devices, few, width = piece.shape
+    peers = devices // parts
+    count = table.shape[1]
+    depth, span = back.shape[0] // 2, back.shape[1]
+    groups = count * mp // LANES
+    extra = [] if carried is None else [carried]
     return pl.pallas_call(
-        functools.partial(uncycle_kernel, mp, parts),
-        out_shape=(shape, TOKEN),
-        in_specs=[SMEM] + [HBM] * (parts + 4),
-        out_specs=(HBM, VMEM),
+        functools.partial(return_kernel, comp, mp, parts, peers),
+        out_shape=jax.ShapeDtypeStruct((3, few, groups * span), F32),
+        in_specs=[HBM] * (4 + len(extra)),
+        out_specs=HBM,
         scratch_shapes=[
-            pltpu.VMEM((mp * rows, count), BF),
-            pltpu.VMEM((mp * rows, count), BF),
-            pltpu.VMEM((parts, rows, width), F32),
-            pltpu.VMEM((count, count), BF),
-            pltpu.VMEM((count, count), BF),
+            pltpu.VMEM((2 * mp * peers * few, count), BF),
+            pltpu.VMEM((2 * groups * few, depth), BF),
+            pltpu.VMEM(piece.shape, F32),
+            pltpu.VMEM(table.shape, BF),
             pltpu.VMEM(weave.shape, BF),
-            pltpu.VMEM((rows, mp * count), F32),
-            pltpu.SemaphoreType.DMA((parts + 3 + count // LANES,)),
+            pltpu.VMEM(back.shape, BF),
+            pltpu.VMEM((few, groups * span), F32),
+            pltpu.SemaphoreType.DMA((5,)),
         ],
-        compiler_params=params(),
+        input_output_aliases={4: 0} if extra else {},
+        compiler_params=params(32),
         cost_estimate=cost(0),
-        name="uncycle_stage",
-    )(ids, *pieces, *table, weave, after)
-
-
-def radial_kernel(comp, piece, th_ref, tl_ref, *refs):
-    out, token, xh, xl, raw, th, tl, sems = refs[-8:]
-    token[...] = jnp.zeros_like(token)
-    peers, few, width = piece.shape
-    groups = width // LANES
-    span = th.shape[1]
-    copies = fetch(
-        [piece.at[j] for j in range(peers)] + [th_ref, tl_ref],
-        [raw.at[j] for j in range(peers)] + [th, tl],
-        sems,
-    )
-    for j in range(peers):
-        copies[j].wait()
-        for g in range(groups):
-            hi, lo = split(raw[j, :, g * LANES : (g + 1) * LANES])
-            xh[g * few : (g + 1) * few, j * LANES : (j + 1) * LANES] = hi
-            xl[g * few : (g + 1) * few, j * LANES : (j + 1) * LANES] = lo
-    copies[peers].wait()
-    copies[peers + 1].wait()
-    value = dot3(xh[...], xl[...], th[...], tl[...])
-    for g in range(groups):
-        out[0, :, g * span : (g + 1) * span] = value[g * few : (g + 1) * few, :]
-
-
-def radial_stage(comp, piece, table, carried, after):
-    peers, few, width = piece.shape
-    groups = width // LANES
-    depth, span = table[0].shape
-    shape = jax.ShapeDtypeStruct((3, few, groups * span), F32)
-    extra = [after] if carried is None else [after, carried]
-    return pl.pallas_call(
-        functools.partial(radial_kernel, comp),
-        out_shape=(shape, TOKEN),
-        grid=(1,),
-        in_specs=[HBM] * (3 + len(extra)),
-        out_specs=(pl.BlockSpec((1, few, groups * span), lambda g: (comp, 0, 0)), VMEM),
-        scratch_shapes=[
-            pltpu.VMEM((groups * few, depth), BF),
-            pltpu.VMEM((groups * few, depth), BF),
-            pltpu.VMEM((peers, few, width), F32),
-            pltpu.VMEM((depth, span), BF),
-            pltpu.VMEM((depth, span), BF),
-            pltpu.SemaphoreType.DMA((peers + 2,)),
-        ],
-        input_output_aliases={4: 0} if carried is not None else {},
-        compiler_params=params(),
-        cost_estimate=cost(0),
-        name="radial_stage",
-    )(piece, *table, *extra)
-
-
-def gate_kernel(block, after, out):
-    del block, after, out
-
-
-def gate(block, after):
-    return pl.pallas_call(
-        gate_kernel,
-        out_shape=jax.ShapeDtypeStruct(block.shape, block.dtype),
-        in_specs=[HBM, HBM],
-        out_specs=HBM,
-        input_output_aliases={0: 0},
-        compiler_params=params(),
-        cost_estimate=cost(0),
-        name="gate",
-    )(block, after)
+        name="return_stage",
+    )(piece, table, weave, back, *extra)
 
 
 def across(block, axis):
@@ -919,22 +891,17 @@
 
 ORDER = (
     ("stencil", (0,)),
-    ("send", 0),
     ("stencil", (1, 2)),
-    ("send", 1),
     ("cycle", 0),
+    ("tables", None),
     ("axial", 0),
-    ("send", 2),
     ("cycle", 1),
     ("axial", 1),
-    ("uncycle", 0),
     ("cycle", 2),
+    ("return", 0),
     ("axial", 2),
-    ("uncycle", 1),
-    ("radial", 0),
-    ("uncycle", 2),
-    ("radial", 1),
-    ("radial", 2),
+    ("return", 1),
+    ("return", 2),
 )
 
 
@@ -973,41 +940,40 @@
     right_corner = lax.ppermute(to_left, "circ", back_around)
     left_corner = lax.ppermute(to_right, "circ", around)
     front = front_tables(radial_slope, radial_basis, mp)
-    back = back_tables(radial_basis, mp, peers)
     halos = (top, bottom, left, left_corner, right, right_corner)
 
-    cycle_table_parts = host_split(host_cycle(count_c))
-    axial_table_parts = host_split(host_axial(count_a))
+    cycle_table_stack = host_split(host_cycle(count_c))
+    axial_table_stack = host_split(host_axial(count_a))
     weave = host_weave(mp)
     cyc = cycle_eig[:, None]
     axial = axial_eig[None, :]
 
     lines = [None] * 3
-    out, token = None, ids
-    for step in ORDER:
-        kind, i = step
+    out, after = None, ids
+    for kind, i in ORDER:
         if kind == "stencil":
-            *sent, token = stencil(
-                i, mp, peers, modulus, displace, load, history, stiffen, halos, front, token
+            after = stencil(
+                i, mp, peers, modulus, displace, load, history, stiffen, halos, front, after
             )
-            for comp, block in zip(i, sent, strict=True):
-                lines[comp] = block
-        elif kind == "send":
-            block = lines[i] if i < 2 else gate(lines[i], token)
-            lines[i] = across(block, "circ").reshape(count_c, mp * rows)
+            block = across(after, "circ")
+            for index, comp in enumerate(i):
+                lines[comp] = (index, block)
+        elif kind == "tables":
+            after = back = back_tables(radial_basis, mp, peers, after)
         elif kind == "cycle":
-            *sent, token = cycle_stage(ids, lines[i], cycle_table_parts, parts, token)
-            lines[i] = swap(sent, "ax")
+            index, block = lines[i]
+            sent = cycle_stage(index, ids, block, cycle_table_stack, parts, after)
+            after = sent[0]
+            lines[i] = swap(list(sent), "ax")
         elif kind == "axial":
-            *sent, token = axial_stage(
-                ids, radial_eig, cyc, axial, lines[i], axial_table_parts, mp, token
+            after = axial_stage(
+                ids, radial_eig, cyc, axial, lines[i], axial_table_stack, mp, after
             )
-            lines[i] = swap(sent, "ax")
-        elif kind == "uncycle":
-            sent, token = uncycle_stage(ids, lines[i], cycle_table_parts, weave, mp, token)
-            lines[i] = across(sent.reshape(peers, rows // peers, mp * count_c), "circ")
+            block = after.reshape(parts * peers, rows // peers, -1)
+            lines[i] = across(block, ("ax", "circ"))
         else:
-            out, token = radial_stage(i, lines[i], back, out, token)
+            out = return_stage(i, lines[i], cycle_table_stack, weave, back, mp, parts, out)
+            after = out
     return out
 
 

time: 264 us -> 250 us (0.947)
  starting transfers between devices: 61.4 us -> 47.5 us
  Pallas kernels: 107 us -> 100 us
  waiting for transfers between devices: 78.9 us -> 85.7 us
    all_to_all x6 -> x5, waiting for transfers between devices: 28.7 us -> 41.7 us  [across(): return lax.all_to_all(block, axis, split_axis=0, concat_axis=0, tiled=True)]
    ppermute x18 -> x9, starting transfers between devices: 20.7 us -> 11 us  [swap(): lax.ppermute(pieces[d], axis, [(i, i ^ d) for i in range(count)])]
    pallas_call x14 -> x10, Pallas kernels: 49.4 us -> 40.9 us  [the longest x3 15.4 us: return_stage(): pl.pallas_call(functools.partial(return_kernel, comp, mp, parts, peers),...]
    ppermute x18 -> x9, waiting for transfers between devices: 44.4 us -> 38.2 us  [swap(): lax.ppermute(pieces[d], axis, [(i, i ^ d) for i in range(count)])]
    all_to_all x6 -> x5, starting transfers between devices: 27.3 us -> 23.3 us  [across(): return lax.all_to_all(block, axis, split_axis=0, concat_axis=0, tiled=True)]
    unnamed x72 -> x52, local copies, waits for them, and re-layouts: 15 us -> 14.5 us
  transfers between devices with their start and end apart: 30 -> 20, of which waited for: 14 -> 12; matrix products, arithmetic and copies ran while one was open for 0% -> 0% of each run, Pallas kernels for 29% -> 28%
where the time goes in v3:
time: 250 us; the launch traced here: 249 us
  Pallas kernels  100 us (40%)
  waiting for transfers between devices  85.7 us (34%)
  starting transfers between devices  47.5 us (19%)
  local copies, waits for them, and re-layouts  14.7 us (6%)
    pallas_call x2, Pallas kernels, stencil(): pl.pallas_call(functools.partial(stencil_kernel, comps, mp, peers), out_s...  51.4 us
    all_to_all x5, waiting for transfers between devices, across(): return lax.all_to_all(block, axis, split_axis=0, concat_axis=0, tiled=True)  41.7 us
    ppermute x9, waiting for transfers between devices, swap(): lax.ppermute(pieces[d], axis, [(i, i ^ d) for i in range(count)])  38.2 us
    all_to_all x5, starting transfers between devices, across(): return lax.all_to_all(block, axis, split_axis=0, concat_axis=0, tiled=True)  23.3 us
    pallas_call x3, Pallas kernels, return_stage(): pl.pallas_call(functools.partial(return_kernel, comp, mp, parts, peers),...  15.4 us
    unnamed x52, local copies, waits for them, and re-layouts  14.5 us
    ppermute x9, starting transfers between devices, swap(): lax.ppermute(pieces[d], axis, [(i, i ^ d) for i in range(count)])  11 us
    pallas_call x3, Pallas kernels, axial_stage(): pl.pallas_call(functools.partial(axial_kernel, mp, parts), out_shape=jax....  10.7 us
  transfers between devices with their start and end apart: 20, of which 12 were waited for; matrix products, arithmetic and copies ran while one was open for 0% of the time, Pallas kernels for 28%

profile of v3, /device:TPU:0, one launch (start us, length us, event | category | flops | bytes accessed | tf_op | source)
XLA Modules:
  0.0 249.0 jit_solution(3698930540100596839)
XLA Ops:
  3.6 4.1 %collective-permute-start.4 = (f32[128,512]{1,0:T(8,128)}, f32[128,512]{1,0:T(8,128)S(1)}, u32[]{:S(2)}, u32[]{:S(2)}) collective-permute-start(f32[128,512]{1,0:T(8,128)} %get-tuple-element.33), channel_id=1, source_target_pairs={{1,0},{2,1},{3,2},{4,3},{5,4},{6,5},{7,6},{0,7},{9,8},{10,9},{11,1... | collective-permute-start | bytes 786440 | tf_op jit(solution)/shard_map/ppermute | solution.py:937
  7.8 3.8 %collective-permute-start = (f32[16,2048]{1,0:T(8,128)}, f32[16,2048]{1,0:T(8,128)S(1)}, u32[]{:S(2)}, u32[]{:S(2)}) collective-permute-start(f32[16,2048]{1,0:T(8,128)} %get-tuple-element.29), channel_id=1, source_target_pairs={{0,8},{8,16},{16,24},{1,9},{9,17},{17,25},{2,10},{10,18},{18,26},{... | collective-permute-start | bytes 393224 | tf_op jit(solution)/shard_map/ppermute | solution.py:936
  14.4 4.3 %collective-permute-done.1.bottom = f32[16,2048]{1,0:T(8,128)S(1)} collective-permute-done((f32[16,2048]{1,0:T(8,128)}, f32[16,2048]{1,0:T(8,128)S(1)}, u32[]{:S(2)}, u32[]{:S(2)}) %collective-permute-start.1) | collective-permute-done | bytes 131104 | tf_op jit(solution)/shard_map/ppermute | solution.py:935
  21.0 3.5 %collective-permute-start.5 = (f32[8,512]{1,0:T(8,128)}, f32[8,512]{1,0:T(8,128)S(1)}, u32[]{:S(2)}, u32[]{:S(2)}) collective-permute-start(f32[8,512]{1,0:T(8,128)} %get-tuple-element.34), channel_id=1, source_target_pairs={{1,0},{2,1},{3,2},{4,3},{5,4},{6,5},{7,6},{0,7},{9,8},{10,9},{11,1... | collective-permute-start | bytes 49160 | tf_op jit(solution)/shard_map/ppermute | solution.py:940
  28.8 21.9 %stencil.2.rest_6_ = f32[8,1,64,512]{3,2,1,0:T(8,128)} custom-call(f32[9,9]{1,0:T(8,128)} %modulus.3, f32[3,128,2048]{2,1,0:T(8,128)} %displace.5, f32[3,128,2048]{2,1,0:T(8,128)} %load.3, f32[9,128,2048]{2,1,0:T(8,128)} %history.5, f32[128,2048]{1,0:T(8,128)} %stiffen.5, f32[16,2048]{1,0:T(8,128)} %copy-done.19, f32[16,2048]{1,0:T(8,128)} %copy-done.20, ...), custom_call_target="tpu_custom_call" | custom-call | flops 1 | bytes 75600000 | tf_op jit(solution)/shard_map/stencil/pallas_call | solution.py:682
  50.7 4.3 %all-to-all-start.1 = ((f32[8,1,64,512]{3,2,1,0:T(8,128)}), f32[8,1,64,512]{3,2,1,0:T(8,128)}, u32[]{:S(2)}, u32[]{:S(2)}) async-start(f32[8,1,64,512]{3,2,1,0:T(8,128)} %stencil.2.rest_6_), calls=%async_computation.1 | async-start | bytes 2097152 | tf_op jit(solution)/shard_map/all_to_all | solution.py:882
  55.0 29.5 %stencil.3.after = f32[8,2,64,512]{3,2,1,0:T(8,128)} custom-call(f32[9,9]{1,0:T(8,128)} %modulus.3, f32[3,128,2048]{2,1,0:T(8,128)} %displace.5, f32[3,128,2048]{2,1,0:T(8,128)} %load.3, f32[9,128,2048]{2,1,0:T(8,128)} %history.5, f32[128,2048]{1,0:T(8,128)} %stiffen.5, f32[16,2048]{1,0:T(8,128)} %copy-done.19, f32[16,2048]{1,0:T(8,128)} %copy-done.20, ...), custom_call_target="tpu_custom_call" | custom-call | flops 1 | bytes 104400000 | tf_op jit(solution)/shard_map/stencil/pallas_call | solution.py:682
  84.6 5.3 %all-to-all-start = ((f32[8,2,64,512]{3,2,1,0:T(8,128)}), f32[8,2,64,512]{3,2,1,0:T(8,128)}, u32[]{:S(2)}, u32[]{:S(2)}) async-start(f32[8,2,64,512]{3,2,1,0:T(8,128)} %stencil.3.after), calls=%async_computation | async-start | bytes 4194304 | tf_op jit(solution)/shard_map/all_to_all | solution.py:882
  89.9 3.8 %cycle_stage.3 = (f32[128,512]{1,0:T(8,128)S(1)}, f32[128,512]{1,0:T(8,128)}, f32[128,512]{1,0:T(8,128)}, f32[128,512]{1,0:T(8,128)}) custom-call(s32[2]{0:T(128)S(1)} %copy-done.16, f32[8,1,64,512]{3,2,1,0:T(8,128)} %all-to-all-done.1.piece, bf16[1024,512]{1,0:T(8,128)(2,1)S(1)} %copy-done.5, f32[8,2,64,512]{3,2,1,0:T(8,128)S(1)} %copy-done.6), custom_call_target="tpu_custom_call" | custom-call | flops 1 | bytes 1 | tf_op jit(solution)/shard_map/cycle_stage/pallas_call | solution.py:735
  99.4 4.7 %back_tables.1.refs_5_.refs_2_ = bf16[2048,1024]{1,0:T(8,128)(2,1)S(1)} custom-call(f32[32,32]{1,0:T(8,128)S(1)} %copy-done.15, f32[128,512]{1,0:T(8,128)S(1)} %copy-done.13), custom_call_target="tpu_custom_call" | custom-call | tf_op jit(solution)/shard_map/back_tables/pallas_call | solution.py:353
  104.2 6.9 %collective-permute-done.7.refs_2_ = f32[128,512]{1,0:T(8,128)S(1)} collective-permute-done((f32[128,512]{1,0:T(8,128)}, f32[128,512]{1,0:T(8,128)S(1)}, u32[]{:S(2)}, u32[]{:S(2)}) %collective-permute-start.7) | collective-permute-done | bytes 262176 | tf_op jit(solution)/shard_map/ppermute | solution.py:888
  111.1 3.9 %axial_stage.3.after = f32[512,512]{1,0:T(8,128)} custom-call(s32[2]{0:T(128)S(1)} %copy-done.16, f32[32]{0:T(128)S(1)} %copy-done.18, f32[512,1]{1,0:T(8,128)S(1)} %copy.18.cyc, f32[1,512]{1,0:T(1,128)S(1)} %bitcast.8, f32[128,512]{1,0:T(8,128)S(1)} %copy-done.14, f32[128,512]{1,0:T(8,128)S(1)} %collective-permute-done.6.refs_1_, ...), custom_call_target="tpu_custom_call" | custom-call | flops 1 | bytes 1 | tf_op jit(solution)/shard_map/axial_stage/pallas_call | solution.py:790
  117.0 22.0 %all-to-all-done.piece = f32[8,2,64,512]{3,2,1,0:T(8,128)} async-done(((f32[8,2,64,512]{3,2,1,0:T(8,128)}), f32[8,2,64,512]{3,2,1,0:T(8,128)}, u32[]{:S(2)}, u32[]{:S(2)}) %all-to-all-start) | async-done | bytes 2097184 | tf_op jit(solution)/shard_map/all_to_all | solution.py:882
  149.0 10.7 %collective-permute-done.9.refs_1_ = f32[128,512]{1,0:T(8,128)S(1)} collective-permute-done((f32[128,512]{1,0:T(8,128)S(1)}, f32[128,512]{1,0:T(8,128)S(1)}, u32[]{:S(2)}, u32[]{:S(2)}) %collective-permute-start.9) | collective-permute-done | bytes 262176 | tf_op jit(solution)/shard_map/ppermute | solution.py:888
  160.8 7.2 %collective-permute-done.11.refs_3_ = f32[128,512]{1,0:T(8,128)S(1)} collective-permute-done((f32[128,512]{1,0:T(8,128)S(1)}, f32[128,512]{1,0:T(8,128)S(1)}, u32[]{:S(2)}, u32[]{:S(2)}) %collective-permute-start.11) | collective-permute-done | bytes 262176 | tf_op jit(solution)/shard_map/ppermute | solution.py:888
  168.0 3.8 %axial_stage.4.after = f32[512,512]{1,0:T(8,128)} custom-call(s32[2]{0:T(128)S(1)} %copy-done.16, f32[32]{0:T(128)S(1)} %copy-done.18, f32[512,1]{1,0:T(8,128)S(1)} %copy.18.cyc, f32[1,512]{1,0:T(1,128)S(1)} %bitcast.9, f32[128,512]{1,0:T(8,128)S(1)} %get-tuple-element.45.refs_0_.refs_5_, f32[128,512]{1,0:T(8,128)S(1)} %collective-permute-done.9.refs_1_, ...), custom_call_target="tpu_custom_call" | custom-call | flops 1 | bytes 1 | tf_op jit(solution)/shard_map/axial_stage/pallas_call | solution.py:790
  172.8 5.3 %all-to-all-start.4 = ((f32[32,16,512]{2,1,0:T(8,128)}), f32[32,16,512]{2,1,0:T(8,128)}, u32[]{:S(2)}, u32[]{:S(2)}) async-start(f32[32,16,512]{2,1,0:T(8,128)} %bitcast.6), calls=%async_computation.4 | async-start | bytes 2097152 | tf_op jit(solution)/shard_map/all_to_all | solution.py:882
  186.2 4.9 %return_stage.3.refs_5_.refs_3_ = f32[3,16,16384]{2,1,0:T(8,128)} custom-call(f32[32,16,512]{2,1,0:T(8,128)S(1)} %copy-done.10, bf16[1024,512]{1,0:T(8,128)(2,1)S(1)} %copy-done.5, bf16[512,512]{1,0:T(8,128)(2,1)S(1)} %copy-done.8, bf16[2048,1024]{1,0:T(8,128)(2,1)S(1)} %copy-done.1), custom_call_target="tpu_custom_call" | custom-call | flops 1 | bytes 1 | tf_op jit(solution)/shard_map/return_stage/pallas_call | solution.py:859
  191.1 3.6 %collective-permute-done.12.refs_1_ = f32[128,512]{1,0:T(8,128)S(1)} collective-permute-done((f32[128,512]{1,0:T(8,128)S(1)}, f32[128,512]{1,0:T(8,128)S(1)}, u32[]{:S(2)}, u32[]{:S(2)}) %collective-permute-start.12) | collective-permute-done | bytes 262176 | tf_op jit(solution)/shard_map/ppermute | solution.py:888
  196.3 7.1 %collective-permute-done.14.refs_3_ = f32[128,512]{1,0:T(8,128)S(1)} collective-permute-done((f32[128,512]{1,0:T(8,128)S(1)}, f32[128,512]{1,0:T(8,128)S(1)}, u32[]{:S(2)}, u32[]{:S(2)}) %collective-permute-start.14) | collective-permute-done | bytes 262176 | tf_op jit(solution)/shard_map/ppermute | solution.py:888
  209.2 5.0 %all-to-all-start.3 = ((f32[32,16,512]{2,1,0:T(8,128)}), f32[32,16,512]{2,1,0:T(8,128)S(1)}, u32[]{:S(2)}, u32[]{:S(2)}) async-start(f32[32,16,512]{2,1,0:T(8,128)} %bitcast.7), calls=%async_computation.3 | async-start | bytes 2097152 | tf_op jit(solution)/shard_map/all_to_all | solution.py:882
  216.4 5.6 %return_stage.4.refs_3_ = f32[3,16,16384]{2,1,0:T(8,128)} custom-call(f32[32,16,512]{2,1,0:T(8,128)} %all-to-all-done.4.piece, bf16[1024,512]{1,0:T(8,128)(2,1)S(1)} %copy-done.5, bf16[512,512]{1,0:T(8,128)(2,1)S(1)} %copy-done.8, bf16[2048,1024]{1,0:T(8,128)(2,1)S(1)} %copy-done.2, ...), custom_call_target="tpu_custom_call", output_to_operand_aliasing={{}: (4, {})} | custom-call | flops 1 | bytes 1 | tf_op jit(solution)/shard_map/return_stage/pallas_call | solution.py:859
  222.0 19.8 %all-to-all-done.3.piece = f32[32,16,512]{2,1,0:T(8,128)S(1)} async-done(((f32[32,16,512]{2,1,0:T(8,128)}), f32[32,16,512]{2,1,0:T(8,128)S(1)}, u32[]{:S(2)}, u32[]{:S(2)}) %all-to-all-start.3) | async-done | bytes 1048608 | tf_op jit(solution)/shard_map/all_to_all | solution.py:882
  244.0 4.9 %return_stage.5 = f32[3,16,16384]{2,1,0:T(8,128)} custom-call(f32[32,16,512]{2,1,0:T(8,128)S(1)} %all-to-all-done.3.piece, bf16[1024,512]{1,0:T(8,128)(2,1)S(1)} %copy-done.5, bf16[512,512]{1,0:T(8,128)(2,1)S(1)} %copy-done.8, bf16[2048,1024]{1,0:T(8,128)(2,1)S(1)} %copy-done.3, f32[3,16,16384]{2,1,0:T(8,128)} %return_stage.4.refs_3_), custom_call_target="tpu_custom_call", output_to_operand_aliasing={{}: (4, {})} | custom-call | flops 1 | bytes 1 | tf_op jit(solution)/shard_map/return_stage/pallas_call | solution.py:859
  (85 shorter events, 52.5 us)
Async XLA Ops:
  3.1 24.9 %collective-permute-start.2 = (f32[128,512]{1,0:T(8,128)}, f32[128,512]{1,0:T(8,128)S(1)}, u32[]{:S(2)}, u32[]{:S(2)}) collective-permute-start(f32[128,512]{1,0:T(8,128)} %get-tuple-element.31), channel_id=1, source_target_pairs={{0,1},{1,2},{2,3},{3,4},{4,5},{5,6},{6,7},{7,0},{8,9},{9,10},{10,1... | collective-permute-start | bytes 786440 | tf_op jit(solution)/shard_map/ppermute | solution.py:938
  3.6 24.4 %collective-permute-start.4 = (f32[128,512]{1,0:T(8,128)}, f32[128,512]{1,0:T(8,128)S(1)}, u32[]{:S(2)}, u32[]{:S(2)}) collective-permute-start(f32[128,512]{1,0:T(8,128)} %get-tuple-element.33), channel_id=1, source_target_pairs={{1,0},{2,1},{3,2},{4,3},{5,4},{6,5},{7,6},{0,7},{9,8},{10,9},{11,1... | collective-permute-start | bytes 786440 | tf_op jit(solution)/shard_map/ppermute | solution.py:937
  7.8 6.6 %collective-permute-start = (f32[16,2048]{1,0:T(8,128)}, f32[16,2048]{1,0:T(8,128)S(1)}, u32[]{:S(2)}, u32[]{:S(2)}) collective-permute-start(f32[16,2048]{1,0:T(8,128)} %get-tuple-element.29), channel_id=1, source_target_pairs={{0,8},{8,16},{16,24},{1,9},{9,17},{17,25},{2,10},{10,18},{18,26},{... | collective-permute-start | bytes 393224 | tf_op jit(solution)/shard_map/ppermute | solution.py:936
  11.6 7.1 %collective-permute-start.1 = (f32[16,2048]{1,0:T(8,128)}, f32[16,2048]{1,0:T(8,128)S(1)}, u32[]{:S(2)}, u32[]{:S(2)}) collective-permute-start(f32[16,2048]{1,0:T(8,128)} %get-tuple-element.30), channel_id=1, source_target_pairs={{8,0},{16,8},{24,16},{9,1},{17,9},{25,17},{10,2},{18,10},{26,18},{... | collective-permute-start | bytes 393224 | tf_op jit(solution)/shard_map/ppermute | solution.py:935
  21.0 7.0 %collective-permute-start.3 = (f32[8,512]{1,0:T(8,128)}, f32[8,512]{1,0:T(8,128)S(1)}, u32[]{:S(2)}, u32[]{:S(2)}) collective-permute-start(f32[8,512]{1,0:T(8,128)} %get-tuple-element.32), channel_id=1, source_target_pairs={{0,1},{1,2},{2,3},{3,4},{4,5},{5,6},{6,7},{7,0},{8,9},{9,10},{10,1... | collective-permute-start | bytes 49160 | tf_op jit(solution)/shard_map/ppermute | solution.py:941
  21.0 7.0 %collective-permute-start.5 = (f32[8,512]{1,0:T(8,128)}, f32[8,512]{1,0:T(8,128)S(1)}, u32[]{:S(2)}, u32[]{:S(2)}) collective-permute-start(f32[8,512]{1,0:T(8,128)} %get-tuple-element.34), channel_id=1, source_target_pairs={{1,0},{2,1},{3,2},{4,3},{5,4},{6,5},{7,6},{0,7},{9,8},{10,9},{11,1... | collective-permute-start | bytes 49160 | tf_op jit(solution)/shard_map/ppermute | solution.py:940
  50.7 33.9 %all-to-all-start.1 = ((f32[8,1,64,512]{3,2,1,0:T(8,128)}), f32[8,1,64,512]{3,2,1,0:T(8,128)}, u32[]{:S(2)}, u32[]{:S(2)}) async-start(f32[8,1,64,512]{3,2,1,0:T(8,128)} %stencil.2.rest_6_), calls=%async_computation.1 | async-start | bytes 2097152 | tf_op jit(solution)/shard_map/all_to_all | solution.py:882
  84.6 54.4 %all-to-all-start = ((f32[8,2,64,512]{3,2,1,0:T(8,128)}), f32[8,2,64,512]{3,2,1,0:T(8,128)}, u32[]{:S(2)}, u32[]{:S(2)}) async-start(f32[8,2,64,512]{3,2,1,0:T(8,128)} %stencil.3.after), calls=%async_computation | async-start | bytes 4194304 | tf_op jit(solution)/shard_map/all_to_all | solution.py:882
  89.9 21.2 %copy-start.17 = (f32[512]{0:T(512)S(1)}, f32[512]{0:T(512)}, u32[]{:S(2)}) copy-start(f32[512]{0:T(512)} %param.20) | copy-start | bytes 6148
  89.9 21.2 %copy-start.18 = (f32[32]{0:T(128)S(1)}, f32[32]{0:T(128)}, u32[]{:S(2)}) copy-start(f32[32]{0:T(128)} %radial.5) | copy-start | bytes 388
  94.4 16.7 %copy-start.7 = (bf16[1024,512]{1,0:T(8,128)(2,1)S(1)}, bf16[1024,512]{1,0:T(8,128)(2,1)}, u32[]{:S(2)}) copy-start(bf16[1024,512]{1,0:T(8,128)(2,1)} %constant.15.clone.refs_4_) | copy-start | bytes 3145732
  94.4 9.8 %collective-permute-start.6 = (f32[128,512]{1,0:T(8,128)}, f32[128,512]{1,0:T(8,128)S(1)}, u32[]{:S(2)}, u32[]{:S(2)}) collective-permute-start(f32[128,512]{1,0:T(8,128)} %get-tuple-element.42), channel_id=1, source_target_pairs={{0,8},{8,0},{16,24},{24,16},{1,9},{9,1},{17,25},{25,17},{2,10},{10... | collective-permute-start | bytes 786440 | tf_op jit(solution)/shard_map/ppermute | solution.py:888
  96.8 14.3 %collective-permute-start.7 = (f32[128,512]{1,0:T(8,128)}, f32[128,512]{1,0:T(8,128)S(1)}, u32[]{:S(2)}, u32[]{:S(2)}) collective-permute-start(f32[128,512]{1,0:T(8,128)} %get-tuple-element.43), channel_id=1, source_target_pairs={{0,16},{8,24},{16,0},{24,8},{1,17},{9,25},{17,1},{25,9},{2,18},{10... | collective-permute-start | bytes 786440 | tf_op jit(solution)/shard_map/ppermute | solution.py:888
  96.8 14.3 %collective-permute-start.8 = (f32[128,512]{1,0:T(8,128)}, f32[128,512]{1,0:T(8,128)S(1)}, u32[]{:S(2)}, u32[]{:S(2)}) collective-permute-start(f32[128,512]{1,0:T(8,128)} %get-tuple-element.44), channel_id=1, source_target_pairs={{0,24},{8,16},{16,8},{24,0},{1,25},{9,17},{17,9},{25,1},{2,26},{10... | collective-permute-start | bytes 786440 | tf_op jit(solution)/shard_map/ppermute | solution.py:888
  139.0 32.9 %all-to-all-start.2 = ((f32[32,16,512]{2,1,0:T(8,128)}), f32[32,16,512]{2,1,0:T(8,128)S(1)}, u32[]{:S(2)}, u32[]{:S(2)}) async-start(f32[32,16,512]{2,1,0:T(8,128)} %bitcast.4), calls=%async_computation.2 | async-start | bytes 2097152 | tf_op jit(solution)/shard_map/all_to_all | solution.py:882
  145.5 14.3 %collective-permute-start.9 = (f32[128,512]{1,0:T(8,128)S(1)}, f32[128,512]{1,0:T(8,128)S(1)}, u32[]{:S(2)}, u32[]{:S(2)}) collective-permute-start(f32[128,512]{1,0:T(8,128)S(1)} %get-tuple-element.46), channel_id=1, source_target_pairs={{0,8},{8,0},{16,24},{24,16},{1,9},{9,1},{17,25},{25,17},{2,10},{10... | collective-permute-start | bytes 786440 | tf_op jit(solution)/shard_map/ppermute | solution.py:888
  147.3 13.5 %collective-permute-start.10 = (f32[128,512]{1,0:T(8,128)S(1)}, f32[128,512]{1,0:T(8,128)S(1)}, u32[]{:S(2)}, u32[]{:S(2)}) collective-permute-start(f32[128,512]{1,0:T(8,128)S(1)} %get-tuple-element.47), channel_id=1, source_target_pairs={{0,16},{8,24},{16,0},{24,8},{1,17},{9,25},{17,1},{25,9},{2,18},{10... | collective-permute-start | bytes 786440 | tf_op jit(solution)/shard_map/ppermute | solution.py:888
  148.8 19.2 %collective-permute-start.11 = (f32[128,512]{1,0:T(8,128)S(1)}, f32[128,512]{1,0:T(8,128)S(1)}, u32[]{:S(2)}, u32[]{:S(2)}) collective-permute-start(f32[128,512]{1,0:T(8,128)S(1)} %get-tuple-element.48), channel_id=1, source_target_pairs={{0,24},{8,16},{16,8},{24,0},{1,25},{9,17},{17,9},{25,1},{2,26},{10... | collective-permute-start | bytes 786440 | tf_op jit(solution)/shard_map/ppermute | solution.py:888
  172.8 12.2 %copy-start.8 = (bf16[512,512]{1,0:T(8,128)(2,1)S(1)}, bf16[512,512]{1,0:T(8,128)(2,1)}, u32[]{:S(2)}) copy-start(bf16[512,512]{1,0:T(8,128)(2,1)} %constant.16.clone.refs_1_) | copy-start | bytes 1572868
  172.8 36.3 %all-to-all-start.4 = ((f32[32,16,512]{2,1,0:T(8,128)}), f32[32,16,512]{2,1,0:T(8,128)}, u32[]{:S(2)}, u32[]{:S(2)}) async-start(f32[32,16,512]{2,1,0:T(8,128)} %bitcast.6), calls=%async_computation.4 | async-start | bytes 2097152 | tf_op jit(solution)/shard_map/all_to_all | solution.py:882
  181.4 13.3 %collective-permute-start.12 = (f32[128,512]{1,0:T(8,128)S(1)}, f32[128,512]{1,0:T(8,128)S(1)}, u32[]{:S(2)}, u32[]{:S(2)}) collective-permute-start(f32[128,512]{1,0:T(8,128)S(1)} %get-tuple-element.50), channel_id=1, source_target_pairs={{0,8},{8,0},{16,24},{24,16},{1,9},{9,1},{17,25},{25,17},{2,10},{10... | collective-permute-start | bytes 786440 | tf_op jit(solution)/shard_map/ppermute | solution.py:888
  183.0 13.3 %collective-permute-start.13 = (f32[128,512]{1,0:T(8,128)S(1)}, f32[128,512]{1,0:T(8,128)S(1)}, u32[]{:S(2)}, u32[]{:S(2)}) collective-permute-start(f32[128,512]{1,0:T(8,128)S(1)} %get-tuple-element.51), channel_id=1, source_target_pairs={{0,16},{8,24},{16,0},{24,8},{1,17},{9,25},{17,1},{25,9},{2,18},{10... | collective-permute-start | bytes 786440 | tf_op jit(solution)/shard_map/ppermute | solution.py:888
  184.5 18.9 %collective-permute-start.14 = (f32[128,512]{1,0:T(8,128)S(1)}, f32[128,512]{1,0:T(8,128)S(1)}, u32[]{:S(2)}, u32[]{:S(2)}) collective-permute-start(f32[128,512]{1,0:T(8,128)S(1)} %get-tuple-element.52), channel_id=1, source_target_pairs={{0,24},{8,16},{16,8},{24,0},{1,25},{9,17},{17,9},{25,1},{2,26},{10... | collective-permute-start | bytes 786440 | tf_op jit(solution)/shard_map/ppermute | solution.py:888
  209.2 32.6 %all-to-all-start.3 = ((f32[32,16,512]{2,1,0:T(8,128)}), f32[32,16,512]{2,1,0:T(8,128)S(1)}, u32[]{:S(2)}, u32[]{:S(2)}) async-start(f32[32,16,512]{2,1,0:T(8,128)} %bitcast.7), calls=%async_computation.3 | async-start | bytes 2097152 | tf_op jit(solution)/shard_map/all_to_all | solution.py:882
  (22 other events, 72.2 us)
